TPU v7x, 128 devices: a whole 4x4x4 slice. The times are simulated.
128 devices in a mesh: dp: 32 (over x, z, y_hi), tensor: 4 (over y_lo, core).
Axes of the slice: x: 4, y: 4 (y_hi: 2, y_lo: 2; y = y_hi * 2 + y_lo), z: 4, core: 2. Of those that a mesh axis runs over, the one named last changes fastest.
Arguments:
- hidden_in: bfloat16 [32768, 1536], P(('dp', 'tensor')), may hold values from -6 to 6
- seg_ids: int32 [32768], P('dp'), may hold values from 0 to 4, as said below
- pre_gain: float32 [1536], replicated, may hold values from 0.1 to 1.9
- proj_gate: bfloat16 [1536, 3072], P('dp', 'tensor'), may hold values from -0.15625 to 0.15625
- proj_x: bfloat16 [1536, 3072], P('dp', 'tensor'), may hold values from -0.15625 to 0.15625
- proj_bc: bfloat16 [1536, 256], P('dp'), may hold values from -0.15625 to 0.15625
- proj_dt: bfloat16 [1536, 48], P('dp', 'tensor'), may hold values from -0.15625 to 0.15625
- conv_x: float32 [4, 3072], replicated, may hold values from -0.5 to 0.5
- conv_bias_x: float32 [3072], replicated, may hold values from -0.5 to 0.5
- conv_bc: float32 [4, 256], replicated, may hold values from -0.5 to 0.5
- conv_bias_bc: float32 [256], replicated, may hold values from -0.5 to 0.5
- dt_bias: float32 [48], replicated, may hold values from -9 to -3
- a_log: float32 [48], replicated, may hold values from -1 to 2.77
- skip_d: float32 [48], replicated, may hold values from 0.5 to 1.5
- gate_gain: float32 [3072], replicated, may hold values from 0.1 to 1.9
- proj_out: bfloat16 [3072, 1536], P('tensor', 'dp'), may hold values from -0.109375 to 0.109375
- cotangent: bfloat16 [32768, 1536], P(('dp', 'tensor')), may hold values from -6 to 6
Outputs:
- out: bfloat16 [32768, 1536], P(('dp', 'tensor'))
- d_hidden: float32 [32768, 1536], P(('dp', 'tensor'))
- d_pre_gain: float32 [1536], replicated
- d_proj_gate: float32 [1536, 3072], P('dp', 'tensor')
- d_proj_x: float32 [1536, 3072], P('dp', 'tensor')
- d_proj_bc: float32 [1536, 256], P('dp')
- d_proj_dt: float32 [1536, 48], P('dp', 'tensor')
- d_conv_x: float32 [4, 3072], replicated
- d_conv_bias_x: float32 [3072], replicated
- d_conv_bc: float32 [4, 256], replicated
- d_conv_bias_bc: float32 [256], replicated
- d_dt_bias: float32 [48], replicated
- d_a_log: float32 [48], replicated
- d_skip_d: float32 [48], replicated
- d_gate_gain: float32 [3072], replicated
- d_proj_out: float32 [3072, 1536], P('tensor', 'dp')
Inputs may be any that keep to these rules, and one draw needn't show every extreme that they name: `seg_ids`: within each sequence of 1024 tokens (those of one index of dp) the numbers start at 0, never fall and rise by one at each of exactly four document starts; one document's first token has an index of at most 128 within its sequence (counting from 0), and its last token an index of at least 895.
All inputs are finite; a program needn't handle non-finite values.
Results may differ from a plain program's by a relative error of at most 0.0082.
Values may be sent and summed in bfloat16 or wider, within the bound.
A program may use at most 128 MiB of HBM per device.

v0:
```python
import jax
import jax.numpy as jnp
from jax import lax
from jax.sharding import PartitionSpec as P

GROUP = 256
INNER = 3072


EPS = 1e-05


def pre_norm(hidden, gain_vec):
    inv_rms = lax.rsqrt(jnp.mean(hidden * hidden, axis=1) + EPS)
    return hidden * inv_rms[:, None] * gain_vec[None, :]


def causal_conv(values, kernel, offset_bias, segment):
    kernel_len = kernel.shape[0]
    seq_len = values.shape[0]
    padded = jnp.pad(values, ((kernel_len - 1, 0), (0, 0)))
    seg_pad = jnp.pad(segment, (kernel_len - 1, 0), constant_values=-1)
    result = jnp.zeros_like(values) + offset_bias[None, :]
    for shift_at in range(kernel_len):
        matches = (seg_pad[shift_at : shift_at + seq_len] == segment).astype(jnp.float32)
        result = (
            result
            + kernel[shift_at][None, :] * padded[shift_at : shift_at + seq_len] * matches[:, None]
        )
    return result


def block_step(decay_rates, carried, block_in):
    x_block, dt_block, b_block, c_block, seg_block, seg_before = block_in
    block_rows = seg_block.shape[0]
    log_decay = jnp.cumsum(dt_block * decay_rates[None, :], axis=0)
    cum_heads = log_decay.T
    position = lax.iota(jnp.int32, block_rows)
    allowed = (position[:, None] >= position[None, :]) & (seg_block[:, None] == seg_block[None, :])
    log_gaps = jnp.where(allowed[None], cum_heads[:, :, None] - cum_heads[:, None, :], 0.0)
    decay_mat = jnp.where(allowed[None], jnp.exp(log_gaps), 0.0)
    query_key = jnp.dot(
        c_block, b_block.T, precision=lax.Precision.HIGHEST, preferred_element_type=jnp.float32
    )
    mixing = decay_mat * query_key[None] * dt_block.T[:, None, :]
    within = jnp.einsum("hts,shp->thp", mixing, x_block, precision=lax.Precision.HIGHEST)
    carry_on = (seg_block == seg_before).astype(jnp.float32)
    from_state = jnp.einsum("tn,hpn->thp", c_block, carried, precision=lax.Precision.HIGHEST)
    from_past = from_state * (jnp.exp(log_decay) * carry_on[:, None])[:, :, None]
    last_seg = seg_block[block_rows - 1]
    tail_weight = (
        jnp.exp(log_decay[block_rows - 1][None, :] - log_decay)
        * (seg_block == last_seg).astype(jnp.float32)[:, None]
        * dt_block
    )
    keep_state = jnp.exp(log_decay[block_rows - 1]) * (last_seg == seg_before).astype(jnp.float32)
    new_state = carried * keep_state[:, None, None] + jnp.einsum(
        "sh,sn,shp->hpn", tail_weight, b_block, x_block, precision=lax.Precision.HIGHEST
    )
    return (new_state, within + from_past)


def scan_ssd(x_heads, step_sizes, decay_rates, b_all, c_all, segment):
    seq_len, head_count, head_size = x_heads.shape
    blocks = seq_len // GROUP
    state_size = b_all.shape[1]
    seg_blocks = segment.reshape(blocks, GROUP)
    seg_before = jnp.concatenate([jnp.full((1,), -1, dtype=jnp.int32), seg_blocks[:-1, GROUP - 1]])
    initial = jnp.zeros((head_count, head_size, state_size), jnp.float32)
    stepper = jax.checkpoint(block_step)

    def scan_body(carried, block_in):
        return stepper(decay_rates, carried, block_in)

    final_state, outputs = lax.scan(
        scan_body,
        initial,
        (
            x_heads.reshape(blocks, GROUP, head_count, head_size),
            step_sizes.reshape(blocks, GROUP, head_count),
            b_all.reshape(blocks, GROUP, state_size),
            c_all.reshape(blocks, GROUP, state_size),
            seg_blocks,
            seg_before,
        ),
    )
    return outputs.reshape(seq_len, head_count, head_size)


def ssm_mixer(
    x_proj,
    bc_proj,
    dt_proj,
    gate_proj,
    conv_x,
    conv_bias_x,
    conv_bc,
    conv_bias_bc,
    dt_bias,
    a_log,
    skip_d,
    segment,
):
    x_conv = jax.nn.silu(causal_conv(x_proj, conv_x, conv_bias_x, segment))
    bc_conv = jax.nn.silu(causal_conv(bc_proj, conv_bc, conv_bias_bc, segment))
    state_size = bc_conv.shape[1] // 2
    step_sizes = jax.nn.softplus(dt_proj + dt_bias[None, :])
    decay_rates = -jnp.exp(a_log)
    seq_len = x_proj.shape[0]
    head_count = dt_proj.shape[1]
    x_heads = x_conv.reshape(seq_len, head_count, -1)
    scanned = scan_ssd(
        x_heads, step_sizes, decay_rates, bc_conv[:, :state_size], bc_conv[:, state_size:], segment
    )
    scanned = scanned + skip_d[None, :, None] * x_heads
    return scanned.reshape(seq_len, -1) * jax.nn.silu(gate_proj)


def times_transposed(left, right):
    return lax.dot_general(
        left, right, (((1,), (1,)), ((), ())), preferred_element_type=jnp.float32
    )


def rows_product(left, right):
    return lax.dot_general(
        left, right, (((0,), (0,)), ((), ())), preferred_element_type=jnp.float32
    )


def spread_out(local_part, whole_like, tensor_at):
    last_axis = local_part.ndim - 1
    zeros_whole = jnp.zeros(whole_like.shape, jnp.float32)
    return lax.dynamic_update_slice_in_dim(
        zeros_whole, local_part, tensor_at * local_part.shape[last_axis], last_axis
    )


def per_device(
    hidden_in,
    seg_ids,
    pre_gain,
    proj_gate,
    proj_x,
    proj_bc,
    proj_dt,
    conv_x,
    conv_bias_x,
    conv_bc,
    conv_bias_bc,
    dt_bias,
    a_log,
    skip_d,
    gate_gain,
    proj_out,
    cotangent,
):
    tensor_at = lax.axis_index("tensor")
    inner_dev = proj_gate.shape[1]
    heads_dev = proj_dt.shape[1]
    conv_x_dev = lax.dynamic_slice_in_dim(conv_x, tensor_at * inner_dev, inner_dev, 1)
    bias_x_dev = lax.dynamic_slice_in_dim(conv_bias_x, tensor_at * inner_dev, inner_dev, 0)
    dt_bias_dev = lax.dynamic_slice_in_dim(dt_bias, tensor_at * heads_dev, heads_dev, 0)
    a_log_dev = lax.dynamic_slice_in_dim(a_log, tensor_at * heads_dev, heads_dev, 0)
    skip_dev = lax.dynamic_slice_in_dim(skip_d, tensor_at * heads_dev, heads_dev, 0)
    gain_dev = lax.dynamic_slice_in_dim(gate_gain, tensor_at * inner_dev, inner_dev, 0)
    hidden = hidden_in.astype(jnp.float32)
    normed_own, norm_back = jax.vjp(pre_norm, hidden, pre_gain)
    normed_all = lax.all_gather(normed_own.astype(jnp.bfloat16), "tensor", axis=0, tiled=True)
    pieces = (
        lax.all_gather(proj_gate, "dp", axis=0, tiled=True),
        lax.all_gather(proj_x, "dp", axis=0, tiled=True),
        lax.all_gather(proj_bc, "dp", axis=0, tiled=True),
        lax.all_gather(proj_dt, "dp", axis=0, tiled=True),
    )
    columns = normed_all
    gate_val, x_val, bc_val, dt_val = tuple(
        (jnp.dot(columns, piece_one, preferred_element_type=jnp.float32) for piece_one in pieces)
    )

    def local_mixer(
        x_proj,
        bc_proj,
        dt_proj,
        gate_proj,
        conv_x_in,
        bias_x_in,
        conv_bc_in,
        bias_bc_in,
        dt_bias_in,
        a_log_in,
        skip_in,
    ):
        return ssm_mixer(
            x_proj,
            bc_proj,
            dt_proj,
            gate_proj,
            conv_x_in,
            bias_x_in,
            conv_bc_in,
            bias_bc_in,
            dt_bias_in,
            a_log_in,
            skip_in,
            seg_ids,
        )

    gated_out, mixer_back = jax.vjp(
        local_mixer,
        x_val,
        bc_val,
        dt_val,
        gate_val,
        conv_x_dev,
        bias_x_dev,
        conv_bc,
        conv_bias_bc,
        dt_bias_dev,
        a_log_dev,
        skip_dev,
    )
    square_sum = lax.psum(jnp.sum(gated_out * gated_out, axis=1), "tensor")
    inv_scale = lax.rsqrt(square_sum / INNER + EPS)
    normed_out = (gated_out * inv_scale[:, None] * gain_dev[None, :]).astype(jnp.bfloat16)
    partial_out = jnp.dot(
        normed_out,
        lax.all_gather(proj_out, "dp", axis=1, tiled=True),
        preferred_element_type=jnp.float32,
    )
    own_out = lax.psum_scatter(partial_out, "tensor", scatter_dimension=0, tiled=True)
    output = (hidden + own_out).astype(jnp.bfloat16)
    cot_all = lax.all_gather(cotangent, "tensor", axis=0, tiled=True)
    columns = cot_all
    grad_normed_out = times_transposed(columns, lax.all_gather(proj_out, "dp", axis=1, tiled=True))
    grad_out_t = rows_product(cot_all, normed_out)
    scaled_grad = grad_normed_out * gain_dev[None, :]
    grad_gain_dev = jnp.sum(grad_normed_out * gated_out * inv_scale[:, None], axis=0)
    cross_sum = lax.psum(jnp.sum(scaled_grad * gated_out, axis=1), "tensor")
    grad_gated = (
        scaled_grad * inv_scale[:, None]
        - gated_out * (inv_scale * inv_scale * inv_scale * cross_sum / INNER)[:, None]
    )
    (
        grad_x,
        grad_bc_part,
        grad_dt,
        grad_gate,
        grad_conv_x,
        grad_bias_x,
        grad_conv_bc,
        grad_bias_bc,
        grad_dt_bias,
        grad_a_log,
        grad_skip,
    ) = mixer_back(grad_gated)
    grad_bc = lax.psum(grad_bc_part, "tensor")
    low_gate = grad_gate.astype(jnp.bfloat16)
    low_x = grad_x.astype(jnp.bfloat16)
    low_bc = grad_bc.astype(jnp.bfloat16)
    low_dt = grad_dt.astype(jnp.bfloat16)
    is_first = tensor_at == 0
    pieces = (
        lax.all_gather(proj_gate, "dp", axis=0, tiled=True),
        lax.all_gather(proj_x, "dp", axis=0, tiled=True),
        lax.all_gather(proj_bc, "dp", axis=0, tiled=True),
        lax.all_gather(proj_dt, "dp", axis=0, tiled=True),
    )
    block_sum = (
        times_transposed(low_gate, pieces[0])
        + times_transposed(low_x, pieces[1])
        + times_transposed(low_dt, pieces[3])
    )
    block_sum = block_sum + jnp.where(is_first, times_transposed(low_bc, pieces[2]), 0.0)
    grad_normed_own = lax.psum_scatter(block_sum, "tensor", scatter_dimension=0, tiled=True)
    grad_hidden_norm, grad_pre_gain = norm_back(grad_normed_own)
    grad_hidden = cotangent.astype(jnp.float32) + grad_hidden_norm
    term_gate = rows_product(normed_all, low_gate)
    term_x = rows_product(normed_all, low_x)
    term_bc = rows_product(normed_all, low_bc)
    term_dt = rows_product(normed_all, low_dt)
    grad_sums = (
        lax.psum_scatter(term_gate, "dp", scatter_dimension=0, tiled=True),
        lax.psum_scatter(term_x, "dp", scatter_dimension=0, tiled=True),
        lax.psum_scatter(term_bc, "dp", scatter_dimension=0, tiled=True),
        lax.psum_scatter(term_dt, "dp", scatter_dimension=0, tiled=True),
        lax.psum_scatter(grad_out_t, "dp", scatter_dimension=0, tiled=True),
    )
    grad_proj_out = grad_sums[4].T
    small_sums = lax.psum(
        (
            grad_pre_gain,
            spread_out(grad_conv_x, conv_x, tensor_at),
            spread_out(grad_bias_x, conv_bias_x, tensor_at),
            grad_conv_bc,
            grad_bias_bc,
            spread_out(grad_dt_bias, dt_bias, tensor_at),
            spread_out(grad_a_log, a_log, tensor_at),
            spread_out(grad_skip, skip_d, tensor_at),
            spread_out(grad_gain_dev, gate_gain, tensor_at),
        ),
        ("dp", "tensor"),
    )
    return (
        output,
        grad_hidden,
        small_sums[0],
        grad_sums[0],
        grad_sums[1],
        grad_sums[2],
        grad_sums[3],
        small_sums[1],
        small_sums[2],
        small_sums[3],
        small_sums[4],
        small_sums[5],
        small_sums[6],
        small_sums[7],
        small_sums[8],
        grad_proj_out,
    )


def solution(mesh):
    in_specs = (
        P(("dp", "tensor"), None),
        P("dp"),
        P(),
        P("dp", "tensor"),
        P("dp", "tensor"),
        P("dp", None),
        P("dp", "tensor"),
        P(),
        P(),
        P(),
        P(),
        P(),
        P(),
        P(),
        P(),
        P("tensor", "dp"),
        P(("dp", "tensor"), None),
    )
    out_specs = (
        P(("dp", "tensor"), None),
        P(("dp", "tensor"), None),
        P(),
        P("dp", "tensor"),
        P("dp", "tensor"),
        P("dp", None),
        P("dp", "tensor"),
        P(),
        P(),
        P(),
        P(),
        P(),
        P(),
        P(),
        P(),
        P("tensor", "dp"),
    )
    return jax.shard_map(
        per_device, mesh=mesh, in_specs=in_specs, out_specs=out_specs, check_vma=False
    )
```

profile of v0, /device:TPU:1, one launch (start us, length us, event | category | flops | bytes accessed | tf_op | source)
XLA Modules:
  0.0 2154.1 jit_solution(3108408218932056675)
XLA Ops:
  20.7 84.3 %all-gather = bf16[32,48,12]{1,2,0:T(8,128)(2,1)S(1)} all-gather(bf16[1,48,12]{1,2,0:T(8,128)(2,1)S(1)} %bitcast.396), channel_id=1, replica_groups=mesh['dp'=32,'tensor'=4] {'dp'}, dimensions={0}, use_global_device_ids=true | all-gather | bytes 38016 | tf_op jit(solution)/shard_map/all_gather | solution.py:174
  105.8 83.8 %all_gather.29 = bf16[1536,256]{1,0:T(8,128)(2,1)} all-gather(bf16[48,256]{1,0:T(8,128)(2,1)S(1)} %copy-done.51), channel_id=1, replica_groups=mesh['dp'=32,'tensor'=4] {'dp'}, dimensions={0}, use_global_device_ids=true | all-gather | bytes 811008 | tf_op jit(solution)/shard_map/all_gather | solution.py:173
  191.8 3.7 compare_select_fusion.2
  204.8 4.3 fusion.143
  209.2 4.3 fusion.99
  215.9 3.0 reshape.463
  218.9 4.2 copy.160
  225.4 156.4 %while.42 = (s32[]{:T(128)}, f32[12,64,128]{2,1,0:T(8,128)S(1)}, f32[4,256,12,64]{1,0,3,2:T(4,128)}, f32[4,12,64,128]{3,2,1,0:T(8,128)}, f32[4,256,12]{1,2,0:T(8...) while((s32[]{:T(128)}, f32[12,64,128]{2,1,0:T(8,128)S(1)}, ...), condition=%wide.region_4.5_spmd.clone, body=%wide.region_1.4_spmd.clone.sunk | while | flops 1314242560 | bytes 10592042 | solution.py:75
  236.1 5.0 fusion.239
  246.5 17.9 dynamic_update_slice.94
  275.1 5.0 fusion.239
  285.6 17.9 dynamic_update_slice.94
  314.1 5.0 fusion.239
  324.5 17.9 dynamic_update_slice.94
  353.1 5.0 fusion.239
  363.5 17.9 dynamic_update_slice.94
  381.8 4.3 copy.229
  386.1 3.7 copy.162
  389.9 8.1 multiply_reduce_fusion.11
  397.9 33.1 %psum.84 = f32[1024]{0:T(1024)S(1)} all-reduce(f32[1024]{0:T(1024)S(1)} %get-tuple-element.933), channel_id=1, replica_groups=mesh['dp'=32,'tensor'=4] {'tensor'}, use_global_device_ids=true, to_apply=%region_6.7 | all-reduce | flops 1024 | bytes 8192 | tf_op jit(solution)/shard_map/psum | solution.py:223
  431.1 8.5 multiply_reduce_fusion.4
  439.6 5.8 psum.85
  445.4 8.8 multiply_reduce_fusion.5
  454.2 2.6 copy.163
  456.8 5.2 reshape.467
  466.6 234.2 %while.43 = (s32[]{:T(128)}, f32[12]{0:T(128)}, f32[12,64,128]{2,1,0:T(8,128)S(1)}, f32[4,256,12,64]{1,0,3,2:T(4,128)}, f32[4,256,12]{1,0,2:T(4,128)}, /*index=5...) while((s32[]{:T(128)}, f32[12]{0:T(128)}, ...), condition=%wide.region_23.24_spmd.clone, body=%wide.region_10.23_spmd.clone.sunk | while | flops 3038949376 | bytes 26211572 | solution.py:75
  471.4 2.7 constant_dynamic-slice_fusion.7
  482.6 5.6 fusion.261
  490.7 2.9 fusion.265
  506.8 17.8 dynamic_update_slice.97
  529.3 2.7 constant_dynamic-slice_fusion.7
  540.6 5.6 fusion.261
  548.6 2.9 fusion.265
  565.4 17.8 dynamic_update_slice.97
  587.9 2.7 constant_dynamic-slice_fusion.7
  599.1 5.6 fusion.261
  607.2 2.9 fusion.265
  624.0 17.8 dynamic_update_slice.97
  646.5 2.7 constant_dynamic-slice_fusion.7
  657.7 5.6 fusion.261
  665.7 2.9 fusion.265
  682.6 17.8 dynamic_update_slice.97
  702.7 4.6 fusion.121
  711.8 3.7 copy.168
  715.6 10.4 multiply_reduce_fusion.9
  729.7 28.3 %all-reduce.28 = bf16[1024,256]{1,0:T(8,128)(2,1)} all-reduce(f32[1024,256]{1,0:T(8,128)} %pad_add_fusion.3), channel_id=1, replica_groups=mesh['dp'=32,'tensor'=4] {'tensor'}, use_global_device_ids=true, to_apply=%region_24.25 | all-reduce | flops 262144 | bytes 1572864 | tf_op jit(solution)/shard_map/psum | solution.py:257
  761.9 2.6 fusion.145
  764.6 2.6 fusion.146
  767.3 3.9 select_add_fusion
  773.1 6.4 fusion.133
  781.4 3.2 fusion.149
  784.7 7.8 convolution_bitcast_fusion.2
  792.5 6.1 copy.177
  798.7 6.0 fusion.147
  804.7 5.8 fusion.148
  813.4 113.1 %reduce-scatter.22.cloned.1.call-done = f32[48,12]{1,0:T(8,128)} async-done(((f32[1536,12]{1,0:T(8,128)}), f32[48,12]{1,0:T(8,128)}) %reduce-scatter.22.cloned.1.call-update) | async-done | bytes 2320
  927.8 62.9 %reduce-scatter.14.cloned.1.call-done = f32[256,1536]{1,0:T(8,128)} async-done(((f32[1024,1536]{1,0:T(8,128)}), f32[256,1536]{1,0:T(8,128)}) %reduce-scatter.14.cloned.1.call-update) | async-done | bytes 1572880 | tf_op jit(solution)/shard_map/reduce_scatter | solution.py:275
  993.4 63.3 %reduce-scatter.12.cloned.1.call-done = f32[256,1536]{1,0:T(8,128)} async-done(((f32[1024,1536]{1,0:T(8,128)}), f32[256,1536]{1,0:T(8,128)}) %reduce-scatter.12.cloned.1.call-update) | async-done | bytes 1572880 | tf_op jit(solution)/shard_map/reduce_scatter | solution.py:231
  1056.8 3.3 fusion.104
  1060.1 224.4 %reduce-scatter.20.cloned.1.call-done = f32[48,256]{1,0:T(8,128)} async-done(((f32[1536,256]{1,0:T(8,128)}), f32[48,256]{1,0:T(8,128)}) %reduce-scatter.20.cloned.1.call-update) | async-done | bytes 49168 | tf_op jit(solution)/shard_map/reduce_scatter | solution.py:285
  1284.5 233.6 %reduce-scatter.24.cloned.1.call-done = f32[48,768]{1,0:T(8,128)} async-done(((f32[1536,768]{1,0:T(8,128)}), f32[48,768]{1,0:T(8,128)}) %reduce-scatter.24.cloned.1.call-update) | async-done | bytes 147472
  1518.1 234.4 %reduce-scatter.16.cloned.1.call-done = f32[48,768]{1,0:T(8,128)} async-done(((f32[1536,768]{1,0:T(8,128)}), f32[48,768]{1,0:T(8,128)}) %reduce-scatter.16.cloned.1.call-update) | async-done | bytes 147472 | tf_op jit(solution)/shard_map/reduce_scatter | solution.py:283
  1752.5 233.4 %reduce-scatter.18.cloned.1.call-done = f32[48,768]{1,0:T(8,128)} async-done(((f32[1536,768]{1,0:T(8,128)}), f32[48,768]{1,0:T(8,128)}) %reduce-scatter.18.cloned.1.call-update) | async-done | bytes 147472 | tf_op jit(solution)/shard_map/reduce_scatter | solution.py:284
  1985.9 150.2 %all-reduce.27.cloned.1.call-done = (f32[1536]{0:T(1024)}, f32[4,3072]{1,0:T(4,128)}, f32[3072]{0:T(1024)}, f32[4,256]{1,0:T(4,128)}, f32[256]{0:T(256)}, /*inde...) async-done(((f32[1536]{0:T(1024)}, f32[4,3072]{1,0:T(4,128)}, f32[3072]{0:T(1024)}, f32[4,256]{1,0:T(4,128)}, f32[256]{0:T(256)}, /*index=5*/f32[48]{0:T(128)}, ...) | async-done | bytes 85584 | tf_op jit(solution)/shard_map/psum | solution.py:290
  (609 shorter events, 240.7 us)
Async XLA Ops:
  7.2 6.5 copy-start.76
  7.2 7.7 copy-start.55
  7.2 8.4 copy-start.80
  7.2 9.0 copy-start.81
  7.2 12.1 copy-start.70
  7.2 13.4 copy-start.69
  7.2 98.6 %copy-start.51 = (bf16[48,256]{1,0:T(8,128)(2,1)S(1)}, bf16[48,256]{1,0:T(8,128)(2,1)}, u32[]{:S(2)}) copy-start(bf16[48,256]{1,0:T(8,128)(2,1)} %param.26) | copy-start | bytes 73732
  7.3 184.5 %all-gather.7.cloned.1.call-start = ((), (), s32[]{:S(2)}) async-start(), calls=%async_computation.7 | async-start | bytes 3932160 | tf_op jit(solution)/shard_map/all_gather | solution.py:169
  8.7 6.9 copy-start.67
  8.7 6.9 copy-start.56
  11.0 193.8 %all-gather.9.cloned.1.call-start = ((), (), s32[]{:S(2)}) async-start(), calls=%async_computation.8 | async-start | bytes 2433024 | tf_op jit(solution)/shard_map/all_gather | solution.py:172
  11.7 378.1 %all-gather.11.cloned.1.call-start = ((), (), s32[]{:S(2)}) async-start(), calls=%async_computation.9 | async-start | bytes 2433024 | tf_op jit(solution)/shard_map/all_gather | solution.py:171
  12.5 418.6 %all-gather.13.cloned.1.call-start = ((), (), s32[]{:S(2)}) async-start(), calls=%async_computation.10 | async-start | bytes 2433024 | tf_op jit(solution)/shard_map/all_gather | solution.py:228
  13.0 418.0 %all-gather.15.cloned.1.call-start = ((), (), s32[]{:S(2)}) async-start(), calls=%async_computation.12 | async-start | bytes 3932160 | tf_op jit(solution)/shard_map/all_gather | solution.py:233
  13.6 912.8 %reduce-scatter.22.cloned.1.call-start = ((), (), s32[]{:S(2)}) async-start(), calls=%async_computation.17 | async-start | bytes 811008
  15.6 193.6 %copy-start.31 = (f32[1024]{0:T(1024)}, f32[1024]{0:T(1024)S(1)}, u32[]{:S(2)}) copy-start(f32[1024]{0:T(1024)S(1)} %get-tuple-element.976) | copy-start | bytes 12292
  15.6 193.6 %copy-start.33 = (f32[1024]{0:T(1024)}, f32[1024]{0:T(1024)S(1)}, u32[]{:S(2)}) copy-start(f32[1024]{0:T(1024)S(1)} %get-tuple-element.977) | copy-start | bytes 12292
  15.6 193.6 %copy-start.35 = (f32[1024]{0:T(1024)}, f32[1024]{0:T(1024)S(1)}, u32[]{:S(2)}) copy-start(f32[1024]{0:T(1024)S(1)} %get-tuple-element.978) | copy-start | bytes 12292
  17.9 427.5 %copy-start.26 = (f32[768]{0:T(1024)}, f32[768]{0:T(1024)S(1)}, u32[]{:S(2)}) copy-start(f32[768]{0:T(1024)S(1)} %dynamic_slice.137) | copy-start | bytes 9220
  191.8 6.6 copy-start.2
  431.0 14.4 copy-start.28
  478.8 15.7 copy-start.25
  480.5 14.0 copy-start.12
  480.7 13.8 copy-start.30
  489.1 5.4 copy-start.13
  536.7 15.7 copy-start.25
  538.5 14.0 copy-start.12
  538.7 13.8 copy-start.30
  547.0 5.5 copy-start.13
  595.3 15.7 copy-start.25
  597.0 14.0 copy-start.12
  597.2 13.8 copy-start.30
  605.6 5.5 copy-start.13
  653.9 15.7 copy-start.25
  655.6 14.0 copy-start.12
  655.8 13.8 copy-start.30
  709.2 281.5 %reduce-scatter.14.cloned.1.call-start = ((), (), s32[]{:S(2)}) async-start(), calls=%async_computation.13 | async-start | bytes 7864320 | tf_op jit(solution)/shard_map/reduce_scatter | solution.py:275
  715.5 10.5 copy-start.16
  715.5 10.5 copy-start.17
  715.5 10.5 copy-start.21
  715.6 10.5 copy-start.22
  728.4 29.7 %copy-start.10 = (f32[1024,768]{1,0:T(8,128)S(1)}, f32[1024,768]{1,0:T(8,128)}, u32[]{:S(2)}) copy-start(f32[1024,768]{1,0:T(8,128)} %get-tuple-element.932) | copy-start | bytes 9437188
  728.4 29.7 %copy-start.42 = (f32[768]{0:T(1024)S(1)}, f32[768]{0:T(1024)}, u32[]{:S(2)}) copy-start(f32[768]{0:T(1024)} %get-tuple-element.860) | copy-start | bytes 9220
  728.4 29.7 %copy-start.44 = (f32[768]{0:T(1024)S(1)}, f32[768]{0:T(1024)}, u32[]{:S(2)}) copy-start(f32[768]{0:T(1024)} %get-tuple-element.861) | copy-start | bytes 9220
  728.4 29.7 %copy-start.46 = (f32[768]{0:T(1024)S(1)}, f32[768]{0:T(1024)}, u32[]{:S(2)}) copy-start(f32[768]{0:T(1024)} %get-tuple-element.862) | copy-start | bytes 9220
  728.5 29.7 %copy-start.48 = (f32[768]{0:T(1024)S(1)}, f32[768]{0:T(1024)}, u32[]{:S(2)}) copy-start(f32[768]{0:T(1024)} %get-tuple-element.863) | copy-start | bytes 9220
  771.2 285.5 %reduce-scatter.12.cloned.1.call-start = ((), (), s32[]{:S(2)}) async-start(), calls=%async_computation.11 | async-start | bytes 7864320 | tf_op jit(solution)/shard_map/reduce_scatter | solution.py:231
  779.5 505.0 %reduce-scatter.20.cloned.1.call-start = ((), (), s32[]{:S(2)}) async-start(), calls=%async_computation.16 | async-start | bytes 1622016 | tf_op jit(solution)/shard_map/reduce_scatter | solution.py:285
  784.7 733.5 %reduce-scatter.24.cloned.1.call-start = ((), (), s32[]{:S(2)}) async-start(), calls=%async_computation.18 | async-start | bytes 4866048
  798.6 953.9 %reduce-scatter.16.cloned.1.call-start = ((), (), s32[]{:S(2)}) async-start(), calls=%async_computation.14 | async-start | bytes 4866048 | tf_op jit(solution)/shard_map/reduce_scatter | solution.py:283
  804.6 1181.3 %reduce-scatter.18.cloned.1.call-start = ((), (), s32[]{:S(2)}) async-start(), calls=%async_computation.15 | async-start | bytes 4866048 | tf_op jit(solution)/shard_map/reduce_scatter | solution.py:284
  810.5 180.2 %copy-start.8 = (bf16[256,1536]{1,0:T(8,128)(2,1)S(1)}, bf16[256,1536]{1,0:T(8,128)(2,1)}, u32[]{:S(2)}) copy-start(bf16[256,1536]{1,0:T(8,128)(2,1)} %param.21) | copy-start | bytes 2359300
  810.5 180.2 %copy-start.38 = (f32[1536]{0:T(1024)S(1)}, f32[1536]{0:T(1024)}, u32[]{:S(2)}) copy-start(f32[1536]{0:T(1024)} %param.23) | copy-start | bytes 18436
  810.6 180.2 %copy-start.57 = (f32[256]{0:T(256)S(1)}, f32[256]{0:T(256)}, u32[]{:S(2)}) copy-start(f32[256]{0:T(256)} %copy-done.56) | copy-start | bytes 3076
  810.6 182.8 %copy-start.68 = (f32[256]{0:T(256)S(1)}, f32[256]{0:T(256)}, u32[]{:S(2)}) copy-start(f32[256]{0:T(256)} %copy-done.67) | copy-start | bytes 3076
  810.6 246.2 %copy-start.19 = (bf16[256,1536]{1,0:T(8,128)(2,1)S(1)}, bf16[256,1536]{1,0:T(8,128)(2,1)}, u32[]{:S(2)}) copy-start(bf16[256,1536]{1,0:T(8,128)(2,1)} %param.37) | copy-start | bytes 2359300
  810.6 1325.5 %all-reduce.27.cloned.1.call-start = ((), (), s32[]{:S(2)}) async-start(), calls=%async_computation.19 | async-start | bytes 177152 | tf_op jit(solution)/shard_map/psum | solution.py:290
  811.6 181.7 %copy-start.39 = (f32[3072]{0:T(1024)}, f32[3072]{0:T(1024)S(1)}, u32[]{:S(2)}) copy-start(f32[3072]{0:T(1024)S(1)} %dynamic_update_slice.75) | copy-start | bytes 36868
  812.0 181.4 %copy-start.74 = (f32[48]{0:T(128)}, f32[48]{0:T(128)S(1)}, u32[]{:S(2)}) copy-start(f32[48]{0:T(128)S(1)} %dynamic_update_slice.74) | copy-start | bytes 580
  812.2 181.2 %copy-start.75 = (f32[48]{0:T(128)}, f32[48]{0:T(128)S(1)}, u32[]{:S(2)}) copy-start(f32[48]{0:T(128)S(1)} %dynamic_update_slice.72) | copy-start | bytes 580
  812.5 180.9 %copy-start.40 = (f32[3072]{0:T(1024)}, f32[3072]{0:T(1024)S(1)}, u32[]{:S(2)}) copy-start(f32[3072]{0:T(1024)S(1)} %dynamic_update_slice.71) | copy-start | bytes 36868
  813.1 180.3 %copy-start.37 = (f32[4,3072]{1,0:T(4,128)}, f32[4,3072]{1,0:T(4,128)S(1)}, u32[]{:S(2)}) copy-start(f32[4,3072]{1,0:T(4,128)S(1)} %add_dynamic-update-slice_fusion) | copy-start | bytes 147460
  813.4 180.1 %copy-start.73 = (f32[48]{0:T(128)}, f32[48]{0:T(128)S(1)}, u32[]{:S(2)}) copy-start(f32[48]{0:T(128)S(1)} %multiply_dynamic-update-slice_fusion) | copy-start | bytes 580
  990.7 66.0 %copy-start.14 = (f32[256,1536]{1,0:T(8,128)S(1)}, f32[256,1536]{1,0:T(8,128)}, u32[]{:S(2)}) copy-start(f32[256,1536]{1,0:T(8,128)} %reduce-scatter.14.cloned.1.call-done) | copy-start | bytes 4718596
  (45 other events, 137.6 us)
Sparse Core Ops, SparseCore 0:
  11.1 42.5 all-gather.6
  56.7 72.1 all-gather.8
  131.8 71.1 all-gather.10
  205.8 68.8 all-gather.12
  276.1 36.6 all-gather.14
  709.3 217.0 reduce-scatter.21
  929.0 61.7 reduce-scatter.13
  993.3 63.4 reduce-scatter.11
  1063.0 221.4 reduce-scatter.19
  1290.1 227.9 reduce-scatter.23
  1524.7 227.7 reduce-scatter.15
  1758.1 227.8 reduce-scatter.17
  1994.6 141.5 all-reduce.26
where the time goes:
time: 2160 us; the launch traced here: 2150 us
  waiting for transfers between devices  1320 us (61%)
  local copies, waits for them, and re-layouts  293 us (14%)
  blocking collectives  235 us (11%)
  matrix products  180 us (8%)
  other arithmetic  99.8 us (5%)
    unnamed x15, waiting for transfers between devices  349 us
    reduce_scatter x1, waiting for transfers between devices, per_device(): lax.psum_scatter(term_gate, 'dp', scatter_dimension=0, tiled=True)  234 us
    reduce_scatter x1, waiting for transfers between devices, per_device(): lax.psum_scatter(term_x, 'dp', scatter_dimension=0, tiled=True)  233 us
    reduce_scatter x1, waiting for transfers between devices, per_device(): lax.psum_scatter(term_bc, 'dp', scatter_dimension=0, tiled=True)  224 us
    dynamic_update_slice x24, local copies, waits for them, and re-layouts, scan_ssd(): lax.scan(scan_body, initial, (x_heads.reshape(blocks, GROUP, head_count,...  155 us
    psum x1, waiting for transfers between devices, per_device(): lax.psum((grad_pre_gain, spread_out(grad_conv_x, conv_x, tensor_at), spre...  150 us
    all_gather x1, blocking collectives, per_device(): lax.all_gather(proj_dt, 'dp', axis=0, tiled=True)  84.3 us
    all_gather x1, blocking collectives, per_device(): lax.all_gather(proj_bc, 'dp', axis=0, tiled=True)  83.8 us
  transfers between devices with their start and end apart: 13, of which 8 were waited for; matrix products, arithmetic and copies ran while one was open for 13% of the time, Pallas kernels for 0%

commit v1 on v0

v1 whole, which is shorter than its diff:
```python
import functools

import jax
import jax.numpy as jnp
from jax import lax
from jax.experimental import pallas as pl
from jax.experimental.pallas import tpu as pltpu
from jax.sharding import PartitionSpec as P

MESH = pl.DeviceIdType.MESH
F32 = jnp.float32
BF = jnp.bfloat16


def place():
    dp = lax.axis_index("dp")
    t = lax.axis_index("tensor")
    return dp // 8, (dp // 2) % 4, dp % 2, t


def dev(x, z, yh, t):
    return ((x * 4 + z) * 2 + yh, t)


def ag_kernel(ten, wa, wb, h, c, oa, ob, oh, oc, lsem, wsend, wrecv, tsend, trecv):
    x, z, yh, t = place()
    yl = t // 2; co = t % 2
    m4 = lambda v: (v + 8) % 4
    def nb(axis, d):
        if axis == "x": return dev(m4(x + d), z, yh, t)
        return dev(x, m4(z + d), yh, t)
    ypeer = dev(x, z, 1 - yh, t)
    tc_ = dev(x, z, yh, yl * 2 + (1 - co))
    ty = dev(x, z, yh, (1 - yl) * 2 + co)
    bar = pltpu.get_barrier_semaphore()
    peers = [ypeer, nb("x", 1), nb("x", -1), nb("z", 1), nb("z", -1), tc_, ty]
    for p in peers:
        pl.semaphore_signal(bar, inc=1, device_id=p, device_id_type=MESH)
    pl.semaphore_wait(bar, len(peers))
    sends = []
    def rc(src, dst, ss, rs, to):
        cp = pltpu.make_async_remote_copy(src_ref=src, dst_ref=dst, send_sem=ss, recv_sem=rs, device_id=to, device_id_type=MESH)
        cp.start(); sends.append(cp); return cp
    halves = ((wa, oa, "x", "z"), (wb, ob, "z", "x"))
    def blk(o, r1, d1, d2, y=None, yn=None):
        ix, iz = (m4(x + d1), m4(z + d2)) if r1 == "x" else (m4(x + d2), m4(z + d1))
        return o.at[ix, iz] if y is None else o.at[ix, iz, y]
    sem = [0, 0]
    def wc(i, src, dst, to):
        k = sem[i]; sem[i] += 1
        return rc(src, dst, wsend.at[i, k], wrecv.at[i, k], to)
    loc = []
    for i, (w, o, *_) in enumerate(halves):
        cp = pltpu.make_async_copy(w, o.at[x, z, yh], lsem.at[i]); cp.start(); loc.append(cp)
    for i, (s, o) in enumerate(((h, oh), (c, oc))):
        cp = pltpu.make_async_copy(s, o.at[t], lsem.at[2 + i]); cp.start(); loc.append(cp)
    yc = []; a0 = []; b0 = []
    for i, (w, o, r1, r2) in enumerate(halves):
        yc.append(wc(i, w, o.at[x, z, yh], ypeer))
    for i, (w, o, r1, r2) in enumerate(halves):
        me = o.at[x, z, yh]
        a0.append([wc(i, w, me, nb(r1, d)) for d in (1, -1)])
    for i, (w, o, r1, r2) in enumerate(halves):
        me = o.at[x, z, yh]
        b0.append([wc(i, w, me, nb(r2, d)) for d in (1, -1)])
    a1 = []; b1 = []
    for i, (w, o, r1, r2) in enumerate(halves):
        yc[i].wait_recv()
        pe = o.at[x, z, 1 - yh]
        a1.append([wc(i, pe, pe, nb(r1, d)) for d in (1, -1)])
    if ten:
        tc1 = []
        for i, (s, o) in enumerate(((h, oh), (c, oc))):
            a = rc(s, o.at[t], tsend.at[i, 0], trecv.at[i, 0], ty)
            b = rc(s, o.at[t], tsend.at[i, 1], trecv.at[i, 1], tc_)
            tc1.append((a, b))
    for i, (w, o, r1, r2) in enumerate(halves):
        pe = o.at[x, z, 1 - yh]
        b1.append([wc(i, pe, pe, nb(r2, d)) for d in (1, -1)])
    a2 = []; b2 = []
    for i, (w, o, r1, r2) in enumerate(halves):
        for k in (0, 1):
            a0[i][k].wait_recv(); a1[i][k].wait_recv()
        l_ = blk(o, r1, -1, 0, 0); r_ = blk(o, r1, 1, 0, 1)
        a2.append((wc(i, l_, l_, nb(r1, 1)), wc(i, r_, r_, nb(r1, -1))))
    for i, (w, o, r1, r2) in enumerate(halves):
        bb = []
        for d1 in (-1, 1):
            bl = blk(o, r1, d1, 0)
            bb.append([wc(i, bl, bl, nb(r2, d)) for d in (1, -1)])
        b2.append(bb)
    b3 = []
    for i, (w, o, r1, r2) in enumerate(halves):
        a2[i][0].wait_recv(); a2[i][1].wait_recv()
        bl = blk(o, r1, 2, 0)
        b3.append([wc(i, bl, bl, nb(r2, d)) for d in (1, -1)])
    if ten:
        tc2 = []
        for i, (s, o) in enumerate(((h, oh), (c, oc))):
            tc1[i][0].wait_recv()
            bk = o.at[(1 - yl) * 2 + co]
            tc2.append(rc(bk, bk, tsend.at[i, 2], trecv.at[i, 2], tc_))
    last = []
    def fw(i, o, r1, d1):
        l_ = blk(o, r1, d1, -1, 0); r_ = blk(o, r1, d1, 1, 1); n = halves[i][3]
        last.append(wc(i, l_, l_, nb(n, 1))); last.append(wc(i, r_, r_, nb(n, -1)))
    for i, (w, o, r1, r2) in enumerate(halves):
        for k in (0, 1):
            b0[i][k].wait_recv(); b1[i][k].wait_recv()
        fw(i, o, r1, 0)
    for i, (w, o, r1, r2) in enumerate(halves):
        for j, d1 in enumerate((-1, 1)):
            for k in (0, 1): b2[i][j][k].wait_recv()
            fw(i, o, r1, d1)
    for i, (w, o, r1, r2) in enumerate(halves):
        for k in (0, 1): b3[i][k].wait_recv()
        fw(i, o, r1, 2)
    for l in loc: l.wait()
    if ten:
        for i in range(2):
            tc1[i][1].wait_recv(); tc2[i].wait_recv()
    for cp in last: cp.wait_recv()
    for cp in sends: cp.wait_send()

def gather(wa, wb, h, c, ten=True, vm=False):
    anyspec = pl.BlockSpec(memory_space=pl.ANY)
    ospec = pl.BlockSpec(memory_space=pltpu.VMEM) if vm else anyspec
    ca, cb = wa.shape[1], wb.shape[1]
    outs = (jax.ShapeDtypeStruct((4, 4, 2, 48, ca), jnp.bfloat16), jax.ShapeDtypeStruct((4, 4, 2, 48, cb), jnp.bfloat16),
            jax.ShapeDtypeStruct((4, 256, 1536), jnp.bfloat16), jax.ShapeDtypeStruct((4, 256, 1536), jnp.bfloat16))
    return pl.pallas_call(functools.partial(ag_kernel, ten), out_shape=outs, in_specs=[anyspec] * 4, out_specs=[ospec] * 4,
        scratch_shapes=[pltpu.SemaphoreType.DMA((4,)), pltpu.SemaphoreType.DMA((2, 25)), pltpu.SemaphoreType.DMA((2, 25)),
                        pltpu.SemaphoreType.DMA((2, 3)), pltpu.SemaphoreType.DMA((2, 3))],
        compiler_params=pltpu.CompilerParams(collective_id=0, has_side_effects=True, vmem_limit_bytes=60*2**20), name="gather_all")(wa, wb, h, c)


def rs_kernel(ga, gb, po, pn, sv, oa, ob, oo, on, osv,
              va, vb, vo, vn, r1a, r1b, r2a, r2b, ha, hb, q1a, q1b, q2a, q2b, ka, kb, ya, yb,
              co_buf, cy_buf, cs_buf, sacc, sx, sz, sy, st, bct,
              lsem, wsend, wrecv, tsend, trecv, ssend, srecv):
    x, z, yh, t = place()
    yl = t // 2; co = t % 2
    m4 = lambda v: (v + 8) % 4
    def nb(axis, d):
        if axis == "x": return dev(m4(x + d), z, yh, t)
        return dev(x, m4(z + d), yh, t)
    ypeer = dev(x, z, 1 - yh, t)
    tcore = dev(x, z, yh, yl * 2 + (1 - co))
    tyl = dev(x, z, yh, (1 - yl) * 2 + co)
    tdiag = dev(x, z, yh, (1 - yl) * 2 + 1 - co)
    bar = pltpu.get_barrier_semaphore()
    peers = [ypeer, tcore, tyl, tdiag] + [nb(a, d) for a in "xz" for d in (1, 2, 3)]
    for p in peers:
        pl.semaphore_signal(bar, inc=1, device_id=p, device_id_type=MESH)
    loads = []
    for i, (s, d) in enumerate(((ga, va), (gb, vb), (po, vo), (pn, vn))):
        cp = pltpu.make_async_copy(s, d, lsem.at[i]); cp.start(); loads.append(cp)
    pl.semaphore_wait(bar, len(peers))
    sends = []
    def rc(src, dst, ss, rs, to):
        cp = pltpu.make_async_remote_copy(src_ref=src, dst_ref=dst, send_sem=ss, recv_sem=rs, device_id=to, device_id_type=MESH)
        cp.start(); sends.append(cp); return cp
    def acc(dst, idx, terms):
        pass
    pos = {"x": x, "z": z}
    halves = ((va, "z", "x", r1a, r2a, ha, q1a, q2a, ka, ya, oa), (vb, "x", "z", r1b, r2b, hb, q1b, q2b, kb, yb, ob))
    def b1(v, a1, d, k=None):
        p = m4(pos[a1] + d)
        if a1 == "z": return v.at[:, p] if k is None else v.at[pl.ds(2 * k, 2), p]
        return v.at[p] if k is None else v.at[p, pl.ds(2 * k, 2)]
    small = []
    for d in (1, 2, 3):
        small.append(rc(sv, sx.at[d - 1], ssend.at[d - 1], srecv.at[d - 1], nb("x", d)))
    for l in loads[:2]: l.wait()
    s1 = []
    for i, (v, a1, a2, r1, r2, *_) in enumerate(halves):
        s1.append((rc(b1(v, a1, 2, 0), r1.at[0], wsend.at[i, 0], wrecv.at[i, 0], nb(a1, 1)),
                   rc(b1(v, a1, 2, 1), r1.at[1], wsend.at[i, 1], wrecv.at[i, 1], nb(a1, -1))))
    s1b = []
    for i, (v, a1, a2, r1, r2, *_) in enumerate(halves):
        s1b.append((rc(b1(v, a1, 1, 1), r2.at[0, pl.ds(2, 2)], wsend.at[i, 2], wrecv.at[i, 2], nb(a1, 1)),
                    rc(b1(v, a1, -1, 0), r2.at[1, pl.ds(0, 2)], wsend.at[i, 3], wrecv.at[i, 3], nb(a1, -1))))
    tr = []
    for l in loads[2:]: l.wait()
    for i, v in enumerate((vo, vn)):
        a = rc(v.at[(1 - yl) * 2 + 1 - co], co_buf.at[i, 0], tsend.at[i, 0], trecv.at[i, 0], tcore)
        b = rc(v.at[yl * 2 + 1 - co], co_buf.at[i, 1], tsend.at[i, 1], trecv.at[i, 1], tcore)
        tr.append((a, b))
    for i, v in enumerate((vo, vn)):
        tr[i][0].wait_recv()
        def addc(j, _, i=i, v=v):
            rows = pl.ds(pl.multiple_of(j * 32, 32), 32)
            cs_buf[i, rows] = (v[(1 - yl) * 2 + co, rows].astype(F32) + co_buf[i, 0, rows].astype(F32)).astype(BF)
            return 0
        lax.fori_loop(0, 8, addc, 0)
        tr[i] = tr[i] + (rc(cs_buf.at[i], cy_buf.at[i], tsend.at[i, 2], trecv.at[i, 2], tyl),)
    for s in small: s.wait_recv()
    sacc[0] = sv[...] + sx[0] + sx[1] + sx[2]
    small = [rc(sacc.at[0], sz.at[d - 1], ssend.at[2 + d], srecv.at[2 + d], nb("z", d)) for d in (1, 2, 3)]
    s1c = []
    for i, (v, a1, a2, r1, r2, *_) in enumerate(halves):
        for side, dd, k in ((0, 1, 0), (1, -1, 1)):
            s1[i][side].wait_recv()
            p = m4(pos[a1] + dd)
            def add1(j, _, v=v, a1=a1, r1=r1, side=side, p=p, k=k):
                e = j // 2 ; y = j % 2
                if a1 == "z":
                    v[2 * k + e, p, y] = (v[2 * k + e, p, y].astype(F32) + r1[side, e, y].astype(F32)).astype(BF)
                else:
                    v[p, 2 * k + e, y] = (v[p, 2 * k + e, y].astype(F32) + r1[side, e, y].astype(F32)).astype(BF)
                return 0
            lax.fori_loop(0, 4, add1, 0)
            s1c.append(rc(b1(v, a1, dd, k), r2.at[side, pl.ds(2 * k, 2)], wsend.at[i, 4 + side], wrecv.at[i, 4 + side], nb(a1, dd)))
    for s in small: s.wait_recv()
    sacc[1] = sacc[0] + sz[0] + sz[1] + sz[2]
    small = [rc(sacc.at[1], sy, ssend.at[6], srecv.at[6], ypeer)]
    s2 = []
    for i, (v, a1, a2, r1, r2, h, q1, q2, kk, yy, oo_) in enumerate(halves):
        s1b[i][0].wait_recv(); s1b[i][1].wait_recv()
        s1c[2 * i].wait_recv(); s1c[2 * i + 1].wait_recv()
        p = pos[a1]
        def add2(j, _, v=v, a1=a1, r2=r2, h=h, p=p):
            e = j // 2; y = j % 2
            own = v[e, p, y] if a1 == "z" else v[p, e, y]
            h[e, y] = (own.astype(F32) + r2[0, e, y].astype(F32) + r2[1, e, y].astype(F32)).astype(BF)
            return 0
        lax.fori_loop(0, 8, add2, 0)
        q = pos[a2]
        s2.append((rc(h.at[m4(q + 2), 0], q1.at[0], wsend.at[i, 6], wrecv.at[i, 6], nb(a2, 1)),
                   rc(h.at[m4(q + 2), 1], q1.at[1], wsend.at[i, 7], wrecv.at[i, 7], nb(a2, -1)),
                   rc(h.at[m4(q + 1), 1], q2.at[0, 1], wsend.at[i, 8], wrecv.at[i, 8], nb(a2, 1)),
                   rc(h.at[m4(q - 1), 0], q2.at[1, 0], wsend.at[i, 9], wrecv.at[i, 9], nb(a2, -1))))
    for s in small: s.wait_recv()
    sacc[2] = sacc[1] + sy[...]
    small = [rc(sacc.at[2], st.at[j], ssend.at[7 + j], srecv.at[7 + j], d_) for j, d_ in enumerate((tcore, tyl, tdiag))]
    s2c = []
    for i, (v, a1, a2, r1, r2, h, q1, q2, kk, yy, oo_) in enumerate(halves):
        q = pos[a2]
        for side, dd in ((0, 1), (1, -1)):
            s2[i][side].wait_recv()
            pp = m4(q + dd)
            h[pp, side] = (h[pp, side].astype(F32) + q1[side].astype(F32)).astype(BF)
            s2c.append(rc(h.at[pp, side], q2.at[side, side], wsend.at[i, 10 + side], wrecv.at[i, 10 + side], nb(a2, dd)))
    s3 = []
    for i, (v, a1, a2, r1, r2, h, q1, q2, kk, yy, oo_) in enumerate(halves):
        q = pos[a2]
        s2[i][2].wait_recv(); s2[i][3].wait_recv()
        s2c[2 * i].wait_recv(); s2c[2 * i + 1].wait_recv()
        kk[...] = (h[q, 1 - yh].astype(F32) + q2[0, 1 - yh].astype(F32) + q2[1, 1 - yh].astype(F32)).astype(BF)
        s3.append(rc(kk, yy, wsend.at[i, 12], wrecv.at[i, 12], ypeer))
    for i, (v, o) in enumerate(((vo, oo), (vn, on))):
        tr[i][1].wait_recv(); tr[i][2].wait_recv()
        def addf(j, _, i=i, v=v, o=o):
            rows = pl.ds(pl.multiple_of(j * 32, 32), 32)
            o[rows] = v[t, rows].astype(F32) + co_buf[i, 1, rows].astype(F32) + cy_buf[i, rows].astype(F32)
            return 0
        lax.fori_loop(0, 8, addf, 0)
    for i, (v, a1, a2, r1, r2, h, q1, q2, kk, yy, o) in enumerate(halves):
        q = pos[a2]
        s3[i].wait_recv()
        o[...] = h[q, yh].astype(F32) + q2[0, yh].astype(F32) + q2[1, yh].astype(F32) + yy[...].astype(F32)
    for s in small: s.wait_recv()
    osv[t] = sacc[2]
    osv[yl * 2 + 1 - co] = st[0]
    osv[(1 - yl) * 2 + co] = st[1]
    osv[(1 - yl) * 2 + 1 - co] = st[2]
    for cp in sends: cp.wait_send()

def reduce_all(ga, gb, po, pn, sv):
    anys = pl.BlockSpec(memory_space=pl.ANY); vm = pl.BlockSpec(memory_space=pltpu.VMEM)
    ca, cb = ga.shape[-1], gb.shape[-1]; R = sv.shape[0]
    outs = (jax.ShapeDtypeStruct((48, ca), F32), jax.ShapeDtypeStruct((48, cb), F32), jax.ShapeDtypeStruct((256, 1536), F32),
            jax.ShapeDtypeStruct((256, 1536), F32), jax.ShapeDtypeStruct((4, R, 128), F32))
    D = pltpu.SemaphoreType.DMA
    V = lambda *s, d=BF: pltpu.VMEM(s, d)
    scratch = [V(4, 4, 2, 48, ca), V(4, 4, 2, 48, cb), V(4, 256, 1536), V(4, 256, 1536),
               V(2, 2, 2, 48, ca), V(2, 2, 2, 48, cb), V(2, 4, 2, 48, ca), V(2, 4, 2, 48, cb),
               V(4, 2, 48, ca), V(4, 2, 48, cb), V(2, 48, ca), V(2, 48, cb), V(2, 2, 48, ca), V(2, 2, 48, cb),
               V(48, ca), V(48, cb), V(48, ca), V(48, cb),
               V(2, 2, 256, 1536), V(2, 256, 1536), V(2, 256, 1536),
               V(3, R, 128, d=F32), V(3, R, 128, d=F32), V(3, R, 128, d=F32), V(R, 128, d=F32), V(3, R, 128, d=F32), V(8, 128, d=F32),
               D((4,)), D((2, 13)), D((2, 13)), D((2, 3)), D((2, 3)), D((10,)), D((10,))]
    return pl.pallas_call(rs_kernel, out_shape=outs, in_specs=[anys] * 4 + [vm], out_specs=[vm] * 5, scratch_shapes=scratch,
        compiler_params=pltpu.CompilerParams(collective_id=1, has_side_effects=True, vmem_limit_bytes=60 * 2**20), name="reduce_all")(ga, gb, po, pn, sv)


GROUP = 256
INNER = 3072
EPS = 1e-05


def causal_conv(values, kernel, offset_bias, segment):
    kernel_len = kernel.shape[0]
    seq_len = values.shape[0]
    padded = jnp.pad(values, ((kernel_len - 1, 0), (0, 0)))
    seg_pad = jnp.pad(segment, (kernel_len - 1, 0), constant_values=-1)
    result = jnp.zeros_like(values) + offset_bias[None, :]
    for shift_at in range(kernel_len):
        matches = (seg_pad[shift_at : shift_at + seq_len] == segment).astype(F32)
        result = result + kernel[shift_at][None, :] * padded[shift_at : shift_at + seq_len] * matches[:, None]
    return result


def block_step(decay_rates, carried, block_in):
    x_block, dt_block, b_block, c_block, seg_block, seg_before = block_in
    block_rows = seg_block.shape[0]
    log_decay = jnp.cumsum(dt_block * decay_rates[None, :], axis=0)
    cum_heads = log_decay.T
    position = lax.iota(jnp.int32, block_rows)
    allowed = (position[:, None] >= position[None, :]) & (seg_block[:, None] == seg_block[None, :])
    log_gaps = jnp.where(allowed[None], cum_heads[:, :, None] - cum_heads[:, None, :], 0.0)
    decay_mat = jnp.where(allowed[None], jnp.exp(log_gaps), 0.0)
    query_key = jnp.dot(c_block, b_block.T, precision=lax.Precision.HIGHEST, preferred_element_type=F32)
    mixing = decay_mat * query_key[None] * dt_block.T[:, None, :]
    within = jnp.einsum("hts,shp->thp", mixing, x_block, precision=lax.Precision.HIGHEST)
    carry_on = (seg_block == seg_before).astype(F32)
    from_state = jnp.einsum("tn,hpn->thp", c_block, carried, precision=lax.Precision.HIGHEST)
    from_past = from_state * (jnp.exp(log_decay) * carry_on[:, None])[:, :, None]
    last_seg = seg_block[block_rows - 1]
    tail_weight = (
        jnp.exp(log_decay[block_rows - 1][None, :] - log_decay)
        * (seg_block == last_seg).astype(F32)[:, None]
        * dt_block
    )
    keep_state = jnp.exp(log_decay[block_rows - 1]) * (last_seg == seg_before).astype(F32)
    new_state = carried * keep_state[:, None, None] + jnp.einsum(
        "sh,sn,shp->hpn", tail_weight, b_block, x_block, precision=lax.Precision.HIGHEST
    )
    return (new_state, within + from_past)


def scan_ssd(x_heads, step_sizes, decay_rates, b_all, c_all, segment):
    seq_len, head_count, head_size = x_heads.shape
    blocks = seq_len // GROUP
    state_size = b_all.shape[1]
    seg_blocks = segment.reshape(blocks, GROUP)
    seg_before = jnp.concatenate([jnp.full((1,), -1, dtype=jnp.int32), seg_blocks[:-1, GROUP - 1]])
    initial = jnp.zeros((head_count, head_size, state_size), F32)
    stepper = jax.checkpoint(block_step)

    def scan_body(carried, block_in):
        return stepper(decay_rates, carried, block_in)

    _, outputs = lax.scan(
        scan_body,
        initial,
        (
            x_heads.reshape(blocks, GROUP, head_count, head_size),
            step_sizes.reshape(blocks, GROUP, head_count),
            b_all.reshape(blocks, GROUP, state_size),
            c_all.reshape(blocks, GROUP, state_size),
            seg_blocks,
            seg_before,
        ),
    )
    return outputs.reshape(seq_len, head_count, head_size)


def ssm_mixer(segment, x_proj, bc_proj, dt_proj, gate_proj, conv_x, conv_bias_x, conv_bc, conv_bias_bc, dt_bias, a_log, skip_d):
    x_conv = jax.nn.silu(causal_conv(x_proj, conv_x, conv_bias_x, segment))
    bc_conv = jax.nn.silu(causal_conv(bc_proj, conv_bc, conv_bias_bc, segment))
    state_size = bc_conv.shape[1] // 2
    step_sizes = jax.nn.softplus(dt_proj + dt_bias[None, :])
    decay_rates = -jnp.exp(a_log)
    seq_len = x_proj.shape[0]
    head_count = dt_proj.shape[1]
    x_heads = x_conv.reshape(seq_len, head_count, -1)
    scanned = scan_ssd(
        x_heads, step_sizes, decay_rates, bc_conv[:, :state_size], bc_conv[:, state_size:], segment
    )
    scanned = scanned + skip_d[None, :, None] * x_heads
    return scanned.reshape(seq_len, -1) * jax.nn.silu(gate_proj)


def dot_nt(left, right):
    return lax.dot_general(left, right, (((1,), (1,)), ((), ())), preferred_element_type=F32)


def dot_tn(left, right):
    return lax.dot_general(left, right, (((0,), (0,)), ((), ())), preferred_element_type=F32)


def per_device(
    hidden_in, seg_ids, pre_gain, proj_gate, proj_x, proj_bc, proj_dt, conv_x, conv_bias_x, conv_bc, conv_bias_bc,
    dt_bias, a_log, skip_d, gate_gain, proj_out, cotangent,
):
    t = lax.axis_index("tensor")
    inner = proj_gate.shape[1]
    heads = proj_dt.shape[1]
    own = lambda v, n: lax.dynamic_slice_in_dim(v, t * n, n, v.ndim - 1)
    gain_dev = own(gate_gain, inner)
    hidden = hidden_in.astype(F32)
    inv_rms = lax.rsqrt(jnp.mean(hidden * hidden, axis=1) + EPS)
    normed_own = (hidden * inv_rms[:, None] * pre_gain[None, :]).astype(BF)
    rows = proj_x.shape[0]
    wa = jnp.concatenate([proj_x, proj_bc, proj_dt, jnp.zeros((rows, 128 - heads), BF)], axis=1)
    wb = jnp.concatenate([proj_gate, proj_out.T], axis=1)
    wa, wb, normed_all, cot_all = gather(wa, wb, normed_own, cotangent)
    wa = wa.reshape(-1, wa.shape[-1])
    wb = wb.reshape(-1, wb.shape[-1])
    normed_all = normed_all.reshape(-1, normed_all.shape[-1])
    cot_all = cot_all.reshape(-1, cot_all.shape[-1])
    w_gate, w_out = wb[:, :inner], wb[:, inner:]
    vals = jnp.dot(normed_all, wa, preferred_element_type=F32)
    x_val, bc_val, dt_val = vals[:, :inner], vals[:, inner : inner + 256], vals[:, inner + 256 : inner + 256 + heads]
    gate_val = jnp.dot(normed_all, w_gate, preferred_element_type=F32)
    gated, mixer_back = jax.vjp(
        functools.partial(ssm_mixer, seg_ids), x_val, bc_val, dt_val, gate_val,
        own(conv_x, inner), own(conv_bias_x, inner), conv_bc, conv_bias_bc, own(dt_bias, heads), own(a_log, heads), own(skip_d, heads),
    )
    grad_normed_out = jnp.dot(cot_all, w_out, preferred_element_type=F32)
    scaled_grad = grad_normed_out * gain_dev[None, :]
    sums = lax.psum(jnp.stack([jnp.sum(gated * gated, axis=1), jnp.sum(scaled_grad * gated, axis=1)]), "tensor")
    inv_scale = lax.rsqrt(sums[0] / INNER + EPS)
    normed_out = (gated * inv_scale[:, None] * gain_dev[None, :]).astype(BF)
    partial_out = dot_nt(normed_out, w_out).astype(BF)
    term_out = dot_tn(cot_all, normed_out)
    grad_gain_dev = jnp.sum(grad_normed_out * gated * inv_scale[:, None], axis=0)
    grad_gated = scaled_grad * inv_scale[:, None] - gated * (inv_scale * inv_scale * inv_scale * sums[1] / INNER)[:, None]
    (grad_x, grad_bc, grad_dt, grad_gate, g_conv_x, g_bias_x, g_conv_bc, g_bias_bc, g_dt_bias, g_a_log, g_skip) = mixer_back(grad_gated)
    low_a = jnp.concatenate([grad_x, grad_bc, grad_dt, jnp.zeros((grad_dt.shape[0], 128 - heads), F32)], axis=1).astype(BF)
    low_gate = grad_gate.astype(BF)
    grad_normed = (dot_nt(low_gate, w_gate) + dot_nt(low_a, wa)).astype(BF)
    term_a = dot_tn(normed_all, low_a).astype(BF)
    term_b = jnp.concatenate([dot_tn(normed_all, low_gate), term_out], axis=1).astype(BF)
    small = jnp.concatenate(
        [g_conv_x.reshape(-1), g_bias_x, grad_gain_dev, g_conv_bc.reshape(-1), g_bias_bc]
        + [jnp.pad(v, (0, 128 - heads)) for v in (g_dt_bias, g_a_log, g_skip)]
    )
    n_small = small.shape[0]
    small = jnp.pad(small, (0, 8192 - n_small)).reshape(64, 128)
    blocks = (4, 4, 2, rows)
    ra, rb, own_out, grad_own, smalls = reduce_all(
        term_a.reshape(blocks + term_a.shape[1:]), term_b.reshape(blocks + term_b.shape[1:]),
        partial_out.reshape(4, 256, -1), grad_normed.reshape(4, 256, -1), small,
    )
    output = (hidden + own_out).astype(BF)
    scaled = grad_own * pre_gain[None, :]
    proj = jnp.mean(scaled * hidden, axis=1)
    grad_hidden = cotangent.astype(F32) + scaled * inv_rms[:, None] - hidden * (inv_rms * inv_rms * inv_rms * proj)[:, None]
    part_pre = jnp.sum(grad_own * hidden * inv_rms[:, None], axis=0)
    d_pre = lax.psum(part_pre, ("dp", "tensor"))
    smalls = smalls.reshape(4, 8192)
    d_bc = lax.psum(ra[:, inner : inner + 256], "tensor")
    spread = lambda lo, n, k: smalls[:, lo : lo + n * k].reshape(4, k, n).transpose(1, 0, 2).reshape(k, 4 * n)
    d_conv_x = spread(0, inner, 4)
    at = 4 * inner
    d_bias_x = spread(at, inner, 1)[0]
    d_gain = spread(at + inner, inner, 1)[0]
    at = at + 2 * inner
    bc_sums = jnp.sum(smalls[:, at : at + 5 * 256], axis=0)
    at = at + 5 * 256
    d_dt_bias, d_a_log, d_skip = (spread(at + 128 * i, heads, 1)[0] for i in range(3))
    return (
        output, grad_hidden, d_pre, rb[:, :inner], ra[:, :inner], d_bc, ra[:, inner + 256 : inner + 256 + heads],
        d_conv_x, d_bias_x, bc_sums[:1024].reshape(4, 256), bc_sums[1024:], d_dt_bias, d_a_log, d_skip, d_gain,
        rb[:, inner:].T,
    )


def solution(mesh):
    tok = P(("dp", "tensor"), None)
    mat = P("dp", "tensor")
    in_specs = (tok, P("dp"), P(), mat, mat, P("dp", None), mat) + (P(),) * 8 + (P("tensor", "dp"), tok)
    out_specs = (tok, tok, P(), mat, mat, P("dp", None), mat) + (P(),) * 8 + (P("tensor", "dp"),)
    return jax.shard_map(per_device, mesh=mesh, in_specs=in_specs, out_specs=out_specs, check_vma=False)
```

time: 2160 us -> 752 us (0.35)
  waiting for transfers between devices: 1320 us -> 0 us
  blocking collectives: 235 us -> 85.7 us
  Pallas kernels: 0 us -> 125 us
  local copies, waits for them, and re-layouts: 293 us -> 257 us
    reduce_scatter x5 -> x0, waiting for transfers between devices: 818 us -> none  [the longest x1 234 us: per_device(): lax.psum_scatter(term_gate, 'dp', scatter_dimension=0, tiled=True)]
    unnamed x15 -> x0, waiting for transfers between devices: 349 us -> none
    all_gather x2 -> x0, blocking collectives: 168 us -> none  [the longest x1 84.3 us: per_device(): lax.all_gather(proj_dt, 'dp', axis=0, tiled=True)]
    psum x1 -> x0, waiting for transfers between devices: 150 us -> none  [per_device(): lax.psum((grad_pre_gain, spread_out(grad_conv_x, conv_x, tensor_at), spre...]
    pallas_call x0 -> x2, Pallas kernels: none -> 125 us  [the longest x1 62.7 us: gather(): pl.pallas_call(functools.partial(ag_kernel, ten), out_shape=outs, in_spec...]
    unnamed x178 -> x156, local copies, waits for them, and re-layouts: 39.9 us -> 17.2 us
    dot_general x14 -> x9, matrix products: 69.7 us -> 57.8 us  [the longest x3 18.1 us: dot_tn(): lax.dot_general(left, right, (((0,), (0,)), ((), ())), preferred_element_...]
    dynamic_update_slice x24 -> x16, local copies, waits for them, and re-layouts: 155 us -> 149 us  [scan_ssd(): lax.scan(scan_body, initial, (x_heads.reshape(blocks, GROUP, head_count,...]
  transfers between devices with their start and end apart: 13 -> 0, of which waited for: 8 -> 0; matrix products, arithmetic and copies ran while one was open for 13% -> 0% of each run, Pallas kernels for 0% -> 0%
where the time goes in v1:
time: 752 us; the launch traced here: 743 us
  local copies, waits for them, and re-layouts  257 us (34%)
  matrix products  160 us (21%)
  Pallas kernels  125 us (17%)
  other arithmetic  100 us (13%)
  blocking collectives  85.7 us (11%)
  loops' own time  12.9 us (2%)
    dynamic_update_slice x16, local copies, waits for them, and re-layouts, scan_ssd(): lax.scan(scan_body, initial, (x_heads.reshape(blocks, GROUP, head_count,...  149 us
    psum x1, blocking collectives, per_device(): d_pre = lax.psum(part_pre, ('dp', 'tensor'))  64.2 us
    pallas_call x1, Pallas kernels, gather(): pl.pallas_call(functools.partial(ag_kernel, ten), out_shape=outs, in_spec...  62.7 us
    pallas_call x1, Pallas kernels, reduce_all(): pl.pallas_call(rs_kernel, out_shape=outs, in_specs=[anys] * 4 + [vm], out...  62.1 us
    dot_general x12, matrix products, block_step(): jnp.einsum('hts,shp->thp', mixing, x_block, precision=lax.Precision.HIGHEST)  58 us
    dot_general x3, matrix products, dot_tn(): lax.dot_general(left, right, (((0,), (0,)), ((), ())), preferred_element_...  18.1 us
    another operation x46, other arithmetic  17.9 us
    unnamed x156, local copies, waits for them, and re-layouts  17.2 us

profile of v1, /device:TPU:1, one launch (start us, length us, event | category | flops | bytes accessed | tf_op | source)
XLA Modules:
  0.0 742.6 jit_solution(5771191838102340381)
XLA Ops:
  8.9 62.7 %gather_all.1 = (bf16[4,4,2,48,1152]{4,3,2,1,0:T(8,128)(2,1)}, bf16[4,4,2,48,1536]{4,3,2,1,0:T(8,128)(2,1)}, bf16[4,256,1536]{2,1,0:T(8,128)(2,1)}, bf16[4,256,1536]{2,1,0:T(8,128)(2,1)}) custom-call(bf16[48,1152]{1,0:T(8,128)(2,1)} %concatenate.21.wa, bf16[48,1536]{1,0:T(8,128)(2,1)} %pad_maximum_fusion.1.wb, bf16[256,1536]{1,0:T(8,128)(2,1)} %fusion.108.h, ...), custom_call_target="tpu_custom_call" | custom-call | tf_op jit(solution)/shard_map/gather_all/pallas_call | solution.py:131
  71.6 7.2 fusion.148
  83.2 4.4 fusion.98
  87.6 2.4 copy.167
  90.0 3.0 reshape.543
  93.1 4.3 copy.169
  102.7 2.3 broadcast.298.clone2
  105.1 131.8 %while.42 = (s32[]{:T(128)}, f32[12,64,128]{2,1,0:T(8,128)S(1)}, f32[4,256,12,64]{1,0,3,2:T(4,128)}, f32[4,12,64,128]{3,2,1,0:T(8,128)}, f32[4,256,12]{1,2,0:T(8...) while((s32[]{:T(128)}, f32[12,64,128]{2,1,0:T(8,128)S(1)}, ...), condition=%wide.region_4.5_spmd.clone, body=%wide.region_1.4_spmd.clone.sunk | while | flops 1314242560 | bytes 10601195 | solution.py:344
  106.6 5.0 fusion.221
  116.0 17.8 %dynamic_update_slice.69 = f32[4,256,12,64]{1,0,3,2:T(4,128)} dynamic-update-slice(f32[4,256,12,64]{1,0,3,2:T(4,128)} %get-tuple-element.1243, f32[1,256,12,64]{1,0,3,2:T(1,128)S(1)} %copy.266, s32[]{:T(128)} %get-tuple-element.1241, s32[]{:T(128)} %constant.144.clone.1..sunk, s32[]{:T(128)} %constant.144.clone.1..sunk, s32[]{:T(128)} %constant.144.clone.1..sunk) | dynamic-update-slice | bytes 1572868 | tf_op jit(solution)/shard_map/jvp()/while/body/jit(dynamic_update_index_in_dim)/dynamic_update_slice | solution.py:344
  139.6 5.0 fusion.221
  148.9 17.8 %dynamic_update_slice.69 = f32[4,256,12,64]{1,0,3,2:T(4,128)} dynamic-update-slice(f32[4,256,12,64]{1,0,3,2:T(4,128)} %get-tuple-element.1243, f32[1,256,12,64]{1,0,3,2:T(1,128)S(1)} %copy.266, s32[]{:T(128)} %get-tuple-element.1241, s32[]{:T(128)} %constant.144.clone.1..sunk, s32[]{:T(128)} %constant.144.clone.1..sunk, s32[]{:T(128)} %constant.144.clone.1..sunk) | dynamic-update-slice | bytes 1572868 | tf_op jit(solution)/shard_map/jvp()/while/body/jit(dynamic_update_index_in_dim)/dynamic_update_slice | solution.py:344
  172.5 5.0 fusion.221
  181.9 17.8 %dynamic_update_slice.69 = f32[4,256,12,64]{1,0,3,2:T(4,128)} dynamic-update-slice(f32[4,256,12,64]{1,0,3,2:T(4,128)} %get-tuple-element.1243, f32[1,256,12,64]{1,0,3,2:T(1,128)S(1)} %copy.266, s32[]{:T(128)} %get-tuple-element.1241, s32[]{:T(128)} %constant.144.clone.1..sunk, s32[]{:T(128)} %constant.144.clone.1..sunk, s32[]{:T(128)} %constant.144.clone.1..sunk) | dynamic-update-slice | bytes 1572868 | tf_op jit(solution)/shard_map/jvp()/while/body/jit(dynamic_update_index_in_dim)/dynamic_update_slice | solution.py:344
  205.5 5.0 fusion.221
  214.9 17.8 %dynamic_update_slice.69 = f32[4,256,12,64]{1,0,3,2:T(4,128)} dynamic-update-slice(f32[4,256,12,64]{1,0,3,2:T(4,128)} %get-tuple-element.1243, f32[1,256,12,64]{1,0,3,2:T(1,128)S(1)} %copy.266, s32[]{:T(128)} %get-tuple-element.1241, s32[]{:T(128)} %constant.144.clone.1..sunk, s32[]{:T(128)} %constant.144.clone.1..sunk, s32[]{:T(128)} %constant.144.clone.1..sunk) | dynamic-update-slice | bytes 1572868 | tf_op jit(solution)/shard_map/jvp()/while/body/jit(dynamic_update_index_in_dim)/dynamic_update_slice | solution.py:344
  237.9 2.6 copy.241
  240.5 2.7 copy.171
  243.3 7.0 fusion.101
  251.3 10.6 %multiply_reduce_fusion.11 = (f32[1024]{0:T(1024)S(1)}, f32[1024]{0:T(1024)S(1)}, f32[1024,768]{1,0:T(8,128)}, f32[1024,768]{1,0:T(8,128)}) fusion(f32[768]{0:T(1024)S(1)} %dynamic_slice.134, f32[1024,768]{1,0:T(8,128)} %fusion.101, f32[1024,768]{1,0:T(8,128)} %copy.171, f32[1024,768]{1,0:T(8,128)S(1)} %copy-done.2, f32[768]{0:T(1024)S(1)} %mul.1003, ...), kind=kOutput, calls=%fused_computation.170 | convolution fusion | flops 2428499968 | bytes 21248000 | tf_op jit(solution)/shard_map/dot_general | solution.py:411
  261.9 7.9 %psum.21 = f32[2,1024]{1,0:T(2,128)S(1)} all-reduce(f32[2,1024]{1,0:T(2,128)S(1)} %pad_maximum_fusion.2), channel_id=1, replica_groups=mesh['dp'=32,'tensor'=4] {'tensor'}, use_global_device_ids=true, to_apply=%region_7.8 | all-reduce | flops 2048 | bytes 16384 | tf_op jit(solution)/shard_map/psum | solution.py:413
  269.9 8.3 %multiply_reduce_fusion.4 = (f32[768]{0:T(1024)}, f32[1024,768]{1,0:T(8,128)}, bf16[1024,768]{1,0:T(8,128)(2,1)}, f32[768]{0:T(1024)}) fusion(f32[1024,768]{1,0:T(8,128)S(1)} %copy-done.2, f32[1024,768]{1,0:T(8,128)} %fusion.101, f32[1024,768]{1,0:T(8,128)} %get-tuple-element.942, f32[1024]{0:T(1024)S(1)} %fusion.126, f32[1024]{0:T(1024)S(1)} %bitcast.419, ...), kind=kLoop, calls=%fused_computation.161 | loop fusion | flops 22018560 | bytes 20467712 | tf_op jit(solution)/shard_map/transpose(jvp())/reduce_sum | solution.py:371
  278.2 2.4 copy.172
  280.6 3.0 reshape.547
  283.7 2.3 broadcast.298.clone
  288.3 229.8 %while.43 = (s32[]{:T(128)}, f32[12]{0:T(128)}, f32[12,64,128]{2,1,0:T(8,128)S(1)}, f32[4,256,12,64]{1,0,3,2:T(4,128)}, f32[4,256,12]{1,2,0:T(8,128)}, /*index=5...) while((s32[]{:T(128)}, f32[12]{0:T(128)}, ...), condition=%wide.region_21.22_spmd.clone, body=%wide.region_8.21_spmd.clone.sunk | while | flops 3038949376 | bytes 27467704 | solution.py:344
  288.5 2.7 constant_dynamic-slice_fusion.7
  306.0 5.6 fusion.243
  317.5 2.5 reduce-window.74
  321.7 3.9 fusion.247
  326.5 17.9 %dynamic_update_slice.73 = f32[4,256,12,64]{1,0,3,2:T(4,128)} dynamic-update-slice(f32[4,256,12,64]{1,0,3,2:T(4,128)} %get-tuple-element.1294, f32[1,256,12,64]{1,0,3,2:T(1,128)S(1)} %copy.276, s32[]{:T(128)S(6)} %sub.304, s32[]{:T(128)} %constant.144.clone.1..sunk.1, s32[]{:T(128)} %constant.144.clone.1..sunk.1, s32[]{:T(128)} %constant.144.clone.1..sunk.1) | dynamic-update-slice | bytes 1572868 | tf_op jit(solution)/shard_map/transpose(jvp())/while/body/jit(dynamic_update_index_in_dim)/dynamic_update_slice | solution.py:344
  345.8 2.7 constant_dynamic-slice_fusion.7
  363.3 5.6 fusion.243
  374.8 2.5 reduce-window.74
  379.0 3.9 fusion.247
  383.8 17.9 %dynamic_update_slice.73 = f32[4,256,12,64]{1,0,3,2:T(4,128)} dynamic-update-slice(f32[4,256,12,64]{1,0,3,2:T(4,128)} %get-tuple-element.1294, f32[1,256,12,64]{1,0,3,2:T(1,128)S(1)} %copy.276, s32[]{:T(128)S(6)} %sub.304, s32[]{:T(128)} %constant.144.clone.1..sunk.1, s32[]{:T(128)} %constant.144.clone.1..sunk.1, s32[]{:T(128)} %constant.144.clone.1..sunk.1) | dynamic-update-slice | bytes 1572868 | tf_op jit(solution)/shard_map/transpose(jvp())/while/body/jit(dynamic_update_index_in_dim)/dynamic_update_slice | solution.py:344
  403.1 2.7 constant_dynamic-slice_fusion.7
  420.6 5.6 fusion.243
  432.1 2.5 reduce-window.74
  436.3 3.9 fusion.247
  441.0 17.9 %dynamic_update_slice.73 = f32[4,256,12,64]{1,0,3,2:T(4,128)} dynamic-update-slice(f32[4,256,12,64]{1,0,3,2:T(4,128)} %get-tuple-element.1294, f32[1,256,12,64]{1,0,3,2:T(1,128)S(1)} %copy.276, s32[]{:T(128)S(6)} %sub.304, s32[]{:T(128)} %constant.144.clone.1..sunk.1, s32[]{:T(128)} %constant.144.clone.1..sunk.1, s32[]{:T(128)} %constant.144.clone.1..sunk.1) | dynamic-update-slice | bytes 1572868 | tf_op jit(solution)/shard_map/transpose(jvp())/while/body/jit(dynamic_update_index_in_dim)/dynamic_update_slice | solution.py:344
  460.4 2.7 constant_dynamic-slice_fusion.7
  477.9 5.6 fusion.243
  489.4 2.5 reduce-window.74
  493.6 3.9 fusion.247
  498.3 17.9 %dynamic_update_slice.73 = f32[4,256,12,64]{1,0,3,2:T(4,128)} dynamic-update-slice(f32[4,256,12,64]{1,0,3,2:T(4,128)} %get-tuple-element.1294, f32[1,256,12,64]{1,0,3,2:T(1,128)S(1)} %copy.276, s32[]{:T(128)S(6)} %sub.304, s32[]{:T(128)} %constant.144.clone.1..sunk.1, s32[]{:T(128)} %constant.144.clone.1..sunk.1, s32[]{:T(128)} %constant.144.clone.1..sunk.1) | dynamic-update-slice | bytes 1572868 | tf_op jit(solution)/shard_map/transpose(jvp())/while/body/jit(dynamic_update_index_in_dim)/dynamic_update_slice | solution.py:344
  518.1 4.4 multiply_reduce_fusion.14
  522.5 2.4 copy.242
  524.9 3.8 copy.177
  528.9 7.6 %multiply_reduce_fusion.8 = (f32[768]{0:T(1024)S(1)}, f32[768]{0:T(1024)S(1)}, f32[768]{0:T(1024)S(1)}, f32[768]{0:T(1024)S(1)}, f32[768]{0:T(1024)S(1)}, /*index=5*/f32[1024,768]{1,0:T(8,128)}) fusion(f32[1024,768]{1,0:T(8,128)S(1)} %copy-done.1, f32[1024]{0:T(1024)S(1)} %copy-done.32, f32[1024]{0:T(1024)S(1)} %copy-done.34, f32[1024]{0:T(1024)S(1)} %copy-done.30, ...), kind=kLoop, calls=%fused_computation.165 | loop fusion | flops 18084096 | bytes 18905088 | tf_op jit(solution)/shard_map/transpose(jvp())/reduce_sum | solution.py:300
  545.1 3.0 concatenate.24
  548.2 4.9 fusion.99
  553.2 5.8 add_convert_fusion
  559.0 4.3 convolution_convert_fusion.1
  563.3 3.0 copy.180
  566.3 7.2 convolution_convert_fusion.2
  573.5 2.9 copy.179
  576.4 5.1 convolution_convert_fusion.3
  581.5 2.7 pad_maximum_fusion.gb
  584.2 5.8 convolution_convert_fusion
  590.0 62.1 %reduce_all.1 = (f32[48,1152]{1,0:T(8,128)}, f32[48,1536]{1,0:T(8,128)}, f32[256,1536]{1,0:T(8,128)}, f32[256,1536]{1,0:T(8,128)}, f32[4,64,128]{2,1,0:T(8,128)}) custom-call(bf16[4,4,2,48,1152]{4,3,2,1,0:T(8,128)(2,1)} %bitcast.384, bf16[4,4,2,48,1536]{4,3,2,1,0:T(8,128)(2,1)} %pad_maximum_fusion.gb, bf16[4,256,1536]{2,1,0:T(8,128)(2,1)} %bitcast.386, ...), custom_call_target="tpu_custom_call" | custom-call | tf_op jit(solution)/shard_map/reduce_all/pallas_call | solution.py:283
  654.2 3.4 fusion.111
  663.9 13.6 %psum.23 = f32[48,256]{1,0:T(8,128)} all-reduce(f32[48,256]{1,0:T(8,128)S(1)} %slice.252), channel_id=1, replica_groups=mesh['dp'=32,'tensor'=4] {'tensor'}, use_global_device_ids=true, to_apply=%region_39.40 | all-reduce | flops 12288 | bytes 98304 | tf_op jit(solution)/shard_map/psum | solution.py:444
  678.2 64.2 %psum.22 = f32[1536]{0:T(1024)} all-reduce(f32[1536]{0:T(1024)S(1)} %get-tuple-element.871), channel_id=1, replica_groups=mesh['dp'=32,'tensor'=4] {'dp','tensor'}, use_global_device_ids=true, to_apply=%region_38.39 | all-reduce | flops 1536 | bytes 12288 | tf_op jit(solution)/shard_map/psum | solution.py:442
  (662 shorter events, 166.9 us)
Async XLA Ops:
  83.2 15.6 %copy-start.29 = (f32[1024]{0:T(1024)}, f32[1024]{0:T(1024)S(1)}, u32[]{:S(2)}) copy-start(f32[1024]{0:T(1024)S(1)} %get-tuple-element.992) | copy-start | bytes 12292
  83.2 15.6 %copy-start.31 = (f32[1024]{0:T(1024)}, f32[1024]{0:T(1024)S(1)}, u32[]{:S(2)}) copy-start(f32[1024]{0:T(1024)S(1)} %get-tuple-element.993) | copy-start | bytes 12292
  83.2 15.6 %copy-start.33 = (f32[1024]{0:T(1024)}, f32[1024]{0:T(1024)S(1)}, u32[]{:S(2)}) copy-start(f32[1024]{0:T(1024)S(1)} %get-tuple-element.994) | copy-start | bytes 12292
  243.2 7.0 copy-start.82
  243.3 8.0 %copy-start.2 = (f32[1024,768]{1,0:T(8,128)S(1)}, f32[1024,768]{1,0:T(8,128)}, u32[]{:S(2)}) copy-start(f32[1024,768]{1,0:T(8,128)} %get-tuple-element.946) | copy-start | bytes 9437188
  250.5 19.4 %copy-start.52 = (f32[768]{0:T(1024)}, f32[768]{0:T(1024)S(1)}, u32[]{:S(2)}) copy-start(f32[768]{0:T(1024)S(1)} %mul.1003) | copy-start | bytes 9220
  251.3 18.6 %copy-start.61 = (f32[768]{0:T(1024)}, f32[768]{0:T(1024)S(1)}, u32[]{:S(2)}) copy-start(f32[768]{0:T(1024)S(1)} %dynamic_slice.134) | copy-start | bytes 9220
  269.9 8.3 %copy-start.50 = (f32[1,1024]{1,0:T(1,128)}, f32[1,1024]{1,0:T(1,128)S(1)}, u32[]{:S(2)}) copy-start(f32[1,1024]{1,0:T(1,128)S(1)} %get-tuple-element.986) | copy-start | bytes 12292
  288.5 6.7 copy-start.37
  288.5 10.3 %copy-start.40 = (f32[12]{0:T(128)}, f32[12]{0:T(128)S(1)}, u32[]{:S(2)}) copy-start(f32[12]{0:T(128)S(1)} %get-tuple-element.1206) | copy-start | bytes 148 | tf_op jit(solution)/shard_map/transpose(jvp())/while
  301.3 10.3 %copy-start.27 = (f32[12]{0:T(128)}, f32[12]{0:T(128)S(1)}, u32[]{:S(2)}) copy-start(f32[12]{0:T(128)S(1)} %get-tuple-element.1215) | copy-start | bytes 148 | tf_op jit(solution)/shard_map/transpose(jvp())/while
  303.1 8.5 %copy-start.23 = (f32[256]{0:T(256)}, f32[256]{0:T(256)S(1)}, u32[]{:S(2)}) copy-start(f32[256]{0:T(256)S(1)} %get-tuple-element.1216) | copy-start | bytes 3076 | tf_op jit(solution)/shard_map/transpose(jvp())/while
  306.0 8.9 %copy-start.20 = (f32[256,12]{0,1:T(8,128)S(1)}, f32[256,12]{0,1:T(8,128)}, u32[]{:S(2)}) copy-start(f32[256,12]{0,1:T(8,128)} %get-tuple-element.1223) | copy-start | bytes 36868 | tf_op jit(solution)/shard_map/transpose(jvp())/while
  325.6 18.7 %copy-start.28 = (f32[12]{0:T(128)S(1)}, f32[12]{0:T(128)}, u32[]{:S(2)}) copy-start(f32[12]{0:T(128)} %copy-done.27) | copy-start | bytes 148 | tf_op jit(solution)/shard_map/transpose(jvp())/while
  325.6 19.6 %copy-start.54 = (f32[12]{0:T(128)S(1)}, f32[12]{0:T(128)}, u32[]{:S(2)}) copy-start(f32[12]{0:T(128)} %get-tuple-element.1292) | copy-start | bytes 148 | tf_op jit(solution)/shard_map/transpose(jvp())/while
  325.6 20.2 %copy-start.38 = (s32[4,256]{1,0:T(4,128)S(1)}, s32[4,256]{1,0:T(4,128)}, u32[]{:S(2)}) copy-start(s32[4,256]{1,0:T(4,128)} %copy-done.37) | copy-start | bytes 12292 | tf_op jit(solution)/shard_map/transpose(jvp())/while
  325.6 20.2 %copy-start.41 = (f32[12]{0:T(128)S(1)}, f32[12]{0:T(128)}, u32[]{:S(2)}) copy-start(f32[12]{0:T(128)} %copy-done.40) | copy-start | bytes 148 | tf_op jit(solution)/shard_map/transpose(jvp())/while
  325.6 20.1 %copy-start.84 = (s32[4]{0:T(128)S(1)}, s32[4]{0:T(128)}, u32[]{:S(2)}) copy-start(s32[4]{0:T(128)} %copy-done.83) | copy-start | bytes 52 | tf_op jit(solution)/shard_map/transpose(jvp())/while
  345.8 10.3 %copy-start.40 = (f32[12]{0:T(128)}, f32[12]{0:T(128)S(1)}, u32[]{:S(2)}) copy-start(f32[12]{0:T(128)S(1)} %get-tuple-element.1206) | copy-start | bytes 148 | tf_op jit(solution)/shard_map/transpose(jvp())/while
  358.6 10.3 %copy-start.27 = (f32[12]{0:T(128)}, f32[12]{0:T(128)S(1)}, u32[]{:S(2)}) copy-start(f32[12]{0:T(128)S(1)} %get-tuple-element.1215) | copy-start | bytes 148 | tf_op jit(solution)/shard_map/transpose(jvp())/while
  360.4 8.5 %copy-start.23 = (f32[256]{0:T(256)}, f32[256]{0:T(256)S(1)}, u32[]{:S(2)}) copy-start(f32[256]{0:T(256)S(1)} %get-tuple-element.1216) | copy-start | bytes 3076 | tf_op jit(solution)/shard_map/transpose(jvp())/while
  363.3 8.9 %copy-start.20 = (f32[256,12]{0,1:T(8,128)S(1)}, f32[256,12]{0,1:T(8,128)}, u32[]{:S(2)}) copy-start(f32[256,12]{0,1:T(8,128)} %get-tuple-element.1223) | copy-start | bytes 36868 | tf_op jit(solution)/shard_map/transpose(jvp())/while
  382.9 18.7 %copy-start.28 = (f32[12]{0:T(128)S(1)}, f32[12]{0:T(128)}, u32[]{:S(2)}) copy-start(f32[12]{0:T(128)} %copy-done.27) | copy-start | bytes 148 | tf_op jit(solution)/shard_map/transpose(jvp())/while
  382.9 19.6 %copy-start.54 = (f32[12]{0:T(128)S(1)}, f32[12]{0:T(128)}, u32[]{:S(2)}) copy-start(f32[12]{0:T(128)} %get-tuple-element.1292) | copy-start | bytes 148 | tf_op jit(solution)/shard_map/transpose(jvp())/while
  382.9 20.2 %copy-start.38 = (s32[4,256]{1,0:T(4,128)S(1)}, s32[4,256]{1,0:T(4,128)}, u32[]{:S(2)}) copy-start(s32[4,256]{1,0:T(4,128)} %copy-done.37) | copy-start | bytes 12292 | tf_op jit(solution)/shard_map/transpose(jvp())/while
  382.9 20.1 %copy-start.41 = (f32[12]{0:T(128)S(1)}, f32[12]{0:T(128)}, u32[]{:S(2)}) copy-start(f32[12]{0:T(128)} %copy-done.40) | copy-start | bytes 148 | tf_op jit(solution)/shard_map/transpose(jvp())/while
  382.9 20.1 %copy-start.84 = (s32[4]{0:T(128)S(1)}, s32[4]{0:T(128)}, u32[]{:S(2)}) copy-start(s32[4]{0:T(128)} %copy-done.83) | copy-start | bytes 52 | tf_op jit(solution)/shard_map/transpose(jvp())/while
  403.1 6.7 copy-start.83
  403.1 10.3 %copy-start.40 = (f32[12]{0:T(128)}, f32[12]{0:T(128)S(1)}, u32[]{:S(2)}) copy-start(f32[12]{0:T(128)S(1)} %get-tuple-element.1206) | copy-start | bytes 148 | tf_op jit(solution)/shard_map/transpose(jvp())/while
  415.9 10.3 %copy-start.27 = (f32[12]{0:T(128)}, f32[12]{0:T(128)S(1)}, u32[]{:S(2)}) copy-start(f32[12]{0:T(128)S(1)} %get-tuple-element.1215) | copy-start | bytes 148 | tf_op jit(solution)/shard_map/transpose(jvp())/while
  417.7 8.5 %copy-start.23 = (f32[256]{0:T(256)}, f32[256]{0:T(256)S(1)}, u32[]{:S(2)}) copy-start(f32[256]{0:T(256)S(1)} %get-tuple-element.1216) | copy-start | bytes 3076 | tf_op jit(solution)/shard_map/transpose(jvp())/while
  420.6 8.9 %copy-start.20 = (f32[256,12]{0,1:T(8,128)S(1)}, f32[256,12]{0,1:T(8,128)}, u32[]{:S(2)}) copy-start(f32[256,12]{0,1:T(8,128)} %get-tuple-element.1223) | copy-start | bytes 36868 | tf_op jit(solution)/shard_map/transpose(jvp())/while
  440.2 18.7 %copy-start.28 = (f32[12]{0:T(128)S(1)}, f32[12]{0:T(128)}, u32[]{:S(2)}) copy-start(f32[12]{0:T(128)} %copy-done.27) | copy-start | bytes 148 | tf_op jit(solution)/shard_map/transpose(jvp())/while
  440.2 19.6 %copy-start.54 = (f32[12]{0:T(128)S(1)}, f32[12]{0:T(128)}, u32[]{:S(2)}) copy-start(f32[12]{0:T(128)} %get-tuple-element.1292) | copy-start | bytes 148 | tf_op jit(solution)/shard_map/transpose(jvp())/while
  440.2 20.2 %copy-start.38 = (s32[4,256]{1,0:T(4,128)S(1)}, s32[4,256]{1,0:T(4,128)}, u32[]{:S(2)}) copy-start(s32[4,256]{1,0:T(4,128)} %copy-done.37) | copy-start | bytes 12292 | tf_op jit(solution)/shard_map/transpose(jvp())/while
  440.2 20.2 %copy-start.41 = (f32[12]{0:T(128)S(1)}, f32[12]{0:T(128)}, u32[]{:S(2)}) copy-start(f32[12]{0:T(128)} %copy-done.40) | copy-start | bytes 148 | tf_op jit(solution)/shard_map/transpose(jvp())/while
  440.2 20.1 %copy-start.84 = (s32[4]{0:T(128)S(1)}, s32[4]{0:T(128)}, u32[]{:S(2)}) copy-start(s32[4]{0:T(128)} %copy-done.83) | copy-start | bytes 52 | tf_op jit(solution)/shard_map/transpose(jvp())/while
  460.4 6.7 copy-start.83
  460.4 10.3 %copy-start.40 = (f32[12]{0:T(128)}, f32[12]{0:T(128)S(1)}, u32[]{:S(2)}) copy-start(f32[12]{0:T(128)S(1)} %get-tuple-element.1206) | copy-start | bytes 148 | tf_op jit(solution)/shard_map/transpose(jvp())/while
  473.2 10.3 %copy-start.27 = (f32[12]{0:T(128)}, f32[12]{0:T(128)S(1)}, u32[]{:S(2)}) copy-start(f32[12]{0:T(128)S(1)} %get-tuple-element.1215) | copy-start | bytes 148 | tf_op jit(solution)/shard_map/transpose(jvp())/while
  475.0 8.5 %copy-start.23 = (f32[256]{0:T(256)}, f32[256]{0:T(256)S(1)}, u32[]{:S(2)}) copy-start(f32[256]{0:T(256)S(1)} %get-tuple-element.1216) | copy-start | bytes 3076 | tf_op jit(solution)/shard_map/transpose(jvp())/while
  477.9 8.9 %copy-start.20 = (f32[256,12]{0,1:T(8,128)S(1)}, f32[256,12]{0,1:T(8,128)}, u32[]{:S(2)}) copy-start(f32[256,12]{0,1:T(8,128)} %get-tuple-element.1223) | copy-start | bytes 36868 | tf_op jit(solution)/shard_map/transpose(jvp())/while
  497.5 18.7 %copy-start.28 = (f32[12]{0:T(128)S(1)}, f32[12]{0:T(128)}, u32[]{:S(2)}) copy-start(f32[12]{0:T(128)} %copy-done.27) | copy-start | bytes 148 | tf_op jit(solution)/shard_map/transpose(jvp())/while
  497.5 19.6 %copy-start.54 = (f32[12]{0:T(128)S(1)}, f32[12]{0:T(128)}, u32[]{:S(2)}) copy-start(f32[12]{0:T(128)} %get-tuple-element.1292) | copy-start | bytes 148 | tf_op jit(solution)/shard_map/transpose(jvp())/while
  497.5 20.2 %copy-start.38 = (s32[4,256]{1,0:T(4,128)S(1)}, s32[4,256]{1,0:T(4,128)}, u32[]{:S(2)}) copy-start(s32[4,256]{1,0:T(4,128)} %copy-done.37) | copy-start | bytes 12292 | tf_op jit(solution)/shard_map/transpose(jvp())/while
  497.5 20.2 %copy-start.41 = (f32[12]{0:T(128)S(1)}, f32[12]{0:T(128)}, u32[]{:S(2)}) copy-start(f32[12]{0:T(128)} %copy-done.40) | copy-start | bytes 148 | tf_op jit(solution)/shard_map/transpose(jvp())/while
  497.5 20.1 %copy-start.84 = (s32[4]{0:T(128)S(1)}, s32[4]{0:T(128)}, u32[]{:S(2)}) copy-start(s32[4]{0:T(128)} %copy-done.83) | copy-start | bytes 52 | tf_op jit(solution)/shard_map/transpose(jvp())/while
  528.7 7.8 %copy-start.63 = (f32[768]{0:T(1024)S(1)}, f32[768]{0:T(1024)}, u32[]{:S(2)}) copy-start(f32[768]{0:T(1024)} %get-tuple-element.966) | copy-start | bytes 9220
  528.8 7.8 %copy-start.25 = (f32[4,256,12]{1,2,0:T(8,128)S(1)}, f32[4,256,12]{1,2,0:T(8,128)}, u32[]{:S(2)}) copy-start(f32[4,256,12]{1,2,0:T(8,128)} %get-tuple-element.496) | copy-start | bytes 147460
  528.8 8.0 %copy-start.76 = (f32[12]{0:T(128)S(1)}, f32[12]{0:T(128)}, u32[]{:S(2)}) copy-start(f32[12]{0:T(128)} %copy-done.75) | copy-start | bytes 148
  528.8 9.6 %copy-start.56 = (f32[12]{0:T(128)S(1)}, f32[12]{0:T(128)}, u32[]{:S(2)}) copy-start(f32[12]{0:T(128)} %get-tuple-element.497) | copy-start | bytes 148
  528.8 9.6 %copy-start.79 = (f32[48]{0:T(128)S(1)}, f32[48]{0:T(128)}, u32[]{:S(2)}) copy-start(f32[48]{0:T(128)} %param.33) | copy-start | bytes 580
  528.8 9.7 %copy-start.60 = (f32[768]{0:T(1024)S(1)}, f32[768]{0:T(1024)}, u32[]{:S(2)}) copy-start(f32[768]{0:T(1024)} %get-tuple-element.936) | copy-start | bytes 9220
  528.8 10.5 %copy-start.65 = (f32[1,256]{1,0:T(1,128)S(1)}, f32[1,256]{1,0:T(1,128)}, u32[]{:S(2)}) copy-start(f32[1,256]{1,0:T(1,128)} %copy-done.64) | copy-start | bytes 3076
  528.8 10.5 %copy-start.67 = (f32[1,256]{1,0:T(1,128)S(1)}, f32[1,256]{1,0:T(1,128)}, u32[]{:S(2)}) copy-start(f32[1,256]{1,0:T(1,128)} %copy-done.66) | copy-start | bytes 3076
  528.8 10.5 %copy-start.69 = (f32[1,256]{1,0:T(1,128)S(1)}, f32[1,256]{1,0:T(1,128)}, u32[]{:S(2)}) copy-start(f32[1,256]{1,0:T(1,128)} %copy-done.68) | copy-start | bytes 3076
  528.9 10.5 %copy-start.71 = (f32[1,256]{1,0:T(1,128)S(1)}, f32[1,256]{1,0:T(1,128)}, u32[]{:S(2)}) copy-start(f32[1,256]{1,0:T(1,128)} %copy-done.70) | copy-start | bytes 3076
  548.2 10.8 %slice-start = ((s8[4718592]{0:T(1024)(128)(4,1)}), s8[4194304]{0:T(1024)(128)(4,1)S(1)}, s32[]{:S(2)}) async-start(s8[4718592]{0:T(1024)(128)(4,1)} %bitcast.442), calls=%async_computation | async-start | bytes 8388608
  566.3 7.2 copy-start.13
  590.0 62.1 %copy-start.5 = (bf16[256,1536]{1,0:T(8,128)(2,1)S(1)}, bf16[256,1536]{1,0:T(8,128)(2,1)}, u32[]{:S(2)}) copy-start(bf16[256,1536]{1,0:T(8,128)(2,1)} %param.21) | copy-start | bytes 2359300
  590.0 62.1 %copy-start.39 = (f32[1536]{0:T(1024)S(1)}, f32[1536]{0:T(1024)}, u32[]{:S(2)}) copy-start(f32[1536]{0:T(1024)} %param.23) | copy-start | bytes 18436
  590.0 62.1 %copy-start.59 = (f32[256]{0:T(256)S(1)}, f32[256]{0:T(256)}, u32[]{:S(2)}) copy-start(f32[256]{0:T(256)} %copy-done.58) | copy-start | bytes 3076
  590.0 64.1 %copy-start.73 = (f32[256]{0:T(256)S(1)}, f32[256]{0:T(256)}, u32[]{:S(2)}) copy-start(f32[256]{0:T(256)} %copy-done.72) | copy-start | bytes 3076
  590.0 64.1 %copy-start.12 = (bf16[256,1536]{1,0:T(8,128)(2,1)S(1)}, bf16[256,1536]{1,0:T(8,128)(2,1)}, u32[]{:S(2)}) copy-start(bf16[256,1536]{1,0:T(8,128)(2,1)} %c.1) | copy-start | bytes 2359300
  (74 other events, 312.1 us)

commit v2 on v1

--- a/solution.py
+++ b/solution.py
@@ -134,10 +134,10 @@
         compiler_params=pltpu.CompilerParams(collective_id=0, has_side_effects=True, vmem_limit_bytes=60*2**20), name="gather_all")(wa, wb, h, c)
 
 
-def rs_kernel(ga, gb, po, pn, sv, oa, ob, oo, on, osv,
+def rs_kernel(bc0, ga, gb, po, pn, sv, oa, ob, oo, on, osv,
               va, vb, vo, vn, r1a, r1b, r2a, r2b, ha, hb, q1a, q1b, q2a, q2b, ka, kb, ya, yb,
               co_buf, cy_buf, cs_buf, sacc, sx, sz, sy, st, bct,
-              lsem, wsend, wrecv, tsend, trecv, ssend, srecv):
+              lsem, wsend, wrecv, tsend, trecv, ssend, srecv, bsend, brecv):
     x, z, yh, t = place()
     yl = t // 2; co = t % 2
     m4 = lambda v: (v + 8) % 4
@@ -160,8 +160,6 @@
     def rc(src, dst, ss, rs, to):
         cp = pltpu.make_async_remote_copy(src_ref=src, dst_ref=dst, send_sem=ss, recv_sem=rs, device_id=to, device_id_type=MESH)
         cp.start(); sends.append(cp); return cp
-    def acc(dst, idx, terms):
-        pass
     pos = {"x": x, "z": z}
     halves = ((va, "z", "x", r1a, r2a, ha, q1a, q2a, ka, ya, oa), (vb, "x", "z", r1b, r2b, hb, q1b, q2b, kb, yb, ob))
     def b1(v, a1, d, k=None):
@@ -255,10 +253,16 @@
             o[rows] = v[t, rows].astype(F32) + co_buf[i, 1, rows].astype(F32) + cy_buf[i, rows].astype(F32)
             return 0
         lax.fori_loop(0, 8, addf, 0)
+    tens = []
     for i, (v, a1, a2, r1, r2, h, q1, q2, kk, yy, o) in enumerate(halves):
         q = pos[a2]
         s3[i].wait_recv()
         o[...] = h[q, yh].astype(F32) + q2[0, yh].astype(F32) + q2[1, yh].astype(F32) + yy[...].astype(F32)
+        if i == 0:
+            bct[3] = o[:, bc0 : bc0 + 256]
+            tens = [rc(bct.at[3], bct.at[j], bsend.at[j], brecv.at[j], d_) for j, d_ in enumerate((tcore, tyl, tdiag))]
+    for cp in tens: cp.wait_recv()
+    oa[:, bc0 : bc0 + 256] = bct[3] + bct[0] + bct[1] + bct[2]
     for s in small: s.wait_recv()
     osv[t] = sacc[2]
     osv[yl * 2 + 1 - co] = st[0]
@@ -266,7 +270,7 @@
     osv[(1 - yl) * 2 + 1 - co] = st[2]
     for cp in sends: cp.wait_send()
 
-def reduce_all(ga, gb, po, pn, sv):
+def reduce_all(bc0, ga, gb, po, pn, sv):
     anys = pl.BlockSpec(memory_space=pl.ANY); vm = pl.BlockSpec(memory_space=pltpu.VMEM)
     ca, cb = ga.shape[-1], gb.shape[-1]; R = sv.shape[0]
     outs = (jax.ShapeDtypeStruct((48, ca), F32), jax.ShapeDtypeStruct((48, cb), F32), jax.ShapeDtypeStruct((256, 1536), F32),
@@ -278,98 +282,349 @@
                V(4, 2, 48, ca), V(4, 2, 48, cb), V(2, 48, ca), V(2, 48, cb), V(2, 2, 48, ca), V(2, 2, 48, cb),
                V(48, ca), V(48, cb), V(48, ca), V(48, cb),
                V(2, 2, 256, 1536), V(2, 256, 1536), V(2, 256, 1536),
-               V(3, R, 128, d=F32), V(3, R, 128, d=F32), V(3, R, 128, d=F32), V(R, 128, d=F32), V(3, R, 128, d=F32), V(8, 128, d=F32),
-               D((4,)), D((2, 13)), D((2, 13)), D((2, 3)), D((2, 3)), D((10,)), D((10,))]
-    return pl.pallas_call(rs_kernel, out_shape=outs, in_specs=[anys] * 4 + [vm], out_specs=[vm] * 5, scratch_shapes=scratch,
+               V(3, R, 128, d=F32), V(3, R, 128, d=F32), V(3, R, 128, d=F32), V(R, 128, d=F32), V(3, R, 128, d=F32), V(4, 48, 256, d=F32),
+               D((4,)), D((2, 13)), D((2, 13)), D((2, 3)), D((2, 3)), D((10,)), D((10,)), D((3,)), D((3,))]
+    return pl.pallas_call(functools.partial(rs_kernel, bc0), out_shape=outs, in_specs=[anys] * 4 + [vm], out_specs=[vm] * 5, scratch_shapes=scratch,
         compiler_params=pltpu.CompilerParams(collective_id=1, has_side_effects=True, vmem_limit_bytes=60 * 2**20), name="reduce_all")(ga, gb, po, pn, sv)
 
 
-GROUP = 256
+Q = 256
+LOG2E = 1.4426950408889634
+NEG = -1e30
+
+
+def dnn(a, b):
+    return jnp.dot(a, b, preferred_element_type=F32)
+
+
+def dnt(a, b):
+    return lax.dot_general(a, b, (((1,), (1,)), ((), ())), preferred_element_type=F32)
+
+
+def split3(v):
+    hi = v.astype(BF)
+    r = v - hi.astype(F32)
+    mid = r.astype(BF)
+    lo = (r - mid.astype(F32)).astype(BF)
+    return hi, mid, lo
+
+
+def spread3(v, mat):
+    hi, mid, lo = split3(v)
+    return dnn(jnp.concatenate([hi, mid, lo], axis=1), jnp.concatenate([mat, mat, mat], axis=0))
+
+
+def tri_times(mat, v):
+    hi, mid, lo = split3(v)
+    out = dnn(mat, jnp.concatenate([hi, mid, lo], axis=1))
+    w = v.shape[1]
+    return out[:, :w] + out[:, w : 2 * w] + out[:, 2 * w :]
+
+
+def ii(shape, dim):
+    return lax.broadcasted_iota(jnp.int32, shape, dim)
+
+
+def sigmoid(v):
+    return 1.0 / (1.0 + jnp.exp2(v * -LOG2E))
+
+
+def softplus(v):
+    e = jnp.exp2(jnp.abs(v) * -LOG2E)
+    u = 1.0 + e
+    log1p = jnp.where(u == 1.0, e, jnp.log(u) * (e / jnp.where(u == 1.0, 1.0, u - 1.0)))
+    return jnp.maximum(v, 0.0) + log1p
+
+
+def conv_terms(ext, match, taps):
+    n = ext.shape[0] - 8
+    shifted = [ext[8:]] + [jnp.where(match[k], ext[8 - k : 8 + n - k], 0.0) for k in (1, 2, 3)]
+    pre = taps[4:5] + sum(taps[3 - k : 4 - k] * shifted[k] for k in range(4))
+    return pre, shifted
+
+
+def with_earlier(ref, r0, lanes):
+    prev = ref[pl.ds(pl.multiple_of(jnp.maximum(r0 - 8, 0), 8), 8), lanes]
+    return jnp.concatenate([prev, ref[pl.ds(r0, Q), lanes]], axis=0)
+
+
+def match_rows(segc, r0):
+    prev = segc[pl.ds(pl.multiple_of(jnp.maximum(r0 - 8, 0), 8), 8), :]
+    prev = jnp.where(r0 > 0, prev, -1.0)
+    cur = segc[pl.ds(r0, Q), :]
+    ext = jnp.concatenate([prev, cur], axis=0)
+    return [None] + [ext[8 - k : 8 + Q - k] == cur for k in (1, 2, 3)]
+
+
+def block_setup(c, nv, vals, segc, segr, cbc, hp, bt_ref, b_ref, c_ref, ct_ref, qk_ref, bias_ref, cum_ref, cumt_ref, step_ref, tail_ref, keep_ref, ex_ref, keep_out):
+    r0 = pl.multiple_of(c * Q, Q)
+    match = match_rows(segc, r0)
+    m2 = [None] + [jnp.concatenate([m, m], axis=1) for m in match[1:]]
+    ext = with_earlier(vals, r0, pl.ds(nv, 256))
+    pre, shifted = conv_terms(ext, m2, cbc[...])
+    bc = pre * sigmoid(pre)
+    bb = bc[:, :128].astype(BF)
+    cc = bc[:, 128:].astype(BF)
+    b_ref[...] = bb
+    c_ref[...] = cc
+    bt_ref[...] = bc[:, :128].T.astype(BF)
+    if ct_ref is not None:
+        ct_ref[...] = bc[:, 128:].T.astype(BF)
+    qk_ref[...] = dnt(cc, bb)
+    seg = segc[pl.ds(r0, Q), :]
+    segs = segr[0:1, pl.ds(r0, Q)]
+    tt, ss = ii((Q, Q), 0), ii((Q, Q), 1)
+    allowed = (tt >= ss) & (jnp.concatenate([seg, seg], axis=1) == segs)
+    bias_ref[...] = jnp.where(allowed, 0.0, NEG)
+    raw = vals[pl.ds(r0, Q), pl.ds(nv + 256, 128)] + hp[0:1]
+    step = softplus(raw)
+    tri = (tt >= ss).astype(BF)
+    cum = tri_times(tri, step * (hp[1:2] * LOG2E))
+    cumt = cum.T
+    for h in range(nv // 64):
+        cumt_ref[h] = jnp.broadcast_to(cumt[h : h + 1], (8, Q))
+    exm = ex_ref[...]
+    cum_ref[...] = spread3(cum, exm)
+    e64 = (ii((128, nv), 0) == ii((128, nv), 1) // 64).astype(BF)
+    step_ref[...] = spread3(step, e64)
+    prev_seg = jnp.where(c > 0, segc[pl.ds(pl.multiple_of(jnp.maximum(r0 - 8, 0), 8), 8), :][7:8], -1.0)
+    last_seg = seg[Q - 1 :]
+    cum_last = cum[Q - 1 :]
+    carry = (seg == prev_seg).astype(F32)
+    tailm = (seg == last_seg).astype(F32)
+    tail = jnp.exp2(cum_last - cum) * tailm
+    tail_ref[...] = spread3(tail, e64)
+    keep = jnp.exp2(cum_last) * (last_seg == prev_seg).astype(F32)
+    keep_ref[...] = spread3(jnp.broadcast_to(keep, (8, 128)), e64)
+    keep_out[...] = spread3(jnp.exp2(cum) * carry, e64)
+    return match, pre, shifted, raw, step
+
+
+def decay(cum_ref, cumt_ref, bias_ref, h, rows, cols):
+    col = cum_ref[rows, pl.ds(pl.multiple_of(h * 128, 128), 128)]
+    row = cumt_ref[h, 0:1, cols]
+    return jnp.exp2(col - row + bias_ref[rows, cols])
+
+
+def fwd_scratch(nv):
+    V = lambda s, d=F32: pltpu.VMEM(s, d)
+    nh = nv // 64
+    return dict(
+        bt=V((128, Q), BF), b=V((Q, 128), BF), c=V((Q, 128), BF), qk=V((Q, Q)), bias=V((Q, Q)), cum=V((Q, nh * 128)), cumt=V((nh, 8, Q)),
+        step=V((Q, nv)), tail=V((Q, nv)), keep=V((8, nv)), ecum=V((Q, nv)), ex=V((128, nh * 128), BF), state=V((128, nv)), m=V((2, Q, Q), BF),
+    )
+
+
+def ssd_forward(nv, vals, segc, segr, cx, cbc, hp, ssd, states, s):
+    nh = nv // 64
+    s["ex"][...] = (ii((128, nh * 128), 0) == ii((128, nh * 128), 1) // 128).astype(BF)
+    s["state"][...] = jnp.zeros_like(s["state"])
+    s["m"][...] = jnp.zeros_like(s["m"])
+
+    def block(c, _):
+        r0 = pl.multiple_of(c * Q, Q)
+        match, *_r = block_setup(c, nv, vals, segc, segr, cbc, hp, s["bt"], s["b"], s["c"], None, s["qk"], s["bias"], s["cum"], s["cumt"], s["step"], s["tail"], s["keep"], s["ex"], s["ecum"])
+        states[c] = s["state"][...]
+
+        def pair(j, _):
+            lanes = pl.ds(pl.multiple_of(j * 128, 128), 128)
+            pre, _sh = conv_terms(with_earlier(vals, r0, lanes), match, cx[:, lanes])
+            x = pre * sigmoid(pre)
+            u = x * s["step"][:, lanes]
+            ub = u.astype(BF)
+            st = s["state"][:, lanes]
+            y = dnn(s["c"][...], st.astype(BF)) * s["ecum"][:, lanes]
+            y = y + cx[5:6, lanes] * x
+            for e in range(2):
+                for r in range(4):
+                    rows = slice(r * 64, r * 64 + 64)
+                    for k in range(1 if r < 2 else 2):
+                        cols = slice(k * 128, k * 128 + 128)
+                        s["m"][e, rows, cols] = (decay(s["cum"], s["cumt"], s["bias"], 2 * j + e, rows, cols) * s["qk"][rows, cols]).astype(BF)
+            y0 = dnn(s["m"][0], ub)
+            y1 = dnn(s["m"][1], ub)
+            ssd[pl.ds(r0, Q), lanes] = y + jnp.where(ii((Q, 128), 1) < 64, y0, y1)
+            s["state"][:, lanes] = st * s["keep"][0:1, lanes] + dnn(s["bt"][...], (u * s["tail"][:, lanes]).astype(BF))
+            return 0
+
+        lax.fori_loop(0, nv // 128, pair, 0)
+        return 0
+
+    lax.fori_loop(0, vals.shape[0] // Q, block, 0)
+
+
+def bwd_scratch(nv):
+    V = lambda s, d=F32: pltpu.VMEM(s, d)
+    d = fwd_scratch(nv)
+    d.update(ct=V((128, Q), BF), dqk=V((Q, Q)), dstate=V((128, nv)), dcs=V((Q, 128)), dbs=V((Q, 128)), rowg=V((Q, 128)), colg=V((nv // 64, 8, Q)), rs=V((Q, 128)),
+             gs=V((Q, 128)), ds=V((Q, 128)), krow=V((8, nv)), halo=V((8, nv)), halobc=V((8, 256)), dm=V((Q, Q)))
+    return d
+
+
+def to_head(v, j):
+    red = (ii((128, 128), 1) == 2 * j + ii((128, 128), 0) // 64).astype(BF)
+    hi = v.astype(BF)
+    lo = (v - hi.astype(F32)).astype(BF)
+    return dnn(jnp.concatenate([hi, lo], axis=1), jnp.concatenate([red, red], axis=0))
+
+
+def later_sum(dpre, halo, match_ext, taps):
+    ext = jnp.concatenate([dpre, halo], axis=0)
+    n = dpre.shape[0]
+    out = taps[3:4] * dpre
+    for k in (1, 2, 3):
+        out = out + taps[3 - k : 4 - k] * jnp.where(match_ext[k], ext[k : n + k], 0.0)
+    return out
+
+
+def ssd_backward(nv, vals, segc, segr, cx, cbc, hp, dy_ref, states, low, gx, gbc, gh, s):
+    nh = nv // 64
+    nb = vals.shape[0] // Q
+    s["ex"][...] = (ii((128, nh * 128), 0) == ii((128, nh * 128), 1) // 128).astype(BF)
+    for n in ("dstate", "halo", "halobc", "colg", "m"):
+        s[n][...] = jnp.zeros_like(s[n])
+    gx[...] = jnp.zeros_like(gx)
+    gbc[...] = jnp.zeros_like(gbc)
+    gh[...] = jnp.zeros_like(gh)
+
+    def block(i, _):
+        c = nb - 1 - i
+        r0 = pl.multiple_of(c * Q, Q)
+        match, bc_pre, bc_shifted, raw, step = block_setup(c, nv, vals, segc, segr, cbc, hp, s["bt"], s["b"], s["c"], s["ct"], s["qk"], s["bias"], s["cum"], s["cumt"], s["step"], s["tail"], s["keep"], s["ex"], s["ecum"])
+        nxt = segc[pl.ds(pl.multiple_of(jnp.minimum(r0 + Q, segc.shape[0] - 8), 8), 8), :]
+        seg = segc[pl.ds(r0, Q), :]
+        ext = jnp.concatenate([seg, nxt], axis=0)
+        after = [None] + [ext[k : Q + k] == seg for k in (1, 2, 3)]
+        for n in ("dqk", "dcs", "dbs", "rowg", "rs", "gs", "ds"):
+            s[n][...] = jnp.zeros_like(s[n])
+
+        def pair(j, _):
+            lanes = pl.ds(pl.multiple_of(j * 128, 128), 128)
+            taps = cx[:, lanes]
+            pre, shifted = conv_terms(with_earlier(vals, r0, lanes), match, taps)
+            sig = sigmoid(pre)
+            x = pre * sig
+            stepe = s["step"][:, lanes]
+            taile = s["tail"][:, lanes]
+            u = x * stepe
+            ub = u.astype(BF)
+            dy = dy_ref[pl.ds(r0, Q), lanes].astype(F32)
+            dyb = dy.astype(BF)
+            dyt = dy.T.astype(BF)
+            st = states[c, :, lanes]
+            stb = st.astype(BF)
+            dst = s["dstate"][:, lanes]
+            dstb = dst.astype(BF)
+            edy = s["ecum"][:, lanes] * dy
+            edyb = edy.astype(BF)
+            s["rs"][...] += to_head(edy * dnn(s["c"][...], stb), j)
+            s["dcs"][...] += dnt(edyb, stb)
+            tu = taile * u
+            v = dnn(s["b"][...], dstb)
+            s["dbs"][...] += dnt(tu.astype(BF), dstb)
+            s["gs"][...] += to_head(tu * v, j)
+            keep = s["keep"][0:1, lanes]
+            s["krow"][:, lanes] = jnp.broadcast_to(keep * jnp.sum(st * dst, axis=0, keepdims=True), (8, 128))
+            s["dstate"][:, lanes] = keep * dst + dnn(s["ct"][...], edyb)
+            lane = ii((Q, 128), 1)
+            parts = []
+            for e in range(2):
+                h = 2 * j + e
+                mine = (lane < 64) if e == 0 else (lane >= 64)
+                s["dm"][...] = dnt(jnp.where(mine, dy, 0.0).astype(BF), ub)
+                colsum = [jnp.zeros((1, 128), F32), jnp.zeros((1, 128), F32)]
+                for r in range(4):
+                    rows = slice(r * 64, r * 64 + 64)
+                    rowsum = jnp.zeros((64, 128), F32)
+                    for k in range(1 if r < 2 else 2):
+                        cols = slice(k * 128, k * 128 + 128)
+                        dec = decay(s["cum"], s["cumt"], s["bias"], h, rows, cols)
+                        qk = s["qk"][rows, cols]
+                        p = s["dm"][rows, cols] * dec
+                        s["dqk"][rows, cols] += p
+                        g = p * qk
+                        rowsum = rowsum + g
+                        colsum[k] = colsum[k] + jnp.sum(g, axis=0, keepdims=True)
+                        s["m"][e, rows, cols] = (dec * qk).astype(BF)
+                    tot = jnp.sum(rowsum, axis=1, keepdims=True)
+                    s["rowg"][rows] += jnp.where(ii((64, 128), 1) == h, tot, 0.0)
+                s["colg"][h] = jnp.broadcast_to(jnp.concatenate(colsum, axis=1), (8, Q))
+                parts.append(dnn(dyt[e * 64 : e * 64 + 64], s["m"][e]))
+            du = jnp.concatenate(parts, axis=0).T + taile * v
+            s["ds"][...] += to_head(du * x, j)
+            skip = taps[5:6]
+            dx = du * stepe + skip * dy
+            dpre = dx * (sig + x * (1.0 - sig))
+            low[pl.ds(r0, Q), lanes] = later_sum(dpre, s["halo"][:, lanes], after, taps).astype(BF)
+            s["halo"][:, lanes] = dpre[:8]
+            gx[:, lanes] += jnp.concatenate(
+                [jnp.sum(dpre * shifted[3 - k], axis=0, keepdims=True) for k in range(4)]
+                + [jnp.sum(dpre, axis=0, keepdims=True), jnp.sum(dy * x, axis=0, keepdims=True), jnp.zeros((2, 128), F32)], axis=0)
+            return 0
+
+        lax.fori_loop(0, nv // 128, pair, 0)
+        tt, ss = ii((Q, Q), 0), ii((Q, Q), 1)
+        e64t = (ii((nv, 128), 0) // 64 == ii((nv, 128), 1)).astype(BF)
+        kh, km, kl = split3(s["krow"][...])
+        kterm = dnn(kh, e64t) + dnn(km, e64t) + dnn(kl, e64t)
+        colg = jnp.concatenate([s["colg"][h, 0:1] for h in range(nh)] + [jnp.zeros((128 - nh, Q), F32)], axis=0)
+        dcum = s["rowg"][...] - colg.T + s["rs"][...]
+        da = tri_times((ss >= tt).astype(BF), dcum) + tri_times((ss < tt).astype(BF), s["gs"][...]) + kterm[0:1]
+        rate = hp[1:2]
+        dstep = s["ds"][...] + rate * da
+        draw = dstep * sigmoid(raw)
+        draw = jnp.where(ii((Q, 128), 1) < nh, draw, 0.0)
+        low[pl.ds(r0, Q), pl.ds(nv + 256, 128)] = draw.astype(BF)
+        gh[...] += jnp.concatenate([jnp.sum(draw, axis=0, keepdims=True), jnp.sum(da * step, axis=0, keepdims=True) * rate, jnp.zeros((6, 128), F32)], axis=0)
+        dqk = s["dqk"][...]
+        dc = dnn(dqk.astype(BF), s["b"][...]) + s["dcs"][...]
+        db = dnn(dqk.T.astype(BF), s["c"][...]) + s["dbs"][...]
+        sig = sigmoid(bc_pre)
+        dpre = jnp.concatenate([db, dc], axis=1) * (sig + bc_pre * sig * (1.0 - sig))
+        after2 = [None] + [jnp.concatenate([m, m], axis=1) for m in after[1:]]
+        low[pl.ds(r0, Q), pl.ds(nv, 256)] = later_sum(dpre, s["halobc"][...], after2, cbc[...]).astype(BF)
+        s["halobc"][...] = dpre[:8]
+        gbc[...] += jnp.concatenate(
+            [jnp.sum(dpre * bc_shifted[3 - k], axis=0, keepdims=True) for k in range(4)] + [jnp.sum(dpre, axis=0, keepdims=True), jnp.zeros((3, 256), F32)], axis=0)
+        return 0
+
+    lax.fori_loop(0, nb, block, 0)
+
+
+def run_forward(nv, vals, segc, segr, cx, cbc, hp):
+    sc = fwd_scratch(nv)
+    names = list(sc)
+    rows = vals.shape[0]
+
+    def kernel(vals, segc, segr, cx, cbc, hp, ssd, states, *scr):
+        ssd_forward(nv, vals, segc, segr, cx, cbc, hp, ssd, states, dict(zip(names, scr)))
+
+    vm = pl.BlockSpec(memory_space=pltpu.VMEM)
+    return pl.pallas_call(
+        kernel, out_shape=(jax.ShapeDtypeStruct((rows, nv), F32), jax.ShapeDtypeStruct((rows // Q, 128, nv), F32)),
+        in_specs=[vm] * 6, out_specs=[vm] * 2, scratch_shapes=[sc[n] for n in names],
+        compiler_params=pltpu.CompilerParams(vmem_limit_bytes=60 * 2**20), name="scan_forward",
+    )(vals, segc, segr, cx, cbc, hp)
+
+
+def run_backward(nv, vals, segc, segr, cx, cbc, hp, dy, states):
+    sc = bwd_scratch(nv)
+    names = list(sc)
+    rows = vals.shape[0]
+
+    def kernel(vals, segc, segr, cx, cbc, hp, dy, states, low, gx, gbc, gh, *scr):
+        ssd_backward(nv, vals, segc, segr, cx, cbc, hp, dy, states, low, gx, gbc, gh, dict(zip(names, scr)))
+
+    vm = pl.BlockSpec(memory_space=pltpu.VMEM)
+    outs = (jax.ShapeDtypeStruct((rows, nv + 384), BF), jax.ShapeDtypeStruct((8, nv), F32), jax.ShapeDtypeStruct((8, 256), F32), jax.ShapeDtypeStruct((8, 128), F32))
+    return pl.pallas_call(
+        kernel, out_shape=outs, in_specs=[vm] * 8, out_specs=[vm] * 4, scratch_shapes=[sc[n] for n in names],
+        compiler_params=pltpu.CompilerParams(vmem_limit_bytes=60 * 2**20), name="scan_backward",
+    )(vals, segc, segr, cx, cbc, hp, dy, states)
+
+
 INNER = 3072
 EPS = 1e-05
-
-
-def causal_conv(values, kernel, offset_bias, segment):
-    kernel_len = kernel.shape[0]
-    seq_len = values.shape[0]
-    padded = jnp.pad(values, ((kernel_len - 1, 0), (0, 0)))
-    seg_pad = jnp.pad(segment, (kernel_len - 1, 0), constant_values=-1)
-    result = jnp.zeros_like(values) + offset_bias[None, :]
-    for shift_at in range(kernel_len):
-        matches = (seg_pad[shift_at : shift_at + seq_len] == segment).astype(F32)
-        result = result + kernel[shift_at][None, :] * padded[shift_at : shift_at + seq_len] * matches[:, None]
-    return result
-
-
-def block_step(decay_rates, carried, block_in):
-    x_block, dt_block, b_block, c_block, seg_block, seg_before = block_in
-    block_rows = seg_block.shape[0]
-    log_decay = jnp.cumsum(dt_block * decay_rates[None, :], axis=0)
-    cum_heads = log_decay.T
-    position = lax.iota(jnp.int32, block_rows)
-    allowed = (position[:, None] >= position[None, :]) & (seg_block[:, None] == seg_block[None, :])
-    log_gaps = jnp.where(allowed[None], cum_heads[:, :, None] - cum_heads[:, None, :], 0.0)
-    decay_mat = jnp.where(allowed[None], jnp.exp(log_gaps), 0.0)
-    query_key = jnp.dot(c_block, b_block.T, precision=lax.Precision.HIGHEST, preferred_element_type=F32)
-    mixing = decay_mat * query_key[None] * dt_block.T[:, None, :]
-    within = jnp.einsum("hts,shp->thp", mixing, x_block, precision=lax.Precision.HIGHEST)
-    carry_on = (seg_block == seg_before).astype(F32)
-    from_state = jnp.einsum("tn,hpn->thp", c_block, carried, precision=lax.Precision.HIGHEST)
-    from_past = from_state * (jnp.exp(log_decay) * carry_on[:, None])[:, :, None]
-    last_seg = seg_block[block_rows - 1]
-    tail_weight = (
-        jnp.exp(log_decay[block_rows - 1][None, :] - log_decay)
-        * (seg_block == last_seg).astype(F32)[:, None]
-        * dt_block
-    )
-    keep_state = jnp.exp(log_decay[block_rows - 1]) * (last_seg == seg_before).astype(F32)
-    new_state = carried * keep_state[:, None, None] + jnp.einsum(
-        "sh,sn,shp->hpn", tail_weight, b_block, x_block, precision=lax.Precision.HIGHEST
-    )
-    return (new_state, within + from_past)
-
-
-def scan_ssd(x_heads, step_sizes, decay_rates, b_all, c_all, segment):
-    seq_len, head_count, head_size = x_heads.shape
-    blocks = seq_len // GROUP
-    state_size = b_all.shape[1]
-    seg_blocks = segment.reshape(blocks, GROUP)
-    seg_before = jnp.concatenate([jnp.full((1,), -1, dtype=jnp.int32), seg_blocks[:-1, GROUP - 1]])
-    initial = jnp.zeros((head_count, head_size, state_size), F32)
-    stepper = jax.checkpoint(block_step)
-
-    def scan_body(carried, block_in):
-        return stepper(decay_rates, carried, block_in)
-
-    _, outputs = lax.scan(
-        scan_body,
-        initial,
-        (
-            x_heads.reshape(blocks, GROUP, head_count, head_size),
-            step_sizes.reshape(blocks, GROUP, head_count),
-            b_all.reshape(blocks, GROUP, state_size),
-            c_all.reshape(blocks, GROUP, state_size),
-            seg_blocks,
-            seg_before,
-        ),
-    )
-    return outputs.reshape(seq_len, head_count, head_size)
-
-
-def ssm_mixer(segment, x_proj, bc_proj, dt_proj, gate_proj, conv_x, conv_bias_x, conv_bc, conv_bias_bc, dt_bias, a_log, skip_d):
-    x_conv = jax.nn.silu(causal_conv(x_proj, conv_x, conv_bias_x, segment))
-    bc_conv = jax.nn.silu(causal_conv(bc_proj, conv_bc, conv_bias_bc, segment))
-    state_size = bc_conv.shape[1] // 2
-    step_sizes = jax.nn.softplus(dt_proj + dt_bias[None, :])
-    decay_rates = -jnp.exp(a_log)
-    seq_len = x_proj.shape[0]
-    head_count = dt_proj.shape[1]
-    x_heads = x_conv.reshape(seq_len, head_count, -1)
-    scanned = scan_ssd(
-        x_heads, step_sizes, decay_rates, bc_conv[:, :state_size], bc_conv[:, state_size:], segment
-    )
-    scanned = scanned + skip_d[None, :, None] * x_heads
-    return scanned.reshape(seq_len, -1) * jax.nn.silu(gate_proj)
 
 
 def dot_nt(left, right):
@@ -402,12 +657,19 @@
     cot_all = cot_all.reshape(-1, cot_all.shape[-1])
     w_gate, w_out = wb[:, :inner], wb[:, inner:]
     vals = jnp.dot(normed_all, wa, preferred_element_type=F32)
-    x_val, bc_val, dt_val = vals[:, :inner], vals[:, inner : inner + 256], vals[:, inner + 256 : inner + 256 + heads]
     gate_val = jnp.dot(normed_all, w_gate, preferred_element_type=F32)
-    gated, mixer_back = jax.vjp(
-        functools.partial(ssm_mixer, seg_ids), x_val, bc_val, dt_val, gate_val,
-        own(conv_x, inner), own(conv_bias_x, inner), conv_bc, conv_bias_bc, own(dt_bias, heads), own(a_log, heads), own(skip_d, heads),
-    )
+    seg = seg_ids.astype(F32)
+    segc = jnp.broadcast_to(seg[:, None], (seg.shape[0], 128))
+    segr = jnp.broadcast_to(seg[None, :], (8, seg.shape[0]))
+    heads_row = lambda v: jnp.pad(own(v, heads), (0, 128 - heads))[None]
+    skip_row = jnp.broadcast_to(own(skip_d, heads)[:, None], (heads, 64)).reshape(1, inner)
+    cx = jnp.concatenate([own(conv_x, inner), own(conv_bias_x, inner)[None], skip_row, jnp.zeros((2, inner), F32)])
+    cbc = jnp.concatenate([conv_bc, conv_bias_bc[None], jnp.zeros((3, 256), F32)])
+    hp = jnp.concatenate([heads_row(dt_bias), -jnp.exp(heads_row(a_log)), jnp.zeros((6, 128), F32)])
+    ssd, states = run_forward(inner, vals, segc, segr, cx, cbc, hp)
+    gate_sig = sigmoid(gate_val)
+    silu_gate = gate_val * gate_sig
+    gated = ssd * silu_gate
     grad_normed_out = jnp.dot(cot_all, w_out, preferred_element_type=F32)
     scaled_grad = grad_normed_out * gain_dev[None, :]
     sums = lax.psum(jnp.stack([jnp.sum(gated * gated, axis=1), jnp.sum(scaled_grad * gated, axis=1)]), "tensor")
@@ -417,43 +679,39 @@
     term_out = dot_tn(cot_all, normed_out)
     grad_gain_dev = jnp.sum(grad_normed_out * gated * inv_scale[:, None], axis=0)
     grad_gated = scaled_grad * inv_scale[:, None] - gated * (inv_scale * inv_scale * inv_scale * sums[1] / INNER)[:, None]
-    (grad_x, grad_bc, grad_dt, grad_gate, g_conv_x, g_bias_x, g_conv_bc, g_bias_bc, g_dt_bias, g_a_log, g_skip) = mixer_back(grad_gated)
-    low_a = jnp.concatenate([grad_x, grad_bc, grad_dt, jnp.zeros((grad_dt.shape[0], 128 - heads), F32)], axis=1).astype(BF)
+    low_a, gx, gbc, gh = run_backward(inner, vals, segc, segr, cx, cbc, hp, grad_gated * silu_gate, states)
+    grad_gate = grad_gated * ssd * (gate_sig + silu_gate * (1.0 - gate_sig))
     low_gate = grad_gate.astype(BF)
-    grad_normed = (dot_nt(low_gate, w_gate) + dot_nt(low_a, wa)).astype(BF)
+    grad_normed = dot_nt(low_gate, w_gate) + dot_nt(low_a, wa)
+    part_pre = jnp.sum(grad_normed * normed_all.astype(F32), axis=0) / pre_gain
+    grad_normed = grad_normed.astype(BF)
     term_a = dot_tn(normed_all, low_a).astype(BF)
     term_b = jnp.concatenate([dot_tn(normed_all, low_gate), term_out], axis=1).astype(BF)
-    small = jnp.concatenate(
-        [g_conv_x.reshape(-1), g_bias_x, grad_gain_dev, g_conv_bc.reshape(-1), g_bias_bc]
-        + [jnp.pad(v, (0, 128 - heads)) for v in (g_dt_bias, g_a_log, g_skip)]
-    )
-    n_small = small.shape[0]
-    small = jnp.pad(small, (0, 8192 - n_small)).reshape(64, 128)
+    small = jnp.concatenate([gx[:5].reshape(-1), grad_gain_dev, gx[5], part_pre, gbc[:5].reshape(-1), gh[:2].reshape(-1)])
+    small = jnp.pad(small, (0, 9216 - small.shape[0])).reshape(72, 128)
     blocks = (4, 4, 2, rows)
     ra, rb, own_out, grad_own, smalls = reduce_all(
-        term_a.reshape(blocks + term_a.shape[1:]), term_b.reshape(blocks + term_b.shape[1:]),
+        inner, term_a.reshape(blocks + term_a.shape[1:]), term_b.reshape(blocks + term_b.shape[1:]),
         partial_out.reshape(4, 256, -1), grad_normed.reshape(4, 256, -1), small,
     )
     output = (hidden + own_out).astype(BF)
     scaled = grad_own * pre_gain[None, :]
     proj = jnp.mean(scaled * hidden, axis=1)
     grad_hidden = cotangent.astype(F32) + scaled * inv_rms[:, None] - hidden * (inv_rms * inv_rms * inv_rms * proj)[:, None]
-    part_pre = jnp.sum(grad_own * hidden * inv_rms[:, None], axis=0)
-    d_pre = lax.psum(part_pre, ("dp", "tensor"))
-    smalls = smalls.reshape(4, 8192)
-    d_bc = lax.psum(ra[:, inner : inner + 256], "tensor")
+    smalls = smalls.reshape(4, 9216)
     spread = lambda lo, n, k: smalls[:, lo : lo + n * k].reshape(4, k, n).transpose(1, 0, 2).reshape(k, 4 * n)
-    d_conv_x = spread(0, inner, 4)
-    at = 4 * inner
-    d_bias_x = spread(at, inner, 1)[0]
-    d_gain = spread(at + inner, inner, 1)[0]
-    at = at + 2 * inner
-    bc_sums = jnp.sum(smalls[:, at : at + 5 * 256], axis=0)
-    at = at + 5 * 256
-    d_dt_bias, d_a_log, d_skip = (spread(at + 128 * i, heads, 1)[0] for i in range(3))
+    x_sums = spread(0, inner, 7)
+    at = 7 * inner
+    width = pre_gain.shape[0]
+    d_skip = x_sums[6].reshape(-1, 64).sum(axis=1)
+    both = jnp.sum(smalls[:, at : at + width + 5 * 256], axis=0)
+    d_pre = both[:width]
+    bc_sums = both[width:]
+    at = at + width + 5 * 256
+    d_dt_bias, d_a_log = (spread(at + 128 * i, 128, 1)[0].reshape(4, 128)[:, :heads].reshape(-1) for i in range(2))
     return (
-        output, grad_hidden, d_pre, rb[:, :inner], ra[:, :inner], d_bc, ra[:, inner + 256 : inner + 256 + heads],
-        d_conv_x, d_bias_x, bc_sums[:1024].reshape(4, 256), bc_sums[1024:], d_dt_bias, d_a_log, d_skip, d_gain,
+        output, grad_hidden, d_pre, rb[:, :inner], ra[:, :inner], ra[:, inner : inner + 256], ra[:, inner + 256 : inner + 256 + heads],
+        x_sums[:4], x_sums[4], bc_sums[:1024].reshape(4, 256), bc_sums[1024:], d_dt_bias, d_a_log, d_skip, x_sums[5],
         rb[:, inner:].T,
     )
 

time: 752 us -> 306 us (0.41); the launches traced: 743 us -> 305 us
  local copies, waits for them, and re-layouts: 257 us -> 28.9 us
  matrix products: 160 us -> 54.4 us
  blocking collectives: 85.7 us -> 8.15 us
  other arithmetic: 100 us -> 22.5 us
  Pallas kernels: 125 us -> 190 us
  loops' own time: 12.9 us -> 0 us
    dynamic_update_slice x16 -> x0, local copies, waits for them, and re-layouts: 149 us -> none  [scan_ssd(): lax.scan(scan_body, initial, (x_heads.reshape(blocks, GROUP, head_count,...]
    dot_general x56 -> x0, matrix products: 102 us -> none  [the longest x12 58 us: block_step(): jnp.einsum('hts,shp->thp', mixing, x_block, precision=lax.Precision.HIGHEST)]
    psum x2 -> x0, blocking collectives: 77.8 us -> none  [the longest x1 64.2 us: per_device(): d_pre = lax.psum(part_pre, ('dp', 'tensor'))]
    pallas_call x1 -> x3, Pallas kernels: 62.1 us -> 128 us  [the longest x1 65.2 us: reduce_all(): pl.pallas_call(functools.partial(rs_kernel, bc0), out_shape=outs, in_spec...]
    reduce_sum x15 -> x3, other arithmetic: 25.1 us -> 2.47 us  [the longest x1 1.81 us: per_device(): proj = jnp.mean(scaled * hidden, axis=1)]
    mul x33 -> x0, other arithmetic: 21.8 us -> none  [the longest x16 6.03 us: block_step(): jnp.exp(log_decay[block_rows - 1]) * (last_seg == seg_before).astype(F32)]
    another operation x50 -> x0, other arithmetic: 18.1 us -> none
    dynamic_slice x20 -> x0, local copies, waits for them, and re-layouts: 15.6 us -> none  [scan_ssd(): lax.scan(scan_body, initial, (x_heads.reshape(blocks, GROUP, head_count,...]
where the time goes in v2:
time: 306 us; the launch traced here: 305 us
  Pallas kernels  190 us (62%)
  matrix products  54.4 us (18%)
  local copies, waits for them, and re-layouts  28.9 us (9%)
  other arithmetic  22.5 us (7%)
  blocking collectives  8.15 us (3%)
    pallas_call x1, Pallas kernels, reduce_all(): pl.pallas_call(functools.partial(rs_kernel, bc0), out_shape=outs, in_spec...  65.2 us
    pallas_call x1, Pallas kernels, gather(): pl.pallas_call(functools.partial(ag_kernel, ten), out_shape=outs, in_spec...  62.6 us
    pallas_call x1, Pallas kernels, run_backward(): pl.pallas_call(kernel, out_shape=outs, in_specs=[vm] * 8, out_specs=[vm]...  40.7 us
    pallas_call x1, Pallas kernels, run_forward(): pl.pallas_call(kernel, out_shape=(jax.ShapeDtypeStruct((rows, nv), F32),...  21.9 us
    dot_general x3, matrix products, dot_tn(): lax.dot_general(left, right, (((0,), (0,)), ((), ())), preferred_element_...  17 us
    dot_general x3, matrix products, dot_nt(): lax.dot_general(left, right, (((1,), (1,)), ((), ())), preferred_element_...  16.9 us
    dot_general x1, matrix products, per_device(): vals = jnp.dot(normed_all, wa, preferred_element_type=F32)  9.36 us
    dot_general x2, local copies, waits for them, and re-layouts, dot_tn(): lax.dot_general(left, right, (((0,), (0,)), ((), ())), preferred_element_...  9.31 us

profile of v2, /device:TPU:1, one launch (start us, length us, event | category | flops | bytes accessed | tf_op | source)
XLA Modules:
  0.0 305.3 jit_solution(6323282954642357550)
XLA Ops:
  0.6 0.0 copy-start
  0.7 0.7 dynamic_slice.21
  1.4 0.7 dynamic_slice.22
  2.1 0.1 pad.20.clone
  2.2 0.7 maximum_maximum_fusion.2.hp
  2.9 0.7 dynamic_slice.20
  3.6 0.1 broadcast_in_dim.24
  3.7 0.1 reshape.147
  3.8 0.8 dynamic_slice.19
  4.6 0.1 pad.27.clone
  4.6 0.7 maximum_maximum_fusion.cx
  5.3 1.4 fusion.8
  6.7 2.3 fusion.10.h
  9.0 1.6 pad_maximum_fusion.1.wb
  10.6 0.8 copy.40
  11.3 1.6 concatenate.23.wa
  13.0 62.6 %gather_all.1 = (bf16[4,4,2,48,1152]{4,3,2,1,0:T(8,128)(2,1)}, bf16[4,4,2,48,1536]{4,3,2,1,0:T(8,128)(2,1)}, bf16[4,256,1536]{2,1,0:T(8,128)(2,1)}, bf16[4,256,1536]{2,1,0:T(8,128)(2,1)}) custom-call(bf16[48,1152]{1,0:T(8,128)(2,1)} %concatenate.23.wa, bf16[48,1536]{1,0:T(8,128)(2,1)} %pad_maximum_fusion.1.wb, bf16[256,1536]{1,0:T(8,128)(2,1)} %fusion.10.h, ...), custom_call_target="tpu_custom_call" | custom-call | tf_op jit(solution)/shard_map/gather_all/pallas_call | solution.py:131
  75.6 0.0 copy-start.18
  75.6 0.0 copy-start.17
  75.6 0.0 copy-start.19
  75.7 9.4 %fusion.26.vals = f32[1024,1152]{1,0:T(8,128)} fusion(bf16[1024,1536]{1,0:T(8,128)(2,1)} %bitcast.62, bf16[1536,1152]{1,0:T(8,128)(2,1)} %bitcast.96), kind=kOutput, calls=%fused_computation.68 | convolution fusion | flops 3623878656 | bytes 11403264 | tf_op jit(solution)/shard_map/dot_general | solution.py:659
  85.0 1.0 broadcast_in_dim.21.segc
  86.0 0.6 broadcast_in_dim.22.segr
  86.6 0.1 pad.23.clone
  86.7 0.7 maximum_maximum_fusion.1.cbc
  87.4 21.9 %scan_forward.1 = (f32[1024,768]{1,0:T(8,128)}, f32[4,128,768]{2,1,0:T(8,128)}) custom-call(f32[1024,1152]{1,0:T(8,128)} %fusion.26.vals, f32[1024,128]{1,0:T(8,128)} %broadcast_in_dim.21.segc, f32[8,1024]{1,0:T(8,128)} %broadcast_in_dim.22.segr, f32[8,768]{1,0:T(8,128)} %maximum_maximum_fusion.cx, f32[8,256]{1,0:T(8,128)} %maximum_maximum_fusion.1.cbc, ...), custom_call_target="tpu_custom_call" | custom-call | tf_op jit(solution)/shard_map/scan_forward/pallas_call | solution.py:603
  109.3 4.4 %fusion.3 = f32[1024,768]{1,0:T(8,128)S(1)} fusion(bf16[1024,1536]{1,0:T(8,128)(2,1)S(1)} %bitcast.64, bf16[1536,1536]{1,0:T(8,128)(2,1)} %bitcast.92), kind=kOutput, calls=%fused_computation.20 | convolution fusion | flops 2415919104 | bytes 8650752 | tf_op jit(solution)/shard_map/dot_general | solution.py:660
  113.7 0.8 dynamic_slice.23
  114.5 6.7 %multiply_reduce_fusion.3 = (f32[1024]{0:T(1024)S(1)}, f32[1024]{0:T(1024)S(1)}, f32[1024,768]{1,0:T(8,128)S(1)}, f32[1024,768]{1,0:T(8,128)}) fusion(f32[768]{0:T(1024)S(1)} %dynamic_slice.23, f32[1024,768]{1,0:T(8,128)S(1)} %copy-done.4, f32[1024,768]{1,0:T(8,128)S(1)} %fusion.3, bf16[1024,1536]{1,0:T(8,128)(2,1)S(1)} %bitcast.67, ...), kind=kOutput, calls=%fused_computation.10 | convolution fusion | flops 2423781376 | bytes 18099200 | tf_op jit(solution)/shard_map/dot_general | solution.py:673
  121.3 8.2 %psum.7 = f32[2,1024]{1,0:T(2,128)S(1)} all-reduce(f32[2,1024]{1,0:T(2,128)S(1)} %pad_maximum_fusion.2), channel_id=1, replica_groups=mesh['dp'=32,'tensor'=4] {'tensor'}, use_global_device_ids=true, to_apply=%region_3.4 | all-reduce | flops 2048 | bytes 16384 | tf_op jit(solution)/shard_map/psum | solution.py:675
  129.5 6.4 %multiply_convert_fusion.1 = (bf16[1024,768]{1,0:T(8,128)(2,1)}, f32[1024,768]{1,0:T(8,128)}, f32[768]{0:T(1024)S(1)}) fusion(f32[1024,768]{1,0:T(8,128)} %get-tuple-element.35, f32[1024,768]{1,0:T(8,128)} %copy-done.5, f32[1024,768]{1,0:T(8,128)S(1)} %get-tuple-element.80, f32[1024]{0:T(1024)S(1)} %fusion.18, f32[1024]{0:T(1024)S(1)} %bitcast.81, ...), kind=kLoop, calls=%fused_computation.7 | loop fusion | flops 14155008 | bytes 17315840 | tf_op jit(solution)/shard_map/convert_element_type | solution.py:684
  135.8 40.7 %scan_backward.1 = (bf16[1024,1152]{1,0:T(8,128)(2,1)}, f32[8,768]{1,0:T(8,128)}, f32[8,256]{1,0:T(8,128)}, f32[8,128]{1,0:T(8,128)}) custom-call(f32[1024,1152]{1,0:T(8,128)} %fusion.26.vals, f32[1024,128]{1,0:T(8,128)} %broadcast_in_dim.21.segc, f32[8,1024]{1,0:T(8,128)} %broadcast_in_dim.22.segr, f32[8,768]{1,0:T(8,128)} %maximum_maximum_fusion.cx, ...), custom_call_target="tpu_custom_call" | custom-call | tf_op jit(solution)/shard_map/scan_backward/pallas_call | solution.py:620
  176.5 0.7 reshape.153
  177.3 0.8 slice_reduce_fusion.2
  178.1 4.9 %fusion.1 = f32[1024,1536]{1,0:T(8,128)S(1)} fusion(bf16[1024,768]{1,0:T(8,128)(2,1)} %get-tuple-element.81, bf16[1536,1536]{1,0:T(8,128)(2,1)} %bitcast.94), kind=kOutput, calls=%fused_computation.18 | convolution fusion | flops 2415919104 | bytes 10223616 | tf_op jit(solution)/shard_map/dot_general | solution.py:631
  183.0 0.0 copy-start.15
  183.0 6.1 %multiply_reduce_fusion = (f32[1536]{0:T(1024)S(1)}, bf16[1024,1536]{1,0:T(8,128)(2,1)}) fusion(bf16[4,256,1536]{2,1,0:T(8,128)(2,1)S(1)} %copy-done.8, f32[1024,1536]{1,0:T(8,128)S(1)} %fusion.1, bf16[1024,1152]{1,0:T(8,128)(2,1)S(1)} %copy-done.21, bf16[1536,1152]{1,0:T(8,128)(2,1)S(1)} %bitcast.97), kind=kOutput, calls=%fused_computation.1 | convolution fusion | flops 3631741440 | bytes 18487296 | tf_op jit(solution)/shard_map/dot_general | solution.py:631
  189.2 0.7 constant_dynamic-update-slice_fusion
  189.9 0.6 pad_bitcast_fusion.sv
  190.5 5.8 %convolution_convert_fusion.1 = bf16[1024,1536]{1,0:T(8,128)(2,1)} fusion(bf16[1536,1536]{1,0:T(8,128)(2,1)} %bitcast.95, f32[1024,768]{1,0:T(8,128)S(1)} %get-tuple-element.80, f32[1024]{0:T(1024)S(1)} %bitcast.82, f32[768]{0:T(1024)S(1)} %dynamic_slice.23), kind=kOutput, calls=%fused_computation.4 | convolution fusion | flops 2419851264 | bytes 8657920 | tf_op jit(solution)/shard_map/dot_general | solution.py:631
  196.4 4.7 %copy.43 = bf16[1536,1024]{1,0:T(8,128)(2,1)} copy(bf16[1536,1024]{0,1:T(8,128)(2,1)} %bitcast.63) | data formatting | bytes 6291456 | tf_op jit(solution)/shard_map/dot_general | solution.py:635
  201.0 6.4 %convolution_convert_fusion.3 = bf16[4,4,2,48,768]{4,3,2,1,0:T(8,128)(2,1)} fusion(bf16[4,4,2,48,1024]{4,3,2,1,0:T(8,128)(2,1)} %bitcast.69, bf16[1024,768]{1,0:T(8,128)(2,1)} %get-tuple-element.81), kind=kOutput, calls=%fused_computation.26 | convolution fusion | flops 2417098752 | bytes 7077888 | tf_op jit(solution)/shard_map/dot_general | solution.py:635
  207.4 4.7 %copy.44 = bf16[1536,1024]{1,0:T(8,128)(2,1)} copy(bf16[1536,1024]{0,1:T(8,128)(2,1)} %bitcast.66) | data formatting | bytes 6291456 | tf_op jit(solution)/shard_map/dot_general | solution.py:635
  212.1 4.8 %convolution_convert_fusion.2 = bf16[4,4,2,48,768]{4,3,2,1,0:T(8,128)(2,1)S(1)} fusion(bf16[4,4,2,48,1024]{4,3,2,1,0:T(8,128)(2,1)} %bitcast.68, f32[1024,768]{1,0:T(8,128)S(1)} %get-tuple-element.80, f32[1024]{0:T(1024)S(1)} %bitcast.83, f32[768]{0:T(1024)S(1)} %dynamic_slice.23), kind=kOutput, calls=%fused_computation.25 | convolution fusion | flops 2419458048 | bytes 8657920 | tf_op jit(solution)/shard_map/dot_general | solution.py:635
  216.9 3.0 pad_maximum_fusion.gb
  219.9 1.3 copy-done.22
  221.2 5.8 %convolution_convert_fusion = bf16[1536,1152]{1,0:T(8,128)(2,1)} fusion(bf16[1024,1536]{1,0:T(8,128)(2,1)S(1)} %bitcast.65, bf16[1024,1152]{1,0:T(8,128)(2,1)S(1)} %copy-done.22), kind=kOutput, calls=%fused_computation | convolution fusion | flops 3625648128 | bytes 9043968 | tf_op jit(solution)/shard_map/dot_general | solution.py:635
  227.0 65.2 %reduce_all.1 = (f32[48,1152]{1,0:T(8,128)}, f32[48,1536]{1,0:T(8,128)}, f32[256,1536]{1,0:T(8,128)}, f32[256,1536]{1,0:T(8,128)}, f32[4,72,128]{2,1,0:T(8,128)}) custom-call(bf16[4,4,2,48,1152]{4,3,2,1,0:T(8,128)(2,1)} %bitcast.61, bf16[4,4,2,48,1536]{4,3,2,1,0:T(8,128)(2,1)} %pad_maximum_fusion.gb, bf16[4,256,1536]{2,1,0:T(8,128)(2,1)} %bitcast.71, ...), custom_call_target="tpu_custom_call" | custom-call | tf_op jit(solution)/shard_map/reduce_all/pallas_call | solution.py:287
  292.2 1.8 fusion.12
  294.0 0.0 copy-done.3
  294.1 3.4 %fusion.13 = (f32[256,1536]{1,0:T(8,128)}, bf16[256,1536]{1,0:T(8,128)(2,1)}) fusion(bf16[256,1536]{1,0:T(8,128)(2,1)S(1)} %copy-done.2, bf16[256,1536]{1,0:T(8,128)(2,1)S(1)} %copy-done.6, f32[256,1536]{1,0:T(8,128)S(1)} %copy-done.3, f32[256]{0:T(256)S(1)} %fusion.21, f32[1536]{0:T(1024)S(1)} %copy-done.15, f32[256]{0:T(256)S(1)} %add_rsqrt_fusion, ...), kind=kLoop, calls=%fused_computation.32 | loop fusion | flops 3538944 | bytes 7086080 | tf_op jit(solution)/shard_map/sub | solution.py:700
  297.6 0.6 fusion.25
  298.2 0.1 reshape_squeeze.3
  298.3 0.6 reduce_sum.79
  299.0 0.6 slice.128
  299.6 0.7 slice_bitcast_fusion
  300.4 0.6 slice.114
  301.0 0.6 slice.126
  301.6 0.6 slice.131
  302.1 0.6 reshape.159
  302.7 0.6 reshape.160
  303.3 0.7 slice.106
  304.0 0.6 slice.107
  304.6 0.7 copy.45
  (66 shorter events, 0.3 us)
Async XLA Ops:
  0.6 2.2 copy-start
  75.6 9.4 %copy-start.18 = (s32[1024]{0:T(1024)S(1)}, s32[1024]{0:T(1024)}, u32[]{:S(2)}) copy-start(s32[1024]{0:T(1024)} %param.18) | copy-start | bytes 12292
  75.6 11.1 %copy-start.17 = (f32[4,256]{1,0:T(4,128)S(1)}, f32[4,256]{1,0:T(4,128)}, u32[]{:S(2)}) copy-start(f32[4,256]{1,0:T(4,128)} %param.26) | copy-start | bytes 12292
  75.6 11.1 %copy-start.19 = (f32[256]{0:T(256)S(1)}, f32[256]{0:T(256)}, u32[]{:S(2)}) copy-start(f32[256]{0:T(256)} %param.27) | copy-start | bytes 3076
  85.0 24.2 %copy-start.7 = (bf16[4,256,1536]{2,1,0:T(8,128)(2,1)S(1)}, bf16[4,256,1536]{2,1,0:T(8,128)(2,1)}, u32[]{:S(2)}) copy-start(bf16[4,256,1536]{2,1,0:T(8,128)(2,1)} %get-tuple-element.31) | copy-start | bytes 9437188
  109.2 5.3 %copy-start.4 = (f32[1024,768]{1,0:T(8,128)S(1)}, f32[1024,768]{1,0:T(8,128)}, u32[]{:S(2)}) copy-start(f32[1024,768]{1,0:T(8,128)} %get-tuple-element.35) | copy-start | bytes 9437188
  109.2 5.3 %copy-start.10 = (bf16[4,256,1536]{2,1,0:T(8,128)(2,1)S(1)}, bf16[4,256,1536]{2,1,0:T(8,128)(2,1)}, u32[]{:S(2)}) copy-start(bf16[4,256,1536]{2,1,0:T(8,128)(2,1)} %get-tuple-element.33) | copy-start | bytes 9437188
  113.7 7.6 %copy-start.5 = (f32[1024,768]{1,0:T(8,128)}, f32[1024,768]{1,0:T(8,128)S(1)}, u32[]{:S(2)}) copy-start(f32[1024,768]{1,0:T(8,128)S(1)} %fusion.3) | copy-start | bytes 9437188
  178.0 5.0 %copy-start.8 = (bf16[4,256,1536]{2,1,0:T(8,128)(2,1)S(1)}, bf16[4,256,1536]{2,1,0:T(8,128)(2,1)}, u32[]{:S(2)}) copy-start(bf16[4,256,1536]{2,1,0:T(8,128)(2,1)} %get-tuple-element.31) | copy-start | bytes 9437188
  178.0 5.0 %copy-start.20 = (bf16[4,4,2,48,1152]{4,3,2,1,0:T(8,128)(2,1)S(1)}, bf16[4,4,2,48,1152]{4,3,2,1,0:T(8,128)(2,1)}, u32[]{:S(2)}) copy-start(bf16[4,4,2,48,1152]{4,3,2,1,0:T(8,128)(2,1)} %get-tuple-element.32) | copy-start | bytes 10616836
  178.0 5.0 %copy-start.21 = (bf16[1024,1152]{1,0:T(8,128)(2,1)S(1)}, bf16[1024,1152]{1,0:T(8,128)(2,1)}, u32[]{:S(2)}) copy-start(bf16[1024,1152]{1,0:T(8,128)(2,1)} %get-tuple-element.37) | copy-start | bytes 7077892
  183.0 6.1 %copy-start.15 = (f32[1536]{0:T(1024)S(1)}, f32[1536]{0:T(1024)}, u32[]{:S(2)}) copy-start(f32[1536]{0:T(1024)} %param.19) | copy-start | bytes 18436
  183.0 6.1 %copy-start.16 = (f32[8,256]{1,0:T(8,128)S(1)}, f32[8,256]{1,0:T(8,128)}, u32[]{:S(2)}) copy-start(f32[8,256]{1,0:T(8,128)} %get-tuple-element.39) | copy-start | bytes 24580
  212.1 4.8 %copy-start.11 = (bf16[4,4,2,48,768]{4,3,2,1,0:T(8,128)(2,1)S(1)}, bf16[4,4,2,48,768]{4,3,2,1,0:T(8,128)(2,1)}, u32[]{:S(2)}) copy-start(bf16[4,4,2,48,768]{4,3,2,1,0:T(8,128)(2,1)} %convolution_convert_fusion.3) | copy-start | bytes 7077892
  216.9 3.0 copy-start.9
  216.9 4.3 %copy-start.22 = (bf16[1024,1152]{1,0:T(8,128)(2,1)S(1)}, bf16[1024,1152]{1,0:T(8,128)(2,1)}, u32[]{:S(2)}) copy-start(bf16[1024,1152]{1,0:T(8,128)(2,1)} %get-tuple-element.37) | copy-start | bytes 7077892
  227.0 65.2 %copy-start.2 = (bf16[256,1536]{1,0:T(8,128)(2,1)S(1)}, bf16[256,1536]{1,0:T(8,128)(2,1)}, u32[]{:S(2)}) copy-start(bf16[256,1536]{1,0:T(8,128)(2,1)} %param.17) | copy-start | bytes 2359300
  227.0 67.0 %copy-start.6 = (bf16[256,1536]{1,0:T(8,128)(2,1)S(1)}, bf16[256,1536]{1,0:T(8,128)(2,1)}, u32[]{:S(2)}) copy-start(bf16[256,1536]{1,0:T(8,128)(2,1)} %c.1) | copy-start | bytes 2359300
  292.2 1.9 copy-start.3
  294.0 11.3 %copy-start.1 = (f32[4,3072]{1,0:T(4,128)S(1)}, f32[4,3072]{1,0:T(4,128)}, u32[]{:S(2)}) copy-start(f32[4,3072]{1,0:T(4,128)} %param.24) | copy-start | bytes 147460
  294.1 3.4 %copy-start.14 = (f32[4,72,128]{2,1,0:T(8,128)S(1)}, f32[4,72,128]{2,1,0:T(8,128)}, u32[]{:S(2)}) copy-start(f32[4,72,128]{2,1,0:T(8,128)} %get-tuple-element.43) | copy-start | bytes 442372
  294.1 5.5 %copy-start.12 = (f32[48,1536]{1,0:T(8,128)S(1)}, f32[48,1536]{1,0:T(8,128)}, u32[]{:S(2)}) copy-start(f32[48,1536]{1,0:T(8,128)} %get-tuple-element.44) | copy-start | bytes 884740
  294.1 9.3 %copy-start.13 = (f32[48,1152]{1,0:T(8,128)S(1)}, f32[48,1152]{1,0:T(8,128)}, u32[]{:S(2)}) copy-start(f32[48,1152]{1,0:T(8,128)} %get-tuple-element.45) | copy-start | bytes 663556

commit v3 on v1

v3 whole, which is shorter than its diff:
```python
import functools

import jax
import jax.numpy as jnp
from jax import lax
from jax.experimental import pallas as pl
from jax.experimental.pallas import tpu as pltpu
from jax.sharding import PartitionSpec as P

MESH = pl.DeviceIdType.MESH
F32 = jnp.float32
BF = jnp.bfloat16


def place():
    dp = lax.axis_index("dp")
    t = lax.axis_index("tensor")
    return dp // 8, (dp // 2) % 4, dp % 2, t


def dev(x, z, yh, t):
    return ((x * 4 + z) * 2 + yh, t)


def m4(v):
    return (v + 8) % 4


def neighbour(axis, d):
    x, z, yh, t = place()
    return dev(m4(x + d), z, yh, t) if axis == "x" else dev(x, m4(z + d), yh, t)


def tensor_peers():
    x, z, yh, t = place()
    yl, co = t // 2, t % 2
    slots = (yl * 2 + 1 - co, (1 - yl) * 2 + co, (1 - yl) * 2 + 1 - co)
    return [dev(x, z, yh, s) for s in slots], slots


def greet(peers):
    bar = pltpu.get_barrier_semaphore()
    for p in peers:
        pl.semaphore_signal(bar, inc=1, device_id=p, device_id_type=MESH)
    pl.semaphore_wait(bar, len(peers))


def send(src, dst, send_sem, recv_sem, to):
    return pltpu.make_async_remote_copy(
        src_ref=src, dst_ref=dst, send_sem=send_sem, recv_sem=recv_sem, device_id=to, device_id_type=MESH
    )


class Gather:
    N = 25

    def __init__(self, own, dst, r1, send_sem, recv_sem):
        x, z, yh, _ = place()
        r2 = "z" if r1 == "x" else "x"
        n = own.shape[0]

        def rows(d1, d2, y=None):
            ix, iz = (m4(x + d1), m4(z + d2)) if r1 == "x" else (m4(x + d2), m4(z + d1))
            first = (ix * 4 + iz) * 2
            if y is None:
                return dst.at[pl.ds(pl.multiple_of(first * n, n), 2 * n)]
            return dst.at[pl.ds(pl.multiple_of((first + y) * n, n), n)]

        self.mine = rows(0, 0, yh)
        self.own = own
        near1, near2 = [neighbour(r1, 1), neighbour(r1, -1)], [neighbour(r2, 1), neighbour(r2, -1)]
        other = rows(0, 0, 1 - yh)
        plan = [(own, self.mine, dev(x, z, 1 - yh, place()[3]))]
        plan += [(own, self.mine, p) for p in near1 + near2]
        plan += [(other, other, p) for p in near1 + near2]
        plan += [(rows(-1, 0, 0),) * 2 + (near1[0],), (rows(1, 0, 1),) * 2 + (near1[1],)]
        for d1 in (-1, 1, 2):
            plan += [(rows(d1, 0),) * 2 + (p,) for p in near2]
        for d1 in (0, -1, 1, 2):
            plan += [(rows(d1, -1, 0),) * 2 + (near2[0],), (rows(d1, 1, 1),) * 2 + (near2[1],)]
        self.plan, self.send_sem, self.recv_sem = plan, send_sem, recv_sem

    def copy(self, k):
        src, dst, to = self.plan[k]
        return send(src, dst, self.send_sem.at[k], self.recv_sem.at[k], to)

    STEPS = (
        ((), (0, 1, 2, 3, 4)),
        ((0,), (5, 6, 7, 8)),
        ((1, 2, 5, 6), (9, 10, 11, 12, 13, 14)),
        ((9, 10), (15, 16)),
        ((3, 4, 7, 8), (17, 18)),
        ((11, 12, 13, 14), (19, 20, 21, 22)),
        ((15, 16), (23, 24)),
        ((17, 18, 19, 20, 21, 22, 23, 24), ()),
    )

    def step(self, k):
        arrive, go = self.STEPS[k]
        for i in arrive:
            self.copy(i).wait_recv()
        for i in go:
            self.copy(i).start()

    def finish(self):
        for k in range(self.N):
            self.copy(k).wait_send()


Q = 256
LOG2E = 1.4426950408889634
NEG = -1e30


def dnn(a, b):
    return jnp.dot(a, b, preferred_element_type=F32)


def dnt(a, b):
    return lax.dot_general(a, b, (((1,), (1,)), ((), ())), preferred_element_type=F32)


def split3(v):
    hi = v.astype(BF)
    r = v - hi.astype(F32)
    mid = r.astype(BF)
    lo = (r - mid.astype(F32)).astype(BF)
    return hi, mid, lo


def spread3(v, mat):
    hi, mid, lo = split3(v)
    return dnn(jnp.concatenate([hi, mid, lo], axis=1), jnp.concatenate([mat, mat, mat], axis=0))


def tri_times(mat, v):
    hi, mid, lo = split3(v)
    out = dnn(mat, jnp.concatenate([hi, mid, lo], axis=1))
    w = v.shape[1]
    return out[:, :w] + out[:, w : 2 * w] + out[:, 2 * w :]


def ii(shape, dim):
    return lax.broadcasted_iota(jnp.int32, shape, dim)


def sigmoid(v):
    return 1.0 / (1.0 + jnp.exp2(v * -LOG2E))


def softplus(v):
    e = jnp.exp2(jnp.abs(v) * -LOG2E)
    u = 1.0 + e
    log1p = jnp.where(u == 1.0, e, jnp.log(u) * (e / jnp.where(u == 1.0, 1.0, u - 1.0)))
    return jnp.maximum(v, 0.0) + log1p


def conv_terms(ext, match, taps):
    n = ext.shape[0] - 8
    shifted = [ext[8:]] + [jnp.where(match[k], ext[8 - k : 8 + n - k], 0.0) for k in (1, 2, 3)]
    pre = taps[4:5] + sum(taps[3 - k : 4 - k] * shifted[k] for k in range(4))
    return pre, shifted


def with_earlier(ref, r0, lanes):
    prev = ref[pl.ds(pl.multiple_of(jnp.maximum(r0 - 8, 0), 8), 8), lanes]
    return jnp.concatenate([prev, ref[pl.ds(r0, Q), lanes]], axis=0)


def match_rows(segc, r0):
    prev = segc[pl.ds(pl.multiple_of(jnp.maximum(r0 - 8, 0), 8), 8), :]
    prev = jnp.where(r0 > 0, prev, -1.0)
    cur = segc[pl.ds(r0, Q), :]
    ext = jnp.concatenate([prev, cur], axis=0)
    return [None] + [ext[8 - k : 8 + Q - k] == cur for k in (1, 2, 3)]


def block_setup(c, nv, vals, segc, segr, cbc, hp, bt_ref, b_ref, c_ref, ct_ref, qk_ref, bias_ref, cum_ref, cumt_ref, step_ref, tail_ref, keep_ref, ex_ref, keep_out):
    r0 = pl.multiple_of(c * Q, Q)
    match = match_rows(segc, r0)
    m2 = [None] + [jnp.concatenate([m, m], axis=1) for m in match[1:]]
    ext = with_earlier(vals, r0, pl.ds(nv, 256))
    pre, shifted = conv_terms(ext, m2, cbc[...])
    bc = pre * sigmoid(pre)
    bb = bc[:, :128].astype(BF)
    cc = bc[:, 128:].astype(BF)
    b_ref[...] = bb
    c_ref[...] = cc
    bt_ref[...] = bc[:, :128].T.astype(BF)
    if ct_ref is not None:
        ct_ref[...] = bc[:, 128:].T.astype(BF)
    qk_ref[...] = dnt(cc, bb)
    seg = segc[pl.ds(r0, Q), :]
    segs = segr[0:1, pl.ds(r0, Q)]
    tt, ss = ii((Q, Q), 0), ii((Q, Q), 1)
    allowed = (tt >= ss) & (jnp.concatenate([seg, seg], axis=1) == segs)
    bias_ref[...] = jnp.where(allowed, 0.0, NEG)
    raw = vals[pl.ds(r0, Q), pl.ds(nv + 256, 128)] + hp[0:1]
    step = softplus(raw)
    tri = (tt >= ss).astype(BF)
    cum = tri_times(tri, step * (hp[1:2] * LOG2E))
    cumt = cum.T
    for h in range(nv // 64):
        cumt_ref[h] = jnp.broadcast_to(cumt[h : h + 1], (8, Q))
    exm = ex_ref[...]
    cum_ref[...] = spread3(cum, exm)
    e64 = (ii((128, nv), 0) == ii((128, nv), 1) // 64).astype(BF)
    step_ref[...] = spread3(step, e64)
    prev_seg = jnp.where(c > 0, segc[pl.ds(pl.multiple_of(jnp.maximum(r0 - 8, 0), 8), 8), :][7:8], -1.0)
    last_seg = seg[Q - 1 :]
    cum_last = cum[Q - 1 :]
    carry = (seg == prev_seg).astype(F32)
    tailm = (seg == last_seg).astype(F32)
    tail = jnp.exp2(cum_last - cum) * tailm
    tail_ref[...] = spread3(tail, e64)
    keep = jnp.exp2(cum_last) * (last_seg == prev_seg).astype(F32)
    keep_ref[...] = spread3(jnp.broadcast_to(keep, (8, 128)), e64)
    keep_out[...] = spread3(jnp.exp2(cum) * carry, e64)
    return match, pre, shifted, raw, step


def decay(cum_ref, cumt_ref, bias_ref, h, rows, cols):
    col = cum_ref[rows, pl.ds(pl.multiple_of(h * 128, 128), 128)]
    row = cumt_ref[h, 0:1, cols]
    return jnp.exp2(col - row + bias_ref[rows, cols])


def fwd_scratch(nv):
    V = lambda s, d=F32: pltpu.VMEM(s, d)
    nh = nv // 64
    return dict(
        bt=V((128, Q), BF), b=V((Q, 128), BF), c=V((Q, 128), BF), qk=V((Q, Q)), bias=V((Q, Q)), cum=V((Q, nh * 128)), cumt=V((nh, 8, Q)),
        step=V((Q, nv)), tail=V((Q, nv)), keep=V((8, nv)), ecum=V((Q, nv)), ex=V((128, nh * 128), BF), state=V((128, nv)), m=V((2, Q, Q), BF),
    )


def ssd_forward(nv, vals, segc, segr, cx, cbc, hp, ssd, states, s, hook=lambda at: None):
    nh = nv // 64
    s["ex"][...] = (ii((128, nh * 128), 0) == ii((128, nh * 128), 1) // 128).astype(BF)
    s["state"][...] = jnp.zeros_like(s["state"])
    s["m"][...] = jnp.zeros_like(s["m"])

    def block(c, _):
        r0 = pl.multiple_of(c * Q, Q)
        match, *_r = block_setup(c, nv, vals, segc, segr, cbc, hp, s["bt"], s["b"], s["c"], None, s["qk"], s["bias"], s["cum"], s["cumt"], s["step"], s["tail"], s["keep"], s["ex"], s["ecum"])
        states[c] = s["state"][...]

        def pair(j, _):
            hook(c * (nv // 128) + j)
            lanes = pl.ds(pl.multiple_of(j * 128, 128), 128)
            pre, _sh = conv_terms(with_earlier(vals, r0, lanes), match, cx[:, lanes])
            x = pre * sigmoid(pre)
            u = x * s["step"][:, lanes]
            ub = u.astype(BF)
            st = s["state"][:, lanes]
            y = dnn(s["c"][...], st.astype(BF)) * s["ecum"][:, lanes]
            y = y + cx[5:6, lanes] * x
            for e in range(2):
                for r in range(4):
                    rows = slice(r * 64, r * 64 + 64)
                    for k in range(1 if r < 2 else 2):
                        cols = slice(k * 128, k * 128 + 128)
                        s["m"][e, rows, cols] = (decay(s["cum"], s["cumt"], s["bias"], 2 * j + e, rows, cols) * s["qk"][rows, cols]).astype(BF)
            y0 = dnn(s["m"][0], ub)
            y1 = dnn(s["m"][1], ub)
            ssd[pl.ds(r0, Q), lanes] = y + jnp.where(ii((Q, 128), 1) < 64, y0, y1)
            s["state"][:, lanes] = st * s["keep"][0:1, lanes] + dnn(s["bt"][...], (u * s["tail"][:, lanes]).astype(BF))
            return 0

        lax.fori_loop(0, nv // 128, pair, 0)
        return 0

    lax.fori_loop(0, vals.shape[0] // Q, block, 0)


def bwd_scratch(nv):
    V = lambda s, d=F32: pltpu.VMEM(s, d)
    d = fwd_scratch(nv)
    d.update(ct=V((128, Q), BF), dqk=V((Q, Q)), dstate=V((128, nv)), dcs=V((Q, 128)), dbs=V((Q, 128)), rowg=V((Q, 128)), colg=V((nv // 64, 8, Q)), rs=V((Q, 128)),
             gs=V((Q, 128)), ds=V((Q, 128)), krow=V((8, nv)), halo=V((8, nv)), halobc=V((8, 256)), dm=V((Q, Q)))
    return d


def to_head(v, j):
    red = (ii((128, 128), 1) == 2 * j + ii((128, 128), 0) // 64).astype(BF)
    hi = v.astype(BF)
    lo = (v - hi.astype(F32)).astype(BF)
    return dnn(jnp.concatenate([hi, lo], axis=1), jnp.concatenate([red, red], axis=0))


def later_sum(dpre, halo, match_ext, taps):
    ext = jnp.concatenate([dpre, halo], axis=0)
    n = dpre.shape[0]
    out = taps[3:4] * dpre
    for k in (1, 2, 3):
        out = out + taps[3 - k : 4 - k] * jnp.where(match_ext[k], ext[k : n + k], 0.0)
    return out


def ssd_backward(nv, vals, segc, segr, cx, cbc, hp, dy_ref, states, low, gx, gbc, gh, s, hook=lambda at: None):
    nh = nv // 64
    nb = vals.shape[0] // Q
    s["ex"][...] = (ii((128, nh * 128), 0) == ii((128, nh * 128), 1) // 128).astype(BF)
    for n in ("dstate", "halo", "halobc", "colg", "m"):
        s[n][...] = jnp.zeros_like(s[n])
    gx[...] = jnp.zeros_like(gx)
    gbc[...] = jnp.zeros_like(gbc)
    gh[...] = jnp.zeros_like(gh)

    def block(i, _):
        c = nb - 1 - i
        r0 = pl.multiple_of(c * Q, Q)
        match, bc_pre, bc_shifted, raw, step = block_setup(c, nv, vals, segc, segr, cbc, hp, s["bt"], s["b"], s["c"], s["ct"], s["qk"], s["bias"], s["cum"], s["cumt"], s["step"], s["tail"], s["keep"], s["ex"], s["ecum"])
        nxt = segc[pl.ds(pl.multiple_of(jnp.minimum(r0 + Q, segc.shape[0] - 8), 8), 8), :]
        seg = segc[pl.ds(r0, Q), :]
        ext = jnp.concatenate([seg, nxt], axis=0)
        after = [None] + [ext[k : Q + k] == seg for k in (1, 2, 3)]
        for n in ("dqk", "dcs", "dbs", "rowg", "rs", "gs", "ds"):
            s[n][...] = jnp.zeros_like(s[n])

        def pair(j, _):
            hook(i * (nv // 128) + j)
            lanes = pl.ds(pl.multiple_of(j * 128, 128), 128)
            taps = cx[:, lanes]
            pre, shifted = conv_terms(with_earlier(vals, r0, lanes), match, taps)
            sig = sigmoid(pre)
            x = pre * sig
            stepe = s["step"][:, lanes]
            taile = s["tail"][:, lanes]
            u = x * stepe
            ub = u.astype(BF)
            dy = dy_ref[pl.ds(r0, Q), lanes].astype(F32)
            dyb = dy.astype(BF)
            dyt = dy.T.astype(BF)
            st = states[c, :, lanes]
            stb = st.astype(BF)
            dst = s["dstate"][:, lanes]
            dstb = dst.astype(BF)
            edy = s["ecum"][:, lanes] * dy
            edyb = edy.astype(BF)
            s["rs"][...] += to_head(edy * dnn(s["c"][...], stb), j)
            s["dcs"][...] += dnt(edyb, stb)
            tu = taile * u
            v = dnn(s["b"][...], dstb)
            s["dbs"][...] += dnt(tu.astype(BF), dstb)
            s["gs"][...] += to_head(tu * v, j)
            keep = s["keep"][0:1, lanes]
            s["krow"][:, lanes] = jnp.broadcast_to(keep * jnp.sum(st * dst, axis=0, keepdims=True), (8, 128))
            s["dstate"][:, lanes] = keep * dst + dnn(s["ct"][...], edyb)
            lane = ii((Q, 128), 1)
            parts = []
            for e in range(2):
                h = 2 * j + e
                mine = (lane < 64) if e == 0 else (lane >= 64)
                s["dm"][...] = dnt(jnp.where(mine, dy, 0.0).astype(BF), ub)
                colsum = [jnp.zeros((1, 128), F32), jnp.zeros((1, 128), F32)]
                for r in range(4):
                    rows = slice(r * 64, r * 64 + 64)
                    rowsum = jnp.zeros((64, 128), F32)
                    for k in range(1 if r < 2 else 2):
                        cols = slice(k * 128, k * 128 + 128)
                        dec = decay(s["cum"], s["cumt"], s["bias"], h, rows, cols)
                        qk = s["qk"][rows, cols]
                        p = s["dm"][rows, cols] * dec
                        s["dqk"][rows, cols] += p
                        g = p * qk
                        rowsum = rowsum + g
                        colsum[k] = colsum[k] + jnp.sum(g, axis=0, keepdims=True)
                        s["m"][e, rows, cols] = (dec * qk).astype(BF)
                    tot = jnp.sum(rowsum, axis=1, keepdims=True)
                    s["rowg"][rows] += jnp.where(ii((64, 128), 1) == h, tot, 0.0)
                s["colg"][h] = jnp.broadcast_to(jnp.concatenate(colsum, axis=1), (8, Q))
                parts.append(dnn(dyt[e * 64 : e * 64 + 64], s["m"][e]))
            du = jnp.concatenate(parts, axis=0).T + taile * v
            s["ds"][...] += to_head(du * x, j)
            skip = taps[5:6]
            dx = du * stepe + skip * dy
            dpre = dx * (sig + x * (1.0 - sig))
            low[pl.ds(r0, Q), lanes] = later_sum(dpre, s["halo"][:, lanes], after, taps).astype(BF)
            s["halo"][:, lanes] = dpre[:8]
            gx[:, lanes] += jnp.concatenate(
                [jnp.sum(dpre * shifted[3 - k], axis=0, keepdims=True) for k in range(4)]
                + [jnp.sum(dpre, axis=0, keepdims=True), jnp.sum(dy * x, axis=0, keepdims=True), jnp.zeros((2, 128), F32)], axis=0)
            return 0

        lax.fori_loop(0, nv // 128, pair, 0)
        tt, ss = ii((Q, Q), 0), ii((Q, Q), 1)
        e64t = (ii((nv, 128), 0) // 64 == ii((nv, 128), 1)).astype(BF)
        kh, km, kl = split3(s["krow"][...])
        kterm = dnn(kh, e64t) + dnn(km, e64t) + dnn(kl, e64t)
        colg = jnp.concatenate([s["colg"][h, 0:1] for h in range(nh)] + [jnp.zeros((128 - nh, Q), F32)], axis=0)
        dcum = s["rowg"][...] - colg.T + s["rs"][...]
        da = tri_times((ss >= tt).astype(BF), dcum) + tri_times((ss < tt).astype(BF), s["gs"][...]) + kterm[0:1]
        rate = hp[1:2]
        dstep = s["ds"][...] + rate * da
        draw = dstep * sigmoid(raw)
        draw = jnp.where(ii((Q, 128), 1) < nh, draw, 0.0)
        low[pl.ds(r0, Q), pl.ds(nv + 256, 128)] = draw.astype(BF)
        gh[...] += jnp.concatenate([jnp.sum(draw, axis=0, keepdims=True), jnp.sum(da * step, axis=0, keepdims=True) * rate, jnp.zeros((6, 128), F32)], axis=0)
        dqk = s["dqk"][...]
        dc = dnn(dqk.astype(BF), s["b"][...]) + s["dcs"][...]
        db = dnn(dqk.T.astype(BF), s["c"][...]) + s["dbs"][...]
        sig = sigmoid(bc_pre)
        dpre = jnp.concatenate([db, dc], axis=1) * (sig + bc_pre * sig * (1.0 - sig))
        after2 = [None] + [jnp.concatenate([m, m], axis=1) for m in after[1:]]
        low[pl.ds(r0, Q), pl.ds(nv, 256)] = later_sum(dpre, s["halobc"][...], after2, cbc[...]).astype(BF)
        s["halobc"][...] = dpre[:8]
        gbc[...] += jnp.concatenate(
            [jnp.sum(dpre * bc_shifted[3 - k], axis=0, keepdims=True) for k in range(4)] + [jnp.sum(dpre, axis=0, keepdims=True), jnp.zeros((3, 256), F32)], axis=0)
        return 0

    lax.fori_loop(0, nb, block, 0)


def run_forward(nv, vals, segc, segr, cx, cbc, hp):
    sc = fwd_scratch(nv)
    names = list(sc)
    rows = vals.shape[0]

    def kernel(vals, segc, segr, cx, cbc, hp, ssd, states, *scr):
        ssd_forward(nv, vals, segc, segr, cx, cbc, hp, ssd, states, dict(zip(names, scr)))

    vm = pl.BlockSpec(memory_space=pltpu.VMEM)
    return pl.pallas_call(
        kernel, out_shape=(jax.ShapeDtypeStruct((rows, nv), F32), jax.ShapeDtypeStruct((rows // Q, 128, nv), F32)),
        in_specs=[vm] * 6, out_specs=[vm] * 2, scratch_shapes=[sc[n] for n in names],
        compiler_params=pltpu.CompilerParams(vmem_limit_bytes=60 * 2**20), name="scan_forward",
    )(vals, segc, segr, cx, cbc, hp)


def run_backward(nv, vals, segc, segr, cx, cbc, hp, dy, states):
    sc = bwd_scratch(nv)
    names = list(sc)
    rows = vals.shape[0]

    def kernel(vals, segc, segr, cx, cbc, hp, dy, states, low, gx, gbc, gh, *scr):
        ssd_backward(nv, vals, segc, segr, cx, cbc, hp, dy, states, low, gx, gbc, gh, dict(zip(names, scr)))

    vm = pl.BlockSpec(memory_space=pltpu.VMEM)
    outs = (jax.ShapeDtypeStruct((rows, nv + 384), BF), jax.ShapeDtypeStruct((8, nv), F32), jax.ShapeDtypeStruct((8, 256), F32), jax.ShapeDtypeStruct((8, 128), F32))
    return pl.pallas_call(
        kernel, out_shape=outs, in_specs=[vm] * 8, out_specs=[vm] * 4, scratch_shapes=[sc[n] for n in names],
        compiler_params=pltpu.CompilerParams(vmem_limit_bytes=60 * 2**20), name="scan_backward",
    )(vals, segc, segr, cx, cbc, hp, dy, states)


INNER = 3072
EPS = 1e-05


def at_step(step, events):
    for k, fn in events:
        pl.when(step == k)(fn)


def forward_kernel(
    names, nv,
    hid, cot_own, w_own0, w_own1, w_own2, w_own3, pgain, segc, segr, cx, cbc, hp, ggain,
    o_w0, o_w1, o_w2, o_w3, o_nrm, o_cot, o_vals, o_states, o_no, o_lg, o_dy, o_gg,
    w0, w1, w2, w3, nrm, cot, vals, states, ssd, gate, gno, no, lg, dy, sums_own, sums_in,
    wsend, wrecv, tsend, trecv, ssend, srecv, lsem, *scan_scratch,
):
    s = dict(zip(names, scan_scratch))
    x, z, yh, t = place()
    yl, co = t // 2, t % 2
    tp, slots = tensor_peers()
    width = hid.shape[1]
    greet([dev(x, z, 1 - yh, t)] + [neighbour(a, d) for a in "xz" for d in (1, -1)] + tp)
    owns, dsts, outs = (w_own0, w_own1, w_own2, w_own3), (w0, w1, w2, w3), (o_w0, o_w1, o_w2, o_w3)
    groups = lambda ks: [Gather(owns[k], dsts[k], "xz"[k % 2], wsend.at[k], wrecv.at[k]) for k in ks]
    first, second = (0, 1), (2, 3)

    def step(ks, n):
        for g in groups(ks):
            g.step(n)

    def saved(i, src, dst):
        return pltpu.make_async_copy(src, dst, lsem.at[i])

    mine = pl.ds(pl.multiple_of(t * 256, 256), 256)
    theirs = pl.ds(pl.multiple_of(slots[1] * 256, 256), 256)

    def tensor_copies(i, own, dst):
        return (
            send(own, dst.at[mine], tsend.at[i, 0], trecv.at[i, 0], tp[1]),
            send(own, dst.at[mine], tsend.at[i, 1], trecv.at[i, 1], tp[0]),
            send(dst.at[theirs], dst.at[theirs], tsend.at[i, 2], trecv.at[i, 2], tp[0]),
        )

    step(first, 0)

    def norm_rows(i, _):
        rows = pl.ds(pl.multiple_of(i * 64, 64), 64)
        h = hid[rows].astype(F32)
        inv = lax.rsqrt(jnp.mean(h * h, axis=1, keepdims=True) + EPS)
        nrm[pl.ds(pl.multiple_of(t * 256 + i * 64, 64), 64)] = (h * inv * pgain[0:1]).astype(BF)
        return 0

    lax.fori_loop(0, 4, norm_rows, 0)
    for k in range(4):
        g = groups((k,))[0]
        g.mine[...] = g.own[...]
    cot[mine] = cot_own[...]
    nrm_copies = tensor_copies(0, nrm.at[mine], nrm)
    cot_copies = tensor_copies(1, cot_own, cot)
    nrm_copies[0].start()
    nrm_copies[1].start()
    for n in (1, 2, 3):
        step(first, n)
    nrm_copies[0].wait_recv()
    nrm_copies[2].start()
    cot_copies[0].start()
    cot_copies[1].start()
    step(second, 0)
    for n in (4, 5, 6):
        step(first, n)
    step(second, 1)
    step(first, 7)
    nrm_copies[1].wait_recv()
    nrm_copies[2].wait_recv()

    def project(i, _):
        rows = pl.ds(pl.multiple_of(i * 256, 256), 256)
        n = nrm[rows]
        at = 0
        for w in (w0, w1):
            c = w.shape[1]
            vals[rows, at : at + c] = jnp.dot(n, w[...], preferred_element_type=F32)
            at += c
        return 0

    lax.fori_loop(0, 4, project, 0)
    early = [(0, w0, o_w0), (1, w1, o_w1), (2, nrm, o_nrm), (3, vals, o_vals)]
    for e in early:
        saved(*e).start()

    def cot_forward():
        cot_copies[0].wait_recv()
        cot_copies[2].start()

    events = [(0, lambda: step(second, 2)), (4, lambda: step(second, 3)), (8, lambda: step(second, 4)), (14, cot_forward), (16, lambda: step(second, 5)), (20, lambda: step(second, 6))]
    ssd_forward(nv, vals, segc, segr, cx, cbc, hp, ssd, states, s, lambda at: at_step(at, events))
    step(second, 7)
    cot_copies[1].wait_recv()
    cot_copies[2].wait_recv()
    late = [(4, w2, o_w2), (5, w3, o_w3), (6, cot, o_cot), (7, states, o_states)]
    for e in late:
        saved(*e).start()

    def inner(i, _):
        rows = pl.ds(pl.multiple_of(i * 256, 256), 256)
        g = jnp.dot(nrm[rows], w2[...], preferred_element_type=F32)
        gate[rows] = g
        o = jnp.dot(cot[rows], w3[...], preferred_element_type=F32)
        gno[rows] = o
        gated = ssd[rows] * (g * sigmoid(g))
        sq = jnp.sum(gated * gated, axis=1, keepdims=True)
        cr = jnp.sum(o * ggain[0:1] * gated, axis=1, keepdims=True)
        lane = ii((256, 128), 1)
        both = jnp.where(lane == 0, sq, jnp.where(lane == 1, cr, 0.0))
        sums_own[:, rows] = both.T[:8]
        return 0

    lax.fori_loop(0, 4, inner, 0)
    small = [send(sums_own, sums_in.at[k], ssend.at[k], srecv.at[k], p) for k, p in enumerate(tp)]
    for c in small:
        c.start()
    for c in small:
        c.wait_recv()
    o_gg[...] = jnp.zeros_like(o_gg)

    def outer(i, _):
        rows = pl.ds(pl.multiple_of(i * 256, 256), 256)
        tot = sums_own[:, rows] + sums_in[0, :, rows] + sums_in[1, :, rows] + sums_in[2, :, rows]
        cols = jnp.concatenate([tot, jnp.zeros((120, 256), F32)], axis=0).T
        inv = lax.rsqrt(cols[:, 0:1] / INNER + EPS)
        cross = inv * inv * inv * cols[:, 1:2] / INNER
        for k in range(nv // 128):
            lanes = pl.ds(k * 128, 128)
            g, y, o, gain = gate[rows, lanes], ssd[rows, lanes], gno[rows, lanes], ggain[0:1, lanes]
            sig = sigmoid(g)
            silu = g * sig
            gated = y * silu
            scaled = gated * inv
            no[rows, lanes] = (scaled * gain).astype(BF)
            o_gg[0:1, lanes] += jnp.sum(o * scaled, axis=0, keepdims=True)
            grad = o * gain * inv - gated * cross
            dy[rows, lanes] = (grad * silu).astype(BF)
            lg[rows, lanes] = (grad * y * (sig + silu * (1.0 - sig))).astype(BF)
        return 0

    lax.fori_loop(0, 4, outer, 0)
    last = [(8, no, o_no), (9, lg, o_lg), (10, dy, o_dy)]
    for e in last:
        saved(*e).start()
    for g in groups((0, 1, 2, 3)):
        g.finish()
    for c in nrm_copies + cot_copies + tuple(small):
        c.wait_send()
    for e in early + late + last:
        saved(*e).wait()


def run_k1(hid, cot_own, w_owns, pgain, segc, segr, cx, cbc, hp, ggain):
    anys, vm = pl.BlockSpec(memory_space=pl.ANY), pl.BlockSpec(memory_space=pltpu.VMEM)
    nv = cx.shape[1]
    rows = segc.shape[0]
    d = hid.shape[1]
    sh = jax.ShapeDtypeStruct
    cols = [w.shape[1] for w in w_owns]
    nvals = cols[0] + cols[1]
    outs = [sh((d, c), BF) for c in cols] + [sh((rows, d), BF)] * 2 + [sh((rows, nvals), F32), sh((rows // Q, 128, nv), F32)] + [sh((rows, nv), BF)] * 3 + [sh((8, nv), F32)]
    V = lambda shape, dt: pltpu.VMEM(shape, dt)
    D = pltpu.SemaphoreType.DMA
    scan = fwd_scratch(nv)
    scratch = [V((d, c), BF) for c in cols] + [V((rows, d), BF)] * 2 + [V((rows, nvals), F32), V((rows // Q, 128, nv), F32)] + [V((rows, nv), F32)] * 3 + [V((rows, nv), BF)] * 3
    scratch += [V((8, rows), F32), V((3, 8, rows), F32), D((4, Gather.N)), D((4, Gather.N)), D((2, 3)), D((2, 3)), D((3,)), D((3,)), D((11,))]
    scratch += list(scan.values())
    return pl.pallas_call(
        functools.partial(forward_kernel, list(scan), nv), out_shape=outs, in_specs=[vm] * 13, out_specs=[anys] * 11 + [vm], scratch_shapes=scratch,
        compiler_params=pltpu.CompilerParams(collective_id=0, has_side_effects=True, vmem_limit_bytes=62 * 2**20), name="forward_all",
    )(hid, cot_own, *w_owns, pgain, segc, segr, cx, cbc, hp, ggain)


def rs_kernel(bc0, ga, gb, po, pn, sv, oa, ob, oo, on, osv,
              va, vb, vo, vn, r1a, r1b, r2a, r2b, ha, hb, q1a, q1b, q2a, q2b, ka, kb, ya, yb,
              co_buf, cy_buf, cs_buf, sacc, sx, sz, sy, st, bct,
              lsem, wsend, wrecv, tsend, trecv, ssend, srecv, bsend, brecv):
    x, z, yh, t = place()
    yl = t // 2; co = t % 2
    m4 = lambda v: (v + 8) % 4
    def nb(axis, d):
        if axis == "x": return dev(m4(x + d), z, yh, t)
        return dev(x, m4(z + d), yh, t)
    ypeer = dev(x, z, 1 - yh, t)
    tcore = dev(x, z, yh, yl * 2 + (1 - co))
    tyl = dev(x, z, yh, (1 - yl) * 2 + co)
    tdiag = dev(x, z, yh, (1 - yl) * 2 + 1 - co)
    bar = pltpu.get_barrier_semaphore()
    peers = [ypeer, tcore, tyl, tdiag] + [nb(a, d) for a in "xz" for d in (1, 2, 3)]
    for p in peers:
        pl.semaphore_signal(bar, inc=1, device_id=p, device_id_type=MESH)
    loads = []
    for i, (s, d) in enumerate(((ga, va), (gb, vb), (po, vo), (pn, vn))):
        cp = pltpu.make_async_copy(s, d, lsem.at[i]); cp.start(); loads.append(cp)
    pl.semaphore_wait(bar, len(peers))
    sends = []
    def rc(src, dst, ss, rs, to):
        cp = pltpu.make_async_remote_copy(src_ref=src, dst_ref=dst, send_sem=ss, recv_sem=rs, device_id=to, device_id_type=MESH)
        cp.start(); sends.append(cp); return cp
    pos = {"x": x, "z": z}
    halves = ((va, "z", "x", r1a, r2a, ha, q1a, q2a, ka, ya, oa), (vb, "x", "z", r1b, r2b, hb, q1b, q2b, kb, yb, ob))
    def b1(v, a1, d, k=None):
        p = m4(pos[a1] + d)
        if a1 == "z": return v.at[:, p] if k is None else v.at[pl.ds(2 * k, 2), p]
        return v.at[p] if k is None else v.at[p, pl.ds(2 * k, 2)]
    small = []
    for d in (1, 2, 3):
        small.append(rc(sv, sx.at[d - 1], ssend.at[d - 1], srecv.at[d - 1], nb("x", d)))
    for l in loads[:2]: l.wait()
    s1 = []
    for i, (v, a1, a2, r1, r2, *_) in enumerate(halves):
        s1.append((rc(b1(v, a1, 2, 0), r1.at[0], wsend.at[i, 0], wrecv.at[i, 0], nb(a1, 1)),
                   rc(b1(v, a1, 2, 1), r1.at[1], wsend.at[i, 1], wrecv.at[i, 1], nb(a1, -1))))
    s1b = []
    for i, (v, a1, a2, r1, r2, *_) in enumerate(halves):
        s1b.append((rc(b1(v, a1, 1, 1), r2.at[0, pl.ds(2, 2)], wsend.at[i, 2], wrecv.at[i, 2], nb(a1, 1)),
                    rc(b1(v, a1, -1, 0), r2.at[1, pl.ds(0, 2)], wsend.at[i, 3], wrecv.at[i, 3], nb(a1, -1))))
    tr = []
    for l in loads[2:]: l.wait()
    for i, v in enumerate((vo, vn)):
        a = rc(v.at[(1 - yl) * 2 + 1 - co], co_buf.at[i, 0], tsend.at[i, 0], trecv.at[i, 0], tcore)
        b = rc(v.at[yl * 2 + 1 - co], co_buf.at[i, 1], tsend.at[i, 1], trecv.at[i, 1], tcore)
        tr.append((a, b))
    for i, v in enumerate((vo, vn)):
        tr[i][0].wait_recv()
        def addc(j, _, i=i, v=v):
            rows = pl.ds(pl.multiple_of(j * 32, 32), 32)
            cs_buf[i, rows] = (v[(1 - yl) * 2 + co, rows].astype(F32) + co_buf[i, 0, rows].astype(F32)).astype(BF)
            return 0
        lax.fori_loop(0, 8, addc, 0)
        tr[i] = tr[i] + (rc(cs_buf.at[i], cy_buf.at[i], tsend.at[i, 2], trecv.at[i, 2], tyl),)
    for s in small: s.wait_recv()
    sacc[0] = sv[...] + sx[0] + sx[1] + sx[2]
    small = [rc(sacc.at[0], sz.at[d - 1], ssend.at[2 + d], srecv.at[2 + d], nb("z", d)) for d in (1, 2, 3)]
    s1c = []
    for i, (v, a1, a2, r1, r2, *_) in enumerate(halves):
        for side, dd, k in ((0, 1, 0), (1, -1, 1)):
            s1[i][side].wait_recv()
            p = m4(pos[a1] + dd)
            def add1(j, _, v=v, a1=a1, r1=r1, side=side, p=p, k=k):
                e = j // 2 ; y = j % 2
                if a1 == "z":
                    v[2 * k + e, p, y] = (v[2 * k + e, p, y].astype(F32) + r1[side, e, y].astype(F32)).astype(BF)
                else:
                    v[p, 2 * k + e, y] = (v[p, 2 * k + e, y].astype(F32) + r1[side, e, y].astype(F32)).astype(BF)
                return 0
            lax.fori_loop(0, 4, add1, 0)
            s1c.append(rc(b1(v, a1, dd, k), r2.at[side, pl.ds(2 * k, 2)], wsend.at[i, 4 + side], wrecv.at[i, 4 + side], nb(a1, dd)))
    for s in small: s.wait_recv()
    sacc[1] = sacc[0] + sz[0] + sz[1] + sz[2]
    small = [rc(sacc.at[1], sy, ssend.at[6], srecv.at[6], ypeer)]
    s2 = []
    for i, (v, a1, a2, r1, r2, h, q1, q2, kk, yy, oo_) in enumerate(halves):
        s1b[i][0].wait_recv(); s1b[i][1].wait_recv()
        s1c[2 * i].wait_recv(); s1c[2 * i + 1].wait_recv()
        p = pos[a1]
        def add2(j, _, v=v, a1=a1, r2=r2, h=h, p=p):
            e = j // 2; y = j % 2
            own = v[e, p, y] if a1 == "z" else v[p, e, y]
            h[e, y] = (own.astype(F32) + r2[0, e, y].astype(F32) + r2[1, e, y].astype(F32)).astype(BF)
            return 0
        lax.fori_loop(0, 8, add2, 0)
        q = pos[a2]
        s2.append((rc(h.at[m4(q + 2), 0], q1.at[0], wsend.at[i, 6], wrecv.at[i, 6], nb(a2, 1)),
                   rc(h.at[m4(q + 2), 1], q1.at[1], wsend.at[i, 7], wrecv.at[i, 7], nb(a2, -1)),
                   rc(h.at[m4(q + 1), 1], q2.at[0, 1], wsend.at[i, 8], wrecv.at[i, 8], nb(a2, 1)),
                   rc(h.at[m4(q - 1), 0], q2.at[1, 0], wsend.at[i, 9], wrecv.at[i, 9], nb(a2, -1))))
    for s in small: s.wait_recv()
    sacc[2] = sacc[1] + sy[...]
    small = [rc(sacc.at[2], st.at[j], ssend.at[7 + j], srecv.at[7 + j], d_) for j, d_ in enumerate((tcore, tyl, tdiag))]
    s2c = []
    for i, (v, a1, a2, r1, r2, h, q1, q2, kk, yy, oo_) in enumerate(halves):
        q = pos[a2]
        for side, dd in ((0, 1), (1, -1)):
            s2[i][side].wait_recv()
            pp = m4(q + dd)
            h[pp, side] = (h[pp, side].astype(F32) + q1[side].astype(F32)).astype(BF)
            s2c.append(rc(h.at[pp, side], q2.at[side, side], wsend.at[i, 10 + side], wrecv.at[i, 10 + side], nb(a2, dd)))
    s3 = []
    for i, (v, a1, a2, r1, r2, h, q1, q2, kk, yy, oo_) in enumerate(halves):
        q = pos[a2]
        s2[i][2].wait_recv(); s2[i][3].wait_recv()
        s2c[2 * i].wait_recv(); s2c[2 * i + 1].wait_recv()
        kk[...] = (h[q, 1 - yh].astype(F32) + q2[0, 1 - yh].astype(F32) + q2[1, 1 - yh].astype(F32)).astype(BF)
        s3.append(rc(kk, yy, wsend.at[i, 12], wrecv.at[i, 12], ypeer))
    for i, (v, o) in enumerate(((vo, oo), (vn, on))):
        tr[i][1].wait_recv(); tr[i][2].wait_recv()
        def addf(j, _, i=i, v=v, o=o):
            rows = pl.ds(pl.multiple_of(j * 32, 32), 32)
            o[rows] = v[t, rows].astype(F32) + co_buf[i, 1, rows].astype(F32) + cy_buf[i, rows].astype(F32)
            return 0
        lax.fori_loop(0, 8, addf, 0)
    tens = []
    for i, (v, a1, a2, r1, r2, h, q1, q2, kk, yy, o) in enumerate(halves):
        q = pos[a2]
        s3[i].wait_recv()
        o[...] = h[q, yh].astype(F32) + q2[0, yh].astype(F32) + q2[1, yh].astype(F32) + yy[...].astype(F32)
        if i == 0:
            bct[3] = o[:, bc0 : bc0 + 256]
            tens = [rc(bct.at[3], bct.at[j], bsend.at[j], brecv.at[j], d_) for j, d_ in enumerate((tcore, tyl, tdiag))]
    for cp in tens: cp.wait_recv()
    oa[:, bc0 : bc0 + 256] = bct[3] + bct[0] + bct[1] + bct[2]
    for s in small: s.wait_recv()
    osv[t] = sacc[2]
    osv[yl * 2 + 1 - co] = st[0]
    osv[(1 - yl) * 2 + co] = st[1]
    osv[(1 - yl) * 2 + 1 - co] = st[2]
    for cp in sends: cp.wait_send()

def reduce_all(bc0, ga, gb, po, pn, sv):
    anys = pl.BlockSpec(memory_space=pl.ANY); vm = pl.BlockSpec(memory_space=pltpu.VMEM)
    ca, cb = ga.shape[-1], gb.shape[-1]; R = sv.shape[0]
    outs = (jax.ShapeDtypeStruct((48, ca), F32), jax.ShapeDtypeStruct((48, cb), F32), jax.ShapeDtypeStruct((256, 1536), F32),
            jax.ShapeDtypeStruct((256, 1536), F32), jax.ShapeDtypeStruct((4, R, 128), F32))
    D = pltpu.SemaphoreType.DMA
    V = lambda *s, d=BF: pltpu.VMEM(s, d)
    scratch = [V(4, 4, 2, 48, ca), V(4, 4, 2, 48, cb), V(4, 256, 1536), V(4, 256, 1536),
               V(2, 2, 2, 48, ca), V(2, 2, 2, 48, cb), V(2, 4, 2, 48, ca), V(2, 4, 2, 48, cb),
               V(4, 2, 48, ca), V(4, 2, 48, cb), V(2, 48, ca), V(2, 48, cb), V(2, 2, 48, ca), V(2, 2, 48, cb),
               V(48, ca), V(48, cb), V(48, ca), V(48, cb),
               V(2, 2, 256, 1536), V(2, 256, 1536), V(2, 256, 1536),
               V(3, R, 128, d=F32), V(3, R, 128, d=F32), V(3, R, 128, d=F32), V(R, 128, d=F32), V(3, R, 128, d=F32), V(4, 48, 256, d=F32),
               D((4,)), D((2, 13)), D((2, 13)), D((2, 3)), D((2, 3)), D((10,)), D((10,)), D((3,)), D((3,))]
    return pl.pallas_call(functools.partial(rs_kernel, bc0), out_shape=outs, in_specs=[anys] * 4 + [vm], out_specs=[vm] * 5, scratch_shapes=scratch,
        compiler_params=pltpu.CompilerParams(collective_id=1, has_side_effects=True, vmem_limit_bytes=60 * 2**20), name="reduce_all")(ga, gb, po, pn, sv)


def dot_nt(left, right):
    return lax.dot_general(left, right, (((1,), (1,)), ((), ())), preferred_element_type=F32)


def dot_tn(left, right):
    return lax.dot_general(left, right, (((0,), (0,)), ((), ())), preferred_element_type=F32)


def per_device(
    hidden_in, seg_ids, pre_gain, proj_gate, proj_x, proj_bc, proj_dt, conv_x, conv_bias_x, conv_bc, conv_bias_bc,
    dt_bias, a_log, skip_d, gate_gain, proj_out, cotangent,
):
    t = lax.axis_index("tensor")
    inner = proj_gate.shape[1]
    heads = proj_dt.shape[1]
    own = lambda v, n: lax.dynamic_slice_in_dim(v, t * n, n, v.ndim - 1)
    gain_dev = own(gate_gain, inner)
    hidden = hidden_in.astype(F32)
    inv_rms = lax.rsqrt(jnp.mean(hidden * hidden, axis=1) + EPS)
    rows = proj_x.shape[0]
    cut = inner - 128
    w_owns = (
        proj_x[:, :cut],
        jnp.concatenate([proj_x[:, cut:], proj_bc, proj_dt, jnp.zeros((rows, 128 - heads), BF)], axis=1),
        proj_gate,
        proj_out.T,
    )
    seg = seg_ids.astype(F32)
    segc = jnp.broadcast_to(seg[:, None], (seg.shape[0], 128))
    segr = jnp.broadcast_to(seg[None, :], (8, seg.shape[0]))
    heads_row = lambda v: jnp.pad(own(v, heads), (0, 128 - heads))[None]
    skip_row = jnp.broadcast_to(own(skip_d, heads)[:, None], (heads, 64)).reshape(1, inner)
    cx = jnp.concatenate([own(conv_x, inner), own(conv_bias_x, inner)[None], skip_row, jnp.zeros((2, inner), F32)])
    cbc = jnp.concatenate([conv_bc, conv_bias_bc[None], jnp.zeros((3, 256), F32)])
    hp = jnp.concatenate([heads_row(dt_bias), -jnp.exp(heads_row(a_log)), jnp.zeros((6, 128), F32)])
    spread8 = lambda v: jnp.broadcast_to(v[None, :], (8, v.shape[0]))
    w0, w1, w_gate, w_out, normed_all, cot_all, vals, states, normed_out, low_gate, dy, gg = run_k1(
        hidden_in, cotangent, w_owns, spread8(pre_gain), segc, segr, cx, cbc, hp, spread8(gain_dev)
    )
    partial_out = dot_nt(normed_out, w_out).astype(BF)
    term_out = dot_tn(cot_all, normed_out)
    low_a, gx, gbc, gh = run_backward(inner, vals, segc, segr, cx, cbc, hp, dy, states)
    grad_normed = dot_nt(low_gate, w_gate) + dot_nt(low_a[:, :cut], w0) + dot_nt(low_a[:, cut:], w1)
    part_pre = jnp.sum(grad_normed * normed_all.astype(F32), axis=0) / pre_gain
    grad_normed = grad_normed.astype(BF)
    term_a = dot_tn(normed_all, low_a).astype(BF)
    term_b = jnp.concatenate([dot_tn(normed_all, low_gate), term_out], axis=1).astype(BF)
    small = jnp.concatenate([gx[:5].reshape(-1), gg[0], gx[5], part_pre, gbc[:5].reshape(-1), gh[:2].reshape(-1)])
    small = jnp.pad(small, (0, 9216 - small.shape[0])).reshape(72, 128)
    blocks = (4, 4, 2, rows)
    ra, rb, own_out, grad_own, smalls = reduce_all(
        inner, term_a.reshape(blocks + term_a.shape[1:]), term_b.reshape(blocks + term_b.shape[1:]),
        partial_out.reshape(4, 256, -1), grad_normed.reshape(4, 256, -1), small,
    )
    output = (hidden + own_out).astype(BF)
    scaled = grad_own * pre_gain[None, :]
    proj = jnp.mean(scaled * hidden, axis=1)
    grad_hidden = cotangent.astype(F32) + scaled * inv_rms[:, None] - hidden * (inv_rms * inv_rms * inv_rms * proj)[:, None]
    smalls = smalls.reshape(4, 9216)
    spread = lambda lo, n, k: smalls[:, lo : lo + n * k].reshape(4, k, n).transpose(1, 0, 2).reshape(k, 4 * n)
    x_sums = spread(0, inner, 7)
    at = 7 * inner
    width = pre_gain.shape[0]
    d_skip = x_sums[6].reshape(-1, 64).sum(axis=1)
    both = jnp.sum(smalls[:, at : at + width + 5 * 256], axis=0)
    d_pre = both[:width]
    bc_sums = both[width:]
    at = at + width + 5 * 256
    d_dt_bias, d_a_log = (spread(at + 128 * i, 128, 1)[0].reshape(4, 128)[:, :heads].reshape(-1) for i in range(2))
    return (
        output, grad_hidden, d_pre, rb[:, :inner], ra[:, :inner], ra[:, inner : inner + 256], ra[:, inner + 256 : inner + 256 + heads],
        x_sums[:4], x_sums[4], bc_sums[:1024].reshape(4, 256), bc_sums[1024:], d_dt_bias, d_a_log, d_skip, x_sums[5],
        rb[:, inner:].T,
    )


def solution(mesh):
    tok = P(("dp", "tensor"), None)
    mat = P("dp", "tensor")
    in_specs = (tok, P("dp"), P(), mat, mat, P("dp", None), mat) + (P(),) * 8 + (P("tensor", "dp"), tok)
    out_specs = (tok, tok, P(), mat, mat, P("dp", None), mat) + (P(),) * 8 + (P("tensor", "dp"),)
    return jax.shard_map(per_device, mesh=mesh, in_specs=in_specs, out_specs=out_specs, check_vma=False)
```

time: 752 us -> 278 us (0.37); the launches traced: 743 us -> 277 us
  local copies, waits for them, and re-layouts: 257 us -> 21.5 us
  matrix products: 160 us -> 30.4 us
  other arithmetic: 100 us -> 13.6 us
  blocking collectives: 85.7 us -> 0 us
  Pallas kernels: 125 us -> 210 us
  loops' own time: 12.9 us -> 0 us
    dynamic_update_slice x16 -> x0, local copies, waits for them, and re-layouts: 149 us -> none  [scan_ssd(): lax.scan(scan_body, initial, (x_heads.reshape(blocks, GROUP, head_count,...]
    dot_general x59 -> x0, matrix products: 127 us -> none  [the longest x12 58 us: block_step(): jnp.einsum('hts,shp->thp', mixing, x_block, precision=lax.Precision.HIGHEST)]
    psum x3 -> x0, blocking collectives: 85.7 us -> none  [the longest x1 64.2 us: per_device(): d_pre = lax.psum(part_pre, ('dp', 'tensor'))]
    pallas_call x2 -> x3, Pallas kernels: 125 us -> 210 us  [the longest x1 105 us: run_k1(): pl.pallas_call(functools.partial(forward_kernel, list(scan), nv), out_sha...]
    reduce_sum x15 -> x2, other arithmetic: 25.1 us -> 0.66 us  [the longest x1 0.63 us: per_device(): d_skip = x_sums[6].reshape(-1, 64).sum(axis=1)]
    mul x34 -> x0, other arithmetic: 21.8 us -> none  [the longest x16 6.03 us: block_step(): jnp.exp(log_decay[block_rows - 1]) * (last_seg == seg_before).astype(F32)]
    another operation x51 -> x0, other arithmetic: 18.1 us -> none
    dynamic_slice x20 -> x0, local copies, waits for them, and re-layouts: 15.6 us -> none  [scan_ssd(): lax.scan(scan_body, initial, (x_heads.reshape(blocks, GROUP, head_count,...]
where the time goes in v3:
time: 278 us; the launch traced here: 277 us
  Pallas kernels  210 us (76%)
  matrix products  30.4 us (11%)
  local copies, waits for them, and re-layouts  21.5 us (8%)
  other arithmetic  13.6 us (5%)
    pallas_call x1, Pallas kernels, run_k1(): pl.pallas_call(functools.partial(forward_kernel, list(scan), nv), out_sha...  105 us
    pallas_call x1, Pallas kernels, reduce_all(): pl.pallas_call(functools.partial(rs_kernel, bc0), out_shape=outs, in_spec...  65.5 us
    pallas_call x1, Pallas kernels, run_backward(): pl.pallas_call(kernel, out_shape=outs, in_specs=[vm] * 8, out_specs=[vm]...  40.2 us
    dot_general x4, matrix products, dot_nt(): lax.dot_general(left, right, (((1,), (1,)), ((), ())), preferred_element_...  18.7 us
    dot_general x3, matrix products, dot_tn(): lax.dot_general(left, right, (((0,), (0,)), ((), ())), preferred_element_...  11.7 us

profile of v3, /device:TPU:1, one launch (start us, length us, event | category | flops | bytes accessed | tf_op | source)
XLA Modules:
  0.0 276.8 jit_solution(1211966496083965009)
XLA Ops:
  0.6 0.0 copy-start
  0.7 0.7 dynamic_slice.21
  1.4 0.7 dynamic_slice.22
  2.1 0.1 pad.18.clone
  2.2 0.7 maximum_maximum_fusion.3.hp
  2.9 0.0 copy-done
  2.9 0.7 dynamic_slice.20
  3.6 0.1 broadcast_in_dim.29
  3.7 0.1 reshape.110
  3.8 0.8 dynamic_slice.19
  4.6 0.1 pad.25.clone
  4.6 0.7 maximum_maximum_fusion.1.cx
  5.3 0.8 dynamic_slice.23
  6.1 0.6 broadcast_in_dim.66.ggain
  6.7 0.7 convert_element_type.32
  7.4 1.0 broadcast_in_dim.26.segc
  8.4 0.6 broadcast_in_dim.27.segr
  9.0 0.1 pad.21.clone
  9.1 1.4 maximum_maximum_fusion.2.cbc
  10.5 0.8 copy.36
  11.2 0.7 slice.99
  12.0 0.1 pad.29.clone
  12.0 1.4 maximum_maximum_fusion.w_own1
  13.4 1.5 slice.98.w_own0
  14.9 1.3 broadcast_in_dim.25.pgain
  16.2 104.6 %forward_all.1 = (bf16[1536,640]{1,0:T(8,128)(2,1)}, bf16[1536,512]{1,0:T(8,128)(2,1)}, bf16[1536,768]{1,0:T(8,128)(2,1)}, bf16[1536,768]{1,0:T(8,128)(2,1)}, bf...) custom-call(bf16[256,1536]{1,0:T(8,128)(2,1)} %hid.1, ...), custom_call_target="tpu_custom_call" | custom-call | tf_op jit(solution)/shard_map/forward_all/pallas_call | solution.py:619
  120.8 40.2 %scan_backward.1 = (bf16[1024,1152]{1,0:T(8,128)(2,1)}, f32[8,768]{1,0:T(8,128)}, f32[8,256]{1,0:T(8,128)}, f32[8,128]{1,0:T(8,128)}) custom-call(f32[1024,1152]{1,0:T(8,128)} %get-tuple-element.38.vals, f32[1024,128]{1,0:T(8,128)} %broadcast_in_dim.26.segc, f32[8,1024]{1,0:T(8,128)} %broadcast_in_dim.27.segr, f32[8,768]{1,0:T(8,128)} %maximum_maximum_fusion.1.cx, ...), custom_call_target="tpu_custom_call" | custom-call | tf_op jit(solution)/shard_map/scan_backward/pallas_call | solution.py:441
  161.0 0.7 reshape.114
  161.7 0.8 slice_reduce_fusion.3
  162.5 0.8 slice_reduce_fusion.2
  163.3 0.0 copy-done.15
  163.3 0.0 copy-start.14
  163.3 0.0 copy-start.17
  163.3 4.1 %fusion.4 = f32[1024,1536]{1,0:T(8,128)S(1)} fusion(bf16[1536,640]{1,0:T(8,128)(2,1)S(1)} %copy-done.15, bf16[1024,1152]{1,0:T(8,128)(2,1)} %get-tuple-element.41), kind=kOutput, calls=%fused_computation.15 | convolution fusion | flops 2013265920 | bytes 9568256 | tf_op jit(solution)/shard_map/dot_general | solution.py:780
  167.4 2.6 fusion.10
  170.1 0.0 copy-done.4
  170.1 0.0 copy-start.11
  170.1 0.0 copy-start.12
  170.1 5.3 %multiply_reduce_fusion = (f32[1536]{0:T(1024)S(1)}, bf16[1024,1536]{1,0:T(8,128)(2,1)}) fusion(bf16[1024,1536]{1,0:T(8,128)(2,1)S(1)} %copy-done.4, bf16[1536,512]{1,0:T(8,128)(2,1)S(1)} %copy-done.6, bf16[1024,1152]{1,0:T(8,128)(2,1)} %get-tuple-element.41, f32[1024,1536]{1,0:T(8,128)S(1)} %fusion.10, f32[1024,1536]{1,0:T(8,128)S(1)} %fusion.4), kind=kOutput, calls=%fused_computation.1 | convolution fusion | flops 1620048384 | bytes 21501952 | tf_op jit(solution)/shard_map/dot_general | solution.py:780
  175.5 0.7 constant_dynamic-update-slice_fusion
  176.1 0.6 pad_bitcast_fusion.sv
  176.8 6.6 %convolution_convert_fusion.1 = bf16[1024,1536]{1,0:T(8,128)(2,1)} fusion(bf16[1024,768]{1,0:T(8,128)(2,1)} %get-tuple-element.44, bf16[1536,768]{1,0:T(8,128)(2,1)} %get-tuple-element.45), kind=kOutput, calls=%fused_computation.4 | convolution fusion | flops 2417491968 | bytes 7077888 | tf_op jit(solution)/shard_map/dot_general | solution.py:780
  183.4 3.0 %convolution_convert_fusion.3 = bf16[1536,768]{1,0:T(8,128)(2,1)S(1)} fusion(bf16[1024,1536]{1,0:T(8,128)(2,1)S(1)} %copy-done.4, bf16[1024,768]{1,0:T(8,128)(2,1)S(1)} %copy-done.18), kind=kOutput, calls=%fused_computation.6 | convolution fusion | flops 2417098752 | bytes 7077888 | tf_op jit(solution)/shard_map/dot_general | solution.py:784
  186.4 3.0 %convolution_convert_fusion.2 = bf16[1536,768]{1,0:T(8,128)(2,1)S(1)} fusion(bf16[1024,1536]{1,0:T(8,128)(2,1)S(1)} %copy-done.13, bf16[1024,768]{1,0:T(8,128)(2,1)S(1)} %copy-done.16), kind=kOutput, calls=%fused_computation.5 | convolution fusion | flops 2417098752 | bytes 7077888 | tf_op jit(solution)/shard_map/dot_general | solution.py:784
  189.4 2.8 %pad_maximum_fusion.gb = bf16[4,4,2,48,1536]{4,3,2,1,0:T(8,128)(2,1)} fusion(bf16[4,4,2,48,768]{4,3,2,1,0:T(8,128)(2,1)S(1)} %bitcast.43, bf16[4,4,2,48,768]{4,3,2,1,0:T(8,128)(2,1)S(1)} %bitcast.42), kind=kLoop, calls=%fused_computation.3 | loop fusion | flops 9437184 | bytes 9437184 | tf_op jit(solution)/shard_map/concatenate | solution.py:825
  192.2 5.8 %convolution_convert_fusion = bf16[1536,1152]{1,0:T(8,128)(2,1)} fusion(bf16[1024,1536]{1,0:T(8,128)(2,1)S(1)} %copy-done.4, bf16[1024,1152]{1,0:T(8,128)(2,1)S(1)} %copy-done.7), kind=kOutput, calls=%fused_computation | convolution fusion | flops 3625648128 | bytes 9043968 | tf_op jit(solution)/shard_map/dot_general | solution.py:784
  198.0 65.5 %reduce_all.1 = (f32[48,1152]{1,0:T(8,128)}, f32[48,1536]{1,0:T(8,128)}, f32[256,1536]{1,0:T(8,128)}, f32[256,1536]{1,0:T(8,128)}, f32[4,72,128]{2,1,0:T(8,128)}) custom-call(bf16[4,4,2,48,1152]{4,3,2,1,0:T(8,128)(2,1)} %bitcast.40, bf16[4,4,2,48,1536]{4,3,2,1,0:T(8,128)(2,1)} %pad_maximum_fusion.gb, bf16[4,256,1536]{2,1,0:T(8,128)(2,1)} %bitcast.41, ...), custom_call_target="tpu_custom_call" | custom-call | tf_op jit(solution)/shard_map/reduce_all/pallas_call | solution.py:775
  263.5 0.0 copy-start.5
  263.5 2.0 fusion.1
  265.5 0.1 copy-done.5
  265.6 3.4 %fusion.3 = (f32[256,1536]{1,0:T(8,128)}, bf16[256,1536]{1,0:T(8,128)(2,1)}) fusion(bf16[256,1536]{1,0:T(8,128)(2,1)S(1)} %copy-done.2, bf16[256,1536]{1,0:T(8,128)(2,1)S(1)} %copy-done.5, f32[256,1536]{1,0:T(8,128)S(1)} %copy-done.3, f32[256]{0:T(256)S(1)} %get-tuple-element.104, f32[256]{0:T(256)S(1)} %get-tuple-element.103, f32[1536]{0:T(1024)S(1)} %copy-done.11, ...), kind=kLoop, calls=%fused_computation.14 | loop fusion | flops 3538944 | bytes 7086080 | tf_op jit(solution)/shard_map/sub | solution.py:836
  269.1 0.6 fusion.9
  269.8 0.1 reshape_squeeze.3
  269.8 0.6 reduce_sum.49
  270.5 0.6 slice.128
  271.1 0.7 slice_bitcast_fusion
  271.9 0.6 slice.118
  272.5 0.6 slice.126
  273.1 0.6 slice.131
  273.6 0.6 reshape.120
  274.2 0.6 reshape.121
  274.8 0.7 slice.110
  275.5 0.6 slice.111
  276.1 0.7 copy.37
  (50 shorter events, 0.3 us)
Async XLA Ops:
  0.6 2.2 copy-start
  120.8 42.5 %copy-start.15 = (bf16[1536,640]{1,0:T(8,128)(2,1)S(1)}, bf16[1536,640]{1,0:T(8,128)(2,1)}, u32[]{:S(2)}) copy-start(bf16[1536,640]{1,0:T(8,128)(2,1)} %get-tuple-element.47) | copy-start | bytes 5898244
  163.3 4.1 %copy-start.14 = (bf16[1536,768]{1,0:T(8,128)(2,1)S(1)}, bf16[1536,768]{1,0:T(8,128)(2,1)}, u32[]{:S(2)}) copy-start(bf16[1536,768]{1,0:T(8,128)(2,1)} %get-tuple-element.46) | copy-start | bytes 7077892
  163.3 4.1 %copy-start.17 = (bf16[1024,768]{1,0:T(8,128)(2,1)S(1)}, bf16[1024,768]{1,0:T(8,128)(2,1)}, u32[]{:S(2)}) copy-start(bf16[1024,768]{1,0:T(8,128)(2,1)} %get-tuple-element.42) | copy-start | bytes 4718596
  167.4 2.7 copy-start.4
  167.4 2.7 copy-start.6
  170.1 5.3 %copy-start.11 = (f32[1536]{0:T(1024)S(1)}, f32[1536]{0:T(1024)}, u32[]{:S(2)}) copy-start(f32[1536]{0:T(1024)} %param.19) | copy-start | bytes 18436
  170.1 5.3 %copy-start.12 = (f32[8,256]{1,0:T(8,128)S(1)}, f32[8,256]{1,0:T(8,128)}, u32[]{:S(2)}) copy-start(f32[8,256]{1,0:T(8,128)} %get-tuple-element.51) | copy-start | bytes 24580
  176.8 6.7 %copy-start.18 = (bf16[1024,768]{1,0:T(8,128)(2,1)S(1)}, bf16[1024,768]{1,0:T(8,128)(2,1)}, u32[]{:S(2)}) copy-start(bf16[1024,768]{1,0:T(8,128)(2,1)} %get-tuple-element.42) | copy-start | bytes 4718596
  183.4 3.0 %copy-start.13 = (bf16[1024,1536]{1,0:T(8,128)(2,1)S(1)}, bf16[1024,1536]{1,0:T(8,128)(2,1)}, u32[]{:S(2)}) copy-start(bf16[1024,1536]{1,0:T(8,128)(2,1)} %get-tuple-element.43) | copy-start | bytes 9437188
  183.4 3.0 %copy-start.16 = (bf16[1024,768]{1,0:T(8,128)(2,1)S(1)}, bf16[1024,768]{1,0:T(8,128)(2,1)}, u32[]{:S(2)}) copy-start(bf16[1024,768]{1,0:T(8,128)(2,1)} %get-tuple-element.44) | copy-start | bytes 4718596
  189.4 2.8 %copy-start.7 = (bf16[1024,1152]{1,0:T(8,128)(2,1)S(1)}, bf16[1024,1152]{1,0:T(8,128)(2,1)}, u32[]{:S(2)}) copy-start(bf16[1024,1152]{1,0:T(8,128)(2,1)} %get-tuple-element.41) | copy-start | bytes 7077892
  198.0 65.5 %copy-start.2 = (bf16[256,1536]{1,0:T(8,128)(2,1)S(1)}, bf16[256,1536]{1,0:T(8,128)(2,1)}, u32[]{:S(2)}) copy-start(bf16[256,1536]{1,0:T(8,128)(2,1)} %hid.1) | copy-start | bytes 2359300
  263.5 2.0 copy-start.3
  263.5 2.1 copy-start.5
  265.6 3.4 %copy-start.10 = (f32[4,72,128]{2,1,0:T(8,128)S(1)}, f32[4,72,128]{2,1,0:T(8,128)}, u32[]{:S(2)}) copy-start(f32[4,72,128]{2,1,0:T(8,128)} %get-tuple-element.55) | copy-start | bytes 442372
  265.6 5.5 %copy-start.8 = (f32[48,1536]{1,0:T(8,128)S(1)}, f32[48,1536]{1,0:T(8,128)}, u32[]{:S(2)}) copy-start(f32[48,1536]{1,0:T(8,128)} %get-tuple-element.56) | copy-start | bytes 884740
  265.6 9.3 %copy-start.9 = (f32[48,1152]{1,0:T(8,128)S(1)}, f32[48,1152]{1,0:T(8,128)}, u32[]{:S(2)}) copy-start(f32[48,1152]{1,0:T(8,128)} %get-tuple-element.57) | copy-start | bytes 663556
  265.6 11.2 %copy-start.1 = (f32[4,3072]{1,0:T(4,128)S(1)}, f32[4,3072]{1,0:T(4,128)}, u32[]{:S(2)}) copy-start(f32[4,3072]{1,0:T(4,128)} %param.24) | copy-start | bytes 147460

commit v4 on v3

--- a/solution.py
+++ b/solution.py
@@ -85,7 +85,7 @@
         return send(src, dst, self.send_sem.at[k], self.recv_sem.at[k], to)
 
     STEPS = (
-        ((), (0, 1, 2, 3, 4)),
+        ((), (1, 2, 3, 4)),
         ((0,), (5, 6, 7, 8)),
         ((1, 2, 5, 6), (9, 10, 11, 12, 13, 14)),
         ((9, 10), (15, 16)),
@@ -94,6 +94,9 @@
         ((15, 16), (23, 24)),
         ((17, 18, 19, 20, 21, 22, 23, 24), ()),
     )
+
+    def begin(self):
+        self.copy(0).start()
 
     def step(self, k):
         arrive, go = self.STEPS[k]
@@ -243,7 +246,7 @@
     def block(c, _):
         r0 = pl.multiple_of(c * Q, Q)
         match, *_r = block_setup(c, nv, vals, segc, segr, cbc, hp, s["bt"], s["b"], s["c"], None, s["qk"], s["bias"], s["cum"], s["cumt"], s["step"], s["tail"], s["keep"], s["ex"], s["ecum"])
-        states[c] = s["state"][...]
+        states[c] = s["state"][...].astype(BF)
 
         def pair(j, _):
             hook(c * (nv // 128) + j)
@@ -332,8 +335,7 @@
             dy = dy_ref[pl.ds(r0, Q), lanes].astype(F32)
             dyb = dy.astype(BF)
             dyt = dy.T.astype(BF)
-            st = states[c, :, lanes]
-            stb = st.astype(BF)
+            stb = states[c, :, lanes]
             dst = s["dstate"][:, lanes]
             dstb = dst.astype(BF)
             edy = s["ecum"][:, lanes] * dy
@@ -345,7 +347,7 @@
             s["dbs"][...] += dnt(tu.astype(BF), dstb)
             s["gs"][...] += to_head(tu * v, j)
             keep = s["keep"][0:1, lanes]
-            s["krow"][:, lanes] = jnp.broadcast_to(keep * jnp.sum(st * dst, axis=0, keepdims=True), (8, 128))
+            s["krow"][:, lanes] = jnp.broadcast_to(keep * jnp.sum(stb.astype(F32) * dst, axis=0, keepdims=True), (8, 128))
             s["dstate"][:, lanes] = keep * dst + dnn(s["ct"][...], edyb)
             lane = ii((Q, 128), 1)
             parts = []
@@ -450,7 +452,10 @@
 
 def at_step(step, events):
     for k, fn in events:
-        pl.when(step == k)(fn)
+
+        @pl.when(step == k)
+        def _(fn=fn):
+            fn()
 
 
 def forward_kernel(
@@ -487,6 +492,8 @@
             send(dst.at[theirs], dst.at[theirs], tsend.at[i, 2], trecv.at[i, 2], tp[0]),
         )
 
+    for g in groups((0, 1, 2, 3)):
+        g.begin()
     step(first, 0)
 
     def norm_rows(i, _):
@@ -505,21 +512,23 @@
     cot_copies = tensor_copies(1, cot_own, cot)
     nrm_copies[0].start()
     nrm_copies[1].start()
-    for n in (1, 2, 3):
+    for n in (1, 4, 2, 3):
         step(first, n)
-    nrm_copies[0].wait_recv()
-    nrm_copies[2].start()
     cot_copies[0].start()
     cot_copies[1].start()
     step(second, 0)
-    for n in (4, 5, 6):
-        step(first, n)
     step(second, 1)
+    step(first, 5)
+    step(first, 6)
+    nrm_copies[0].wait_recv()
+    nrm_copies[2].start()
+    step(second, 4)
     step(first, 7)
     nrm_copies[1].wait_recv()
     nrm_copies[2].wait_recv()
 
     def project(i, _):
+        pl.when(i == 2)(lambda: step(second, 2))
         rows = pl.ds(pl.multiple_of(i * 256, 256), 256)
         n = nrm[rows]
         at = 0
@@ -538,7 +547,7 @@
         cot_copies[0].wait_recv()
         cot_copies[2].start()
 
-    events = [(0, lambda: step(second, 2)), (4, lambda: step(second, 3)), (8, lambda: step(second, 4)), (14, cot_forward), (16, lambda: step(second, 5)), (20, lambda: step(second, 6))]
+    events = [(1, lambda: step(second, 3)), (6, lambda: step(second, 5)), (10, lambda: step(second, 6)), (14, cot_forward)]
     ssd_forward(nv, vals, segc, segr, cx, cbc, hp, ssd, states, s, lambda at: at_step(at, events))
     step(second, 7)
     cot_copies[1].wait_recv()
@@ -609,11 +618,11 @@
     sh = jax.ShapeDtypeStruct
     cols = [w.shape[1] for w in w_owns]
     nvals = cols[0] + cols[1]
-    outs = [sh((d, c), BF) for c in cols] + [sh((rows, d), BF)] * 2 + [sh((rows, nvals), F32), sh((rows // Q, 128, nv), F32)] + [sh((rows, nv), BF)] * 3 + [sh((8, nv), F32)]
+    outs = [sh((d, c), BF) for c in cols] + [sh((rows, d), BF)] * 2 + [sh((rows, nvals), F32), sh((rows // Q, 128, nv), BF)] + [sh((rows, nv), BF)] * 3 + [sh((8, nv), F32)]
     V = lambda shape, dt: pltpu.VMEM(shape, dt)
     D = pltpu.SemaphoreType.DMA
     scan = fwd_scratch(nv)
-    scratch = [V((d, c), BF) for c in cols] + [V((rows, d), BF)] * 2 + [V((rows, nvals), F32), V((rows // Q, 128, nv), F32)] + [V((rows, nv), F32)] * 3 + [V((rows, nv), BF)] * 3
+    scratch = [V((d, c), BF) for c in cols] + [V((rows, d), BF)] * 2 + [V((rows, nvals), F32), V((rows // Q, 128, nv), BF)] + [V((rows, nv), F32)] * 3 + [V((rows, nv), BF)] * 3
     scratch += [V((8, rows), F32), V((3, 8, rows), F32), D((4, Gather.N)), D((4, Gather.N)), D((2, 3)), D((2, 3)), D((3,)), D((3,)), D((11,))]
     scratch += list(scan.values())
     return pl.pallas_call(
@@ -622,158 +631,311 @@
     )(hid, cot_own, *w_owns, pgain, segc, segr, cx, cbc, hp, ggain)
 
 
-def rs_kernel(bc0, ga, gb, po, pn, sv, oa, ob, oo, on, osv,
-              va, vb, vo, vn, r1a, r1b, r2a, r2b, ha, hb, q1a, q1b, q2a, q2b, ka, kb, ya, yb,
-              co_buf, cy_buf, cs_buf, sacc, sx, sz, sy, st, bct,
-              lsem, wsend, wrecv, tsend, trecv, ssend, srecv, bsend, brecv):
+class Scatter:
+    N = 13
+
+    def __init__(self, v, bufs, out, a1, send_sem, recv_sem):
+        x, z, yh, t = place()
+        self.v, self.out, self.a1, self.yh = v, out, a1, yh
+        self.r1, self.r2, self.q1, self.q2, self.kk, self.yy = bufs
+        self.h = self.r2.at[0]
+        a2 = "z" if a1 == "x" else "x"
+        self.p, self.q = (x, z) if a1 == "x" else (z, x)
+        self.send_sem, self.recv_sem = send_sem, recv_sem
+        right1, left1, right2, left2 = neighbour(a1, 1), neighbour(a1, -1), neighbour(a2, 1), neighbour(a2, -1)
+        r1, r2, h, q1, q2, q = self.r1, self.r2, self.h, self.q1, self.q2, self.q
+        self.plan = [
+            (self.half(2, 0), r1.at[0], right1), (self.half(2, 1), r1.at[1], left1),
+            (self.half(1, 1), r2.at[0, pl.ds(2, 2)], right1), (self.half(-1, 0), r2.at[1, pl.ds(0, 2)], left1),
+            (self.half(1, 0), r2.at[0, pl.ds(0, 2)], right1), (self.half(-1, 1), r2.at[1, pl.ds(2, 2)], left1),
+            (h.at[m4(q + 2), 0], q1.at[0], right2), (h.at[m4(q + 2), 1], q1.at[1], left2),
+            (h.at[m4(q + 1), 1], q2.at[0, 1], right2), (h.at[m4(q - 1), 0], q2.at[1, 0], left2),
+            (h.at[m4(q + 1), 0], q2.at[0, 0], right2), (h.at[m4(q - 1), 1], q2.at[1, 1], left2),
+            (self.kk, self.yy, dev(x, z, 1 - yh, t)),
+        ]
+
+    def half(self, d, k):
+        at = m4(self.p + d)
+        return self.v.at[pl.ds(2 * k, 2), at] if self.a1 == "z" else self.v.at[at, pl.ds(2 * k, 2)]
+
+    def copy(self, k):
+        src, dst, to = self.plan[k]
+        return send(src, dst, self.send_sem.at[k], self.recv_sem.at[k], to)
+
+    def start(self, *ks):
+        for k in ks:
+            self.copy(k).start()
+
+    def arrive(self, *ks):
+        for k in ks:
+            self.copy(k).wait_recv()
+
+    def step(self, n):
+        v, r1, r2, h, q1, q2, p, q, yh = self.v, self.r1, self.r2, self.h, self.q1, self.q2, self.p, self.q, self.yh
+        if n == 0:
+            self.start(0, 1, 2, 3)
+        elif n == 1:
+            for side, d in ((0, 1), (1, -1)):
+                self.arrive(side)
+                at = m4(p + d)
+
+                def add(j, _, side=side, at=at):
+                    e, y = j // 2, j % 2
+                    ix = (2 * side + e, at, y) if self.a1 == "z" else (at, 2 * side + e, y)
+                    v[ix] = (v[ix].astype(F32) + r1[side, e, y].astype(F32)).astype(BF)
+                    return 0
+
+                lax.fori_loop(0, 4, add, 0)
+                self.start(4 + side)
+        elif n == 2:
+            self.arrive(2, 3, 4, 5)
+
+            def add(j, _):
+                e, y = j // 2, j % 2
+                own = v[e, p, y] if self.a1 == "z" else v[p, e, y]
+                h[e, y] = (own.astype(F32) + r2[0, e, y].astype(F32) + r2[1, e, y].astype(F32)).astype(BF)
+                return 0
+
+            lax.fori_loop(0, 8, add, 0)
+            self.start(6, 7, 8, 9)
+        elif n == 3:
+            for side, d in ((0, 1), (1, -1)):
+                self.arrive(6 + side)
+                at = m4(q + d)
+                h[at, side] = (h[at, side].astype(F32) + q1[side].astype(F32)).astype(BF)
+                self.start(10 + side)
+        elif n == 4:
+            self.arrive(8, 9, 10, 11)
+            self.kk[...] = (h[q, 1 - yh].astype(F32) + q2[0, 1 - yh].astype(F32) + q2[1, 1 - yh].astype(F32)).astype(BF)
+            self.start(12)
+        else:
+            self.arrive(12)
+            self.out[...] = h[q, yh].astype(F32) + q2[0, yh].astype(F32) + q2[1, yh].astype(F32) + self.yy[...].astype(F32)
+
+    def finish(self):
+        for k in range(self.N):
+            self.copy(k).wait_send()
+
+
+class TokenScatter:
+    def __init__(self, v, from_core, from_chip, out, send_sem, recv_sem):
+        t = place()[3]
+        tp, slots = tensor_peers()
+        self.t, self.v, self.from_core, self.from_chip, self.out = t, v, from_core, from_chip, out
+        rows = lambda s: pl.ds(pl.multiple_of(s * 256, 256), 256)
+        self.pass_on, self.mine = slots[1], rows(t)
+        self.copies = lambda k: (
+            lambda: send(v.at[rows(slots[2])], from_core.at[0], send_sem.at[0], recv_sem.at[0], tp[0]),
+            lambda: send(v.at[rows(slots[0])], from_core.at[1], send_sem.at[1], recv_sem.at[1], tp[0]),
+            lambda: send(v.at[rows(slots[1])], from_chip, send_sem.at[2], recv_sem.at[2], tp[1]),
+        )[k]()
+
+    def step(self, n):
+        if n == 0:
+            self.copies(0).start()
+            self.copies(1).start()
+        elif n == 1:
+            self.copies(0).wait_recv()
+
+            def add(j, _):
+                rows = pl.ds(pl.multiple_of(j * 32, 32), 32)
+                own = pl.ds(pl.multiple_of(self.pass_on * 256 + j * 32, 32), 32)
+                self.v[own] = (self.v[own].astype(F32) + self.from_core[0, rows].astype(F32)).astype(BF)
+                return 0
+
+            lax.fori_loop(0, 8, add, 0)
+            self.copies(2).start()
+        else:
+            self.copies(1).wait_recv()
+            self.copies(2).wait_recv()
+
+            def add(j, _):
+                rows = pl.ds(pl.multiple_of(j * 32, 32), 32)
+                own = self.v[pl.ds(pl.multiple_of(self.t * 256 + j * 32, 32), 32)]
+                self.out[rows] = own.astype(F32) + self.from_core[1, rows].astype(F32) + self.from_chip[rows].astype(F32)
+                return 0
+
+            lax.fori_loop(0, 8, add, 0)
+
+    def finish(self):
+        for k in range(3):
+            self.copies(k).wait_send()
+
+
+def backward_kernel(
+    names, nv,
+    h_w0, h_w1, h_w2, h_w3, h_nrm, h_cot, h_vals, h_states, h_no, h_lg, h_dy, pgain, segc, segr, cx, cbc, hp, gg,
+    o_gate, o_out, o_x0, o_x1, o_bc, o_own, o_grad, o_small,
+    w0, w1, w23, nrm, cot, vals, states, nody, lg, low, po, t_gate, t_out, t_x0, t_x1,
+    own_v, sx, sz, sy, st, sacc, bct, fc0, ch0, fc1, ch1, gx, gbc, gh, pre,
+    wsend, wrecv, tsend, trecv, ssend, srecv, bsend, brecv, lsem, *rest,
+):
+    bufs, s = [rest[6 * k : 6 * k + 6] for k in range(4)], dict(zip(names, rest[24:]))
     x, z, yh, t = place()
-    yl = t // 2; co = t % 2
-    m4 = lambda v: (v + 8) % 4
-    def nb(axis, d):
-        if axis == "x": return dev(m4(x + d), z, yh, t)
-        return dev(x, m4(z + d), yh, t)
-    ypeer = dev(x, z, 1 - yh, t)
-    tcore = dev(x, z, yh, yl * 2 + (1 - co))
-    tyl = dev(x, z, yh, (1 - yl) * 2 + co)
-    tdiag = dev(x, z, yh, (1 - yl) * 2 + 1 - co)
-    bar = pltpu.get_barrier_semaphore()
-    peers = [ypeer, tcore, tyl, tdiag] + [nb(a, d) for a in "xz" for d in (1, 2, 3)]
-    for p in peers:
-        pl.semaphore_signal(bar, inc=1, device_id=p, device_id_type=MESH)
-    loads = []
-    for i, (s, d) in enumerate(((ga, va), (gb, vb), (po, vo), (pn, vn))):
-        cp = pltpu.make_async_copy(s, d, lsem.at[i]); cp.start(); loads.append(cp)
-    pl.semaphore_wait(bar, len(peers))
-    sends = []
-    def rc(src, dst, ss, rs, to):
-        cp = pltpu.make_async_remote_copy(src_ref=src, dst_ref=dst, send_sem=ss, recv_sem=rs, device_id=to, device_id_type=MESH)
-        cp.start(); sends.append(cp); return cp
-    pos = {"x": x, "z": z}
-    halves = ((va, "z", "x", r1a, r2a, ha, q1a, q2a, ka, ya, oa), (vb, "x", "z", r1b, r2b, hb, q1b, q2b, kb, yb, ob))
-    def b1(v, a1, d, k=None):
-        p = m4(pos[a1] + d)
-        if a1 == "z": return v.at[:, p] if k is None else v.at[pl.ds(2 * k, 2), p]
-        return v.at[p] if k is None else v.at[p, pl.ds(2 * k, 2)]
-    small = []
-    for d in (1, 2, 3):
-        small.append(rc(sv, sx.at[d - 1], ssend.at[d - 1], srecv.at[d - 1], nb("x", d)))
-    for l in loads[:2]: l.wait()
-    s1 = []
-    for i, (v, a1, a2, r1, r2, *_) in enumerate(halves):
-        s1.append((rc(b1(v, a1, 2, 0), r1.at[0], wsend.at[i, 0], wrecv.at[i, 0], nb(a1, 1)),
-                   rc(b1(v, a1, 2, 1), r1.at[1], wsend.at[i, 1], wrecv.at[i, 1], nb(a1, -1))))
-    s1b = []
-    for i, (v, a1, a2, r1, r2, *_) in enumerate(halves):
-        s1b.append((rc(b1(v, a1, 1, 1), r2.at[0, pl.ds(2, 2)], wsend.at[i, 2], wrecv.at[i, 2], nb(a1, 1)),
-                    rc(b1(v, a1, -1, 0), r2.at[1, pl.ds(0, 2)], wsend.at[i, 3], wrecv.at[i, 3], nb(a1, -1))))
-    tr = []
-    for l in loads[2:]: l.wait()
-    for i, v in enumerate((vo, vn)):
-        a = rc(v.at[(1 - yl) * 2 + 1 - co], co_buf.at[i, 0], tsend.at[i, 0], trecv.at[i, 0], tcore)
-        b = rc(v.at[yl * 2 + 1 - co], co_buf.at[i, 1], tsend.at[i, 1], trecv.at[i, 1], tcore)
-        tr.append((a, b))
-    for i, v in enumerate((vo, vn)):
-        tr[i][0].wait_recv()
-        def addc(j, _, i=i, v=v):
-            rows = pl.ds(pl.multiple_of(j * 32, 32), 32)
-            cs_buf[i, rows] = (v[(1 - yl) * 2 + co, rows].astype(F32) + co_buf[i, 0, rows].astype(F32)).astype(BF)
+    tp, slots = tensor_peers()
+    loads = [
+        pltpu.make_async_copy(a, b, lsem.at[k])
+        for k, (a, b) in enumerate(((h_no, nody), (h_w3, w23), (h_cot, cot), (h_nrm, nrm), (h_lg, lg), (h_vals, vals), (h_states, states), (h_w0, w0), (h_w1, w1)))
+    ]
+    for c in loads:
+        c.start()
+    load_dy, load_w2 = pltpu.make_async_copy(h_dy, nody, lsem.at[9]), pltpu.make_async_copy(h_w2, w23, lsem.at[10])
+    greet([dev(x, z, 1 - yh, t)] + [neighbour(a, d) for a in "xz" for d in (1, 2, 3)] + tp)
+    scat = [
+        Scatter(v, bufs[k], o, a1, wsend.at[k], wrecv.at[k])
+        for k, (v, o, a1) in enumerate(((t_out, o_out, "x"), (t_gate, o_gate, "z"), (t_x0, o_x0, "x"), (t_x1, o_x1, "z")))
+    ]
+    s_out, s_gate, s_x0, s_x1 = scat
+    k_out = TokenScatter(po, fc0, ch0, o_own, tsend.at[0], trecv.at[0])
+    k_nrm = TokenScatter(cot, fc1, ch1, o_grad, tsend.at[1], trecv.at[1])
+
+    def by_rows(fn):
+        def body(i, _):
+            fn(pl.ds(pl.multiple_of(i * 256, 256), 256))
             return 0
-        lax.fori_loop(0, 8, addc, 0)
-        tr[i] = tr[i] + (rc(cs_buf.at[i], cy_buf.at[i], tsend.at[i, 2], trecv.at[i, 2], tyl),)
-    for s in small: s.wait_recv()
-    sacc[0] = sv[...] + sx[0] + sx[1] + sx[2]
-    small = [rc(sacc.at[0], sz.at[d - 1], ssend.at[2 + d], srecv.at[2 + d], nb("z", d)) for d in (1, 2, 3)]
-    s1c = []
-    for i, (v, a1, a2, r1, r2, *_) in enumerate(halves):
-        for side, dd, k in ((0, 1, 0), (1, -1, 1)):
-            s1[i][side].wait_recv()
-            p = m4(pos[a1] + dd)
-            def add1(j, _, v=v, a1=a1, r1=r1, side=side, p=p, k=k):
-                e = j // 2 ; y = j % 2
-                if a1 == "z":
-                    v[2 * k + e, p, y] = (v[2 * k + e, p, y].astype(F32) + r1[side, e, y].astype(F32)).astype(BF)
-                else:
-                    v[p, 2 * k + e, y] = (v[p, 2 * k + e, y].astype(F32) + r1[side, e, y].astype(F32)).astype(BF)
-                return 0
-            lax.fori_loop(0, 4, add1, 0)
-            s1c.append(rc(b1(v, a1, dd, k), r2.at[side, pl.ds(2 * k, 2)], wsend.at[i, 4 + side], wrecv.at[i, 4 + side], nb(a1, dd)))
-    for s in small: s.wait_recv()
-    sacc[1] = sacc[0] + sz[0] + sz[1] + sz[2]
-    small = [rc(sacc.at[1], sy, ssend.at[6], srecv.at[6], ypeer)]
-    s2 = []
-    for i, (v, a1, a2, r1, r2, h, q1, q2, kk, yy, oo_) in enumerate(halves):
-        s1b[i][0].wait_recv(); s1b[i][1].wait_recv()
-        s1c[2 * i].wait_recv(); s1c[2 * i + 1].wait_recv()
-        p = pos[a1]
-        def add2(j, _, v=v, a1=a1, r2=r2, h=h, p=p):
-            e = j // 2; y = j % 2
-            own = v[e, p, y] if a1 == "z" else v[p, e, y]
-            h[e, y] = (own.astype(F32) + r2[0, e, y].astype(F32) + r2[1, e, y].astype(F32)).astype(BF)
+
+        lax.fori_loop(0, 4, body, 0)
+
+    def outer_product(dst, left, right):
+        def body(i, _):
+            cols = pl.ds(pl.multiple_of(i * 384, 384), 384)
+            r = lax.dot_general(left[:, cols], right[...], (((0,), (0,)), ((), ())), preferred_element_type=F32)
+            dst[i] = r.astype(BF).reshape(dst.shape[1:])
             return 0
-        lax.fori_loop(0, 8, add2, 0)
-        q = pos[a2]
-        s2.append((rc(h.at[m4(q + 2), 0], q1.at[0], wsend.at[i, 6], wrecv.at[i, 6], nb(a2, 1)),
-                   rc(h.at[m4(q + 2), 1], q1.at[1], wsend.at[i, 7], wrecv.at[i, 7], nb(a2, -1)),
-                   rc(h.at[m4(q + 1), 1], q2.at[0, 1], wsend.at[i, 8], wrecv.at[i, 8], nb(a2, 1)),
-                   rc(h.at[m4(q - 1), 0], q2.at[1, 0], wsend.at[i, 9], wrecv.at[i, 9], nb(a2, -1))))
-    for s in small: s.wait_recv()
-    sacc[2] = sacc[1] + sy[...]
-    small = [rc(sacc.at[2], st.at[j], ssend.at[7 + j], srecv.at[7 + j], d_) for j, d_ in enumerate((tcore, tyl, tdiag))]
-    s2c = []
-    for i, (v, a1, a2, r1, r2, h, q1, q2, kk, yy, oo_) in enumerate(halves):
-        q = pos[a2]
-        for side, dd in ((0, 1), (1, -1)):
-            s2[i][side].wait_recv()
-            pp = m4(q + dd)
-            h[pp, side] = (h[pp, side].astype(F32) + q1[side].astype(F32)).astype(BF)
-            s2c.append(rc(h.at[pp, side], q2.at[side, side], wsend.at[i, 10 + side], wrecv.at[i, 10 + side], nb(a2, dd)))
-    s3 = []
-    for i, (v, a1, a2, r1, r2, h, q1, q2, kk, yy, oo_) in enumerate(halves):
-        q = pos[a2]
-        s2[i][2].wait_recv(); s2[i][3].wait_recv()
-        s2c[2 * i].wait_recv(); s2c[2 * i + 1].wait_recv()
-        kk[...] = (h[q, 1 - yh].astype(F32) + q2[0, 1 - yh].astype(F32) + q2[1, 1 - yh].astype(F32)).astype(BF)
-        s3.append(rc(kk, yy, wsend.at[i, 12], wrecv.at[i, 12], ypeer))
-    for i, (v, o) in enumerate(((vo, oo), (vn, on))):
-        tr[i][1].wait_recv(); tr[i][2].wait_recv()
-        def addf(j, _, i=i, v=v, o=o):
-            rows = pl.ds(pl.multiple_of(j * 32, 32), 32)
-            o[rows] = v[t, rows].astype(F32) + co_buf[i, 1, rows].astype(F32) + cy_buf[i, rows].astype(F32)
-            return 0
-        lax.fori_loop(0, 8, addf, 0)
-    tens = []
-    for i, (v, a1, a2, r1, r2, h, q1, q2, kk, yy, o) in enumerate(halves):
-        q = pos[a2]
-        s3[i].wait_recv()
-        o[...] = h[q, yh].astype(F32) + q2[0, yh].astype(F32) + q2[1, yh].astype(F32) + yy[...].astype(F32)
-        if i == 0:
-            bct[3] = o[:, bc0 : bc0 + 256]
-            tens = [rc(bct.at[3], bct.at[j], bsend.at[j], brecv.at[j], d_) for j, d_ in enumerate((tcore, tyl, tdiag))]
-    for cp in tens: cp.wait_recv()
-    oa[:, bc0 : bc0 + 256] = bct[3] + bct[0] + bct[1] + bct[2]
-    for s in small: s.wait_recv()
-    osv[t] = sacc[2]
-    osv[yl * 2 + 1 - co] = st[0]
-    osv[(1 - yl) * 2 + co] = st[1]
-    osv[(1 - yl) * 2 + 1 - co] = st[2]
-    for cp in sends: cp.wait_send()
-
-def reduce_all(bc0, ga, gb, po, pn, sv):
-    anys = pl.BlockSpec(memory_space=pl.ANY); vm = pl.BlockSpec(memory_space=pltpu.VMEM)
-    ca, cb = ga.shape[-1], gb.shape[-1]; R = sv.shape[0]
-    outs = (jax.ShapeDtypeStruct((48, ca), F32), jax.ShapeDtypeStruct((48, cb), F32), jax.ShapeDtypeStruct((256, 1536), F32),
-            jax.ShapeDtypeStruct((256, 1536), F32), jax.ShapeDtypeStruct((4, R, 128), F32))
+
+        lax.fori_loop(0, 4, body, 0)
+
+    for k in (0, 1):
+        loads[k].wait()
+
+    def out_rows(rows):
+        left = nody[rows]
+        for k in range(0, po.shape[1], 512):
+            po[rows, k : k + 512] = dnt(left, w23[k : k + 512]).astype(BF)
+
+    by_rows(out_rows)
+    load_w2.start()
+    k_out.step(0)
+    loads[2].wait()
+    outer_product(t_out, cot, nody)
+    load_dy.start()
+    s_out.step(0)
+    k_out.step(1)
+    loads[3].wait()
+    loads[4].wait()
+    outer_product(t_gate, nrm, lg)
+    s_gate.step(0)
+    for k in (5, 6, 7, 8):
+        loads[k].wait()
+    load_dy.wait()
+    both = lambda n: lambda: (s_out.step(n), s_gate.step(n))
+    events = [(6, both(1)), (12, both(2)), (16, both(3)), (18, both(4)), (20, both(5)), (22, lambda: k_out.step(2))]
+    ssd_backward(nv, vals, segc, segr, cx, cbc, hp, nody, states, low, gx, gbc, gh, s, lambda at: at_step(at, events))
+    load_w2.wait()
+    pre[...] = jnp.zeros_like(pre)
+    c0 = w0.shape[1]
+
+    def grad_rows(rows):
+        for k in range(0, cot.shape[1], 512):
+            cols = slice(k, k + 512)
+            g = dnt(lg[rows], w23[cols]) + dnt(low[rows, :c0], w0[cols]) + dnt(low[rows, c0:], w1[cols])
+            pre[0:1, cols] += jnp.sum(g * nrm[rows, cols].astype(F32), axis=0, keepdims=True)
+            cot[rows, cols] = g.astype(BF)
+
+    by_rows(grad_rows)
+    k_nrm.step(0)
+    outer_product(t_x0, nrm, low.at[:, :c0])
+    s_x0.step(0)
+    k_nrm.step(1)
+    own_v[...] = jnp.zeros_like(own_v)
+    own_v[0:6] = gx[0:6]
+    own_v[6:7] = gg[0:1]
+    pv = pre[0:1] / pgain[0:1]
+    own_v[7:8], own_v[8:9] = pv[:, :nv], pv[:, nv:]
+    for k in range(3):
+        own_v[9:10, k * 256 : k * 256 + 256] = gbc[k : k + 1]
+    for k in range(2):
+        own_v[10:11, k * 256 : k * 256 + 256] = gbc[3 + k : 4 + k]
+        own_v[11:12, k * 128 : k * 128 + 128] = gh[k : k + 1]
+    small = [send(own_v, sx.at[d - 1], ssend.at[d - 1], srecv.at[d - 1], neighbour("x", d)) for d in (1, 2, 3)]
+    for c in small:
+        c.start()
+    outer_product(t_x1, nrm, low.at[:, c0:])
+    s_x1.step(0)
+    last = lambda n: (s_x0.step(n), s_x1.step(n))
+
+    def next_small(have, total, copies):
+        for c in have:
+            c.wait_recv()
+        total()
+        for c in copies:
+            c.start()
+        return copies
+
+    def total_x():
+        sacc[0] = own_v[...] + sx[0] + sx[1] + sx[2]
+
+    def total_z():
+        sacc[1] = sacc[0] + sz[0] + sz[1] + sz[2]
+
+    def total_y():
+        sacc[2] = sacc[1] + sy[...]
+
+    small_z = next_small(small, total_x, [send(sacc.at[0], sz.at[d - 1], ssend.at[2 + d], srecv.at[2 + d], neighbour("z", d)) for d in (1, 2, 3)])
+    last(1)
+    small_y = next_small(small_z, total_z, [send(sacc.at[1], sy, ssend.at[6], srecv.at[6], dev(x, z, 1 - yh, t))])
+    last(2)
+    small_t = next_small(small_y, total_y, [send(sacc.at[2], st.at[k], ssend.at[7 + k], srecv.at[7 + k], p) for k, p in enumerate(tp)])
+    k_nrm.step(2)
+    last(3)
+    last(4)
+    s_x1.step(5)
+    bc0 = o_x1.shape[1] - 384
+    bct[3] = o_x1[:, bc0 : bc0 + 256]
+    bcs = [send(bct.at[3], bct.at[k], bsend.at[k], brecv.at[k], p) for k, p in enumerate(tp)]
+    for c in bcs:
+        c.start()
+    s_x0.step(5)
+    for c in small_t:
+        c.wait_recv()
+    o_small[t] = sacc[2]
+    for k in range(3):
+        o_small[slots[k]] = st[k]
+    for c in bcs:
+        c.wait_recv()
+    o_bc[...] = bct[3] + bct[0] + bct[1] + bct[2]
+    for c in small + small_z + small_y + small_t + bcs:
+        c.wait_send()
+    for g in scat + [k_out, k_nrm]:
+        g.finish()
+
+
+def run_k2(ws, nrm, cot, vals, states, no, lg, dy, pgain, segc, segr, cx, cbc, hp, gg):
+    anys, vm = pl.BlockSpec(memory_space=pl.ANY), pl.BlockSpec(memory_space=pltpu.VMEM)
+    nv = cx.shape[1]
+    rows, d = nrm.shape
+    sh = lambda *s: jax.ShapeDtypeStruct(s, F32)
+    cols = [w.shape[1] for w in ws]
+    n = d // 32
+    V = lambda *s, dt=BF: pltpu.VMEM(s, dt)
     D = pltpu.SemaphoreType.DMA
-    V = lambda *s, d=BF: pltpu.VMEM(s, d)
-    scratch = [V(4, 4, 2, 48, ca), V(4, 4, 2, 48, cb), V(4, 256, 1536), V(4, 256, 1536),
-               V(2, 2, 2, 48, ca), V(2, 2, 2, 48, cb), V(2, 4, 2, 48, ca), V(2, 4, 2, 48, cb),
-               V(4, 2, 48, ca), V(4, 2, 48, cb), V(2, 48, ca), V(2, 48, cb), V(2, 2, 48, ca), V(2, 2, 48, cb),
-               V(48, ca), V(48, cb), V(48, ca), V(48, cb),
-               V(2, 2, 256, 1536), V(2, 256, 1536), V(2, 256, 1536),
-               V(3, R, 128, d=F32), V(3, R, 128, d=F32), V(3, R, 128, d=F32), V(R, 128, d=F32), V(3, R, 128, d=F32), V(4, 48, 256, d=F32),
-               D((4,)), D((2, 13)), D((2, 13)), D((2, 3)), D((2, 3)), D((10,)), D((10,)), D((3,)), D((3,))]
-    return pl.pallas_call(functools.partial(rs_kernel, bc0), out_shape=outs, in_specs=[anys] * 4 + [vm], out_specs=[vm] * 5, scratch_shapes=scratch,
-        compiler_params=pltpu.CompilerParams(collective_id=1, has_side_effects=True, vmem_limit_bytes=60 * 2**20), name="reduce_all")(ga, gb, po, pn, sv)
+    outs = [sh(n, cols[2]), sh(n, cols[3]), sh(n, cols[0]), sh(n, cols[1]), sh(n, 256), sh(256, d), sh(256, d), sh(4, 16, nv)]
+    term = lambda c: V(4, 4, 2, n, c)
+    scratch = [V(d, cols[0]), V(d, cols[1]), V(d, cols[2]), V(rows, d), V(rows, d), V(*vals.shape, dt=F32), V(*states.shape), V(rows, nv), V(rows, nv), V(*vals.shape), V(rows, d)]
+    scratch += [term(cols[2]), term(cols[3]), term(cols[0]), term(cols[1])]
+    sv = (16, nv)
+    scratch += [V(*sv, dt=F32), V(3, *sv, dt=F32), V(3, *sv, dt=F32), V(*sv, dt=F32), V(3, *sv, dt=F32), V(3, *sv, dt=F32), V(4, n, 256, dt=F32)]
+    scratch += [V(2, 256, d), V(256, d)] * 2
+    scratch += [V(8, nv, dt=F32), V(8, 256, dt=F32), V(8, 128, dt=F32), V(8, d, dt=F32)]
+    scratch += [D((4, Scatter.N))] * 2 + [D((2, 3))] * 2 + [D((10,))] * 2 + [D((3,))] * 2 + [D((11,))]
+    for c in (cols[3], cols[2], cols[0], cols[1]):
+        scratch += [V(2, 2, 2, n, c), V(2, 4, 2, n, c), V(2, n, c), V(2, 2, n, c), V(n, c), V(n, c)]
+    scan = bwd_scratch(nv)
+    scratch += list(scan.values())
+    return pl.pallas_call(
+        functools.partial(backward_kernel, list(scan), nv), out_shape=outs, in_specs=[anys] * 11 + [vm] * 7, out_specs=[vm] * 8, scratch_shapes=scratch,
+        compiler_params=pltpu.CompilerParams(collective_id=1, has_side_effects=True, vmem_limit_bytes=64 * 2**20), name="backward_all",
+    )(*ws, nrm, cot, vals, states, no, lg, dy, pgain, segc, segr, cx, cbc, hp, gg)
 
 
 def dot_nt(left, right):
@@ -815,40 +977,24 @@
     w0, w1, w_gate, w_out, normed_all, cot_all, vals, states, normed_out, low_gate, dy, gg = run_k1(
         hidden_in, cotangent, w_owns, spread8(pre_gain), segc, segr, cx, cbc, hp, spread8(gain_dev)
     )
-    partial_out = dot_nt(normed_out, w_out).astype(BF)
-    term_out = dot_tn(cot_all, normed_out)
-    low_a, gx, gbc, gh = run_backward(inner, vals, segc, segr, cx, cbc, hp, dy, states)
-    grad_normed = dot_nt(low_gate, w_gate) + dot_nt(low_a[:, :cut], w0) + dot_nt(low_a[:, cut:], w1)
-    part_pre = jnp.sum(grad_normed * normed_all.astype(F32), axis=0) / pre_gain
-    grad_normed = grad_normed.astype(BF)
-    term_a = dot_tn(normed_all, low_a).astype(BF)
-    term_b = jnp.concatenate([dot_tn(normed_all, low_gate), term_out], axis=1).astype(BF)
-    small = jnp.concatenate([gx[:5].reshape(-1), gg[0], gx[5], part_pre, gbc[:5].reshape(-1), gh[:2].reshape(-1)])
-    small = jnp.pad(small, (0, 9216 - small.shape[0])).reshape(72, 128)
-    blocks = (4, 4, 2, rows)
-    ra, rb, own_out, grad_own, smalls = reduce_all(
-        inner, term_a.reshape(blocks + term_a.shape[1:]), term_b.reshape(blocks + term_b.shape[1:]),
-        partial_out.reshape(4, 256, -1), grad_normed.reshape(4, 256, -1), small,
+    r_gate, r_out, r_x0, r_x1, d_bc, own_out, grad_own, smalls = run_k2(
+        (w0, w1, w_gate, w_out), normed_all, cot_all, vals, states, normed_out, low_gate, dy, spread8(pre_gain), segc, segr, cx, cbc, hp, gg
     )
     output = (hidden + own_out).astype(BF)
     scaled = grad_own * pre_gain[None, :]
     proj = jnp.mean(scaled * hidden, axis=1)
     grad_hidden = cotangent.astype(F32) + scaled * inv_rms[:, None] - hidden * (inv_rms * inv_rms * inv_rms * proj)[:, None]
-    smalls = smalls.reshape(4, 9216)
-    spread = lambda lo, n, k: smalls[:, lo : lo + n * k].reshape(4, k, n).transpose(1, 0, 2).reshape(k, 4 * n)
-    x_sums = spread(0, inner, 7)
-    at = 7 * inner
-    width = pre_gain.shape[0]
-    d_skip = x_sums[6].reshape(-1, 64).sum(axis=1)
-    both = jnp.sum(smalls[:, at : at + width + 5 * 256], axis=0)
-    d_pre = both[:width]
-    bc_sums = both[width:]
-    at = at + width + 5 * 256
-    d_dt_bias, d_a_log = (spread(at + 128 * i, 128, 1)[0].reshape(4, 128)[:, :heads].reshape(-1) for i in range(2))
+    across = lambda i, k=1: smalls[:, i : i + k].transpose(1, 0, 2).reshape(k, -1)
+    d_skip = across(5).reshape(-1, 64).sum(axis=1)
+    both = jnp.sum(smalls[:, 7:11], axis=0)
+    taps = both[2:4].reshape(2, 3, 256)
+    d_conv_bc = jnp.concatenate([taps[0], taps[1, :1]])
+    per_head = lambda i: smalls[:, 11, 128 * i : 128 * i + heads].reshape(-1)
     return (
-        output, grad_hidden, d_pre, rb[:, :inner], ra[:, :inner], ra[:, inner : inner + 256], ra[:, inner + 256 : inner + 256 + heads],
-        x_sums[:4], x_sums[4], bc_sums[:1024].reshape(4, 256), bc_sums[1024:], d_dt_bias, d_a_log, d_skip, x_sums[5],
-        rb[:, inner:].T,
+        output, grad_hidden, both[:2].reshape(-1), r_gate, jnp.concatenate([r_x0, r_x1[:, : inner - cut]], axis=1), d_bc,
+        r_x1[:, inner - cut + 256 : inner - cut + 256 + heads],
+        across(0, 4), across(4)[0], d_conv_bc, taps[1, 1], per_head(0), per_head(1), d_skip, across(6)[0],
+        r_out.T,
     )
 
 

time: 278 us -> 225 us (0.81)
  matrix products: 30.4 us -> 0 us
  Pallas kernels: 210 us -> 193 us
  local copies, waits for them, and re-layouts: 21.5 us -> 17.4 us
    dot_general x7 -> x0, matrix products: 30.4 us -> none  [the longest x4 18.7 us: dot_nt(): lax.dot_general(left, right, (((1,), (1,)), ((), ())), preferred_element_...]
    pallas_call x1, Pallas kernels: 105 us -> 84.3 us  [run_k1(): pl.pallas_call(functools.partial(forward_kernel, list(scan), nv), out_sha...]
    slice x13 -> x7, local copies, waits for them, and re-layouts: 5.84 us -> 1.26 us  [the longest x1 0.63 us: per_device(): across = lambda i, k=1: smalls[:, i:i + k].transpose(1, 0, 2).reshape(k, -1)]
    pallas_call x2 -> x1, Pallas kernels: 106 us -> 108 us  [run_k2(): pl.pallas_call(functools.partial(backward_kernel, list(scan), nv), out_sh...]
where the time goes in v4:
time: 225 us; the launch traced here: 224 us
  Pallas kernels  193 us (86%)
  local copies, waits for them, and re-layouts  17.4 us (8%)
  other arithmetic  13.2 us (6%)
    pallas_call x1, Pallas kernels, run_k2(): pl.pallas_call(functools.partial(backward_kernel, list(scan), nv), out_sh...  108 us
    pallas_call x1, Pallas kernels, run_k1(): pl.pallas_call(functools.partial(forward_kernel, list(scan), nv), out_sha...  84.3 us

profile of v4, /device:TPU:1, one launch (start us, length us, event | category | flops | bytes accessed | tf_op | source)
XLA Modules:
  0.0 224.0 jit_solution(10749244782755448466)
XLA Ops:
  0.7 0.7 dynamic_slice.21
  1.4 0.7 dynamic_slice.22
  2.1 0.7 dynamic_slice.20
  2.9 0.1 pad.26.clone
  2.9 0.1 pad.15.clone
  3.0 0.1 pad.18.clone
  3.1 0.1 pad.22.clone
  3.2 0.7 maximum_maximum_fusion.3.hp
  3.8 0.7 convert_element_type.16
  4.5 0.8 dynamic_slice.19
  5.3 0.8 dynamic_slice.23
  6.1 1.4 maximum_maximum_fusion.2.cbc
  7.4 0.1 broadcast_in_dim.29
  7.5 0.1 reshape.66
  7.6 0.7 constant_dynamic-slice_fusion
  8.3 0.7 maximum_maximum_fusion.1.cx
  9.0 0.8 copy.35
  9.8 0.7 slice.51
  10.5 0.6 broadcast_in_dim.70.ggain
  11.1 1.4 maximum_maximum_fusion.w_own1
  12.5 0.6 broadcast_in_dim.27.segr
  13.1 1.3 broadcast_in_dim.25.pgain
  14.4 1.5 slice.50.w_own0
  15.9 1.0 broadcast_in_dim.26.segc
  16.8 84.3 %forward_all.1 = (bf16[1536,640]{1,0:T(8,128)(2,1)}, bf16[1536,512]{1,0:T(8,128)(2,1)}, bf16[1536,768]{1,0:T(8,128)(2,1)}, bf16[1536,768]{1,0:T(8,128)(2,1)}, bf...) custom-call(bf16[256,1536]{1,0:T(8,128)(2,1)} %hid.1, ...), custom_call_target="tpu_custom_call" | custom-call | tf_op jit(solution)/shard_map/forward_all/pallas_call | solution.py:628
  101.2 108.3 %backward_all.1 = (f32[48,768]{1,0:T(8,128)}, f32[48,768]{1,0:T(8,128)}, f32[48,640]{1,0:T(8,128)}, f32[48,512]{1,0:T(8,128)}, f32[48,256]{1,0:T(8,128)}, /*inde...) custom-call(bf16[1536,640]{1,0:T(8,128)(2,1)} %get-tuple-element.36.h_w0, ...), custom_call_target="tpu_custom_call" | custom-call | tf_op jit(solution)/shard_map/backward_all/pallas_call | solution.py:935
  209.5 0.0 copy-start
  209.5 0.0 copy-start.1
  209.5 0.0 copy-start.6
  209.5 2.2 fusion.1
  211.7 0.0 copy-done
  211.7 0.2 copy-done.1
  211.9 0.0 copy-done.6
  211.9 0.0 copy-start.5
  211.9 0.0 copy-start.8
  211.9 0.0 copy-start.4
  211.9 0.0 copy-start.3
  211.9 0.0 copy-start.7
  211.9 0.0 copy-start.2
  211.9 3.7 %fusion.3 = (f32[256,1536]{1,0:T(8,128)}, bf16[256,1536]{1,0:T(8,128)(2,1)}) fusion(bf16[256,1536]{1,0:T(8,128)(2,1)S(1)} %copy-done, bf16[256,1536]{1,0:T(8,128)(2,1)} %cot_own.1, f32[256,1536]{1,0:T(8,128)S(1)} %copy-done.1, f32[256]{0:T(256)S(1)} %get-tuple-element.104, f32[256]{0:T(256)S(1)} %get-tuple-element.103, f32[1536]{0:T(1024)S(1)} %copy-done.6, ...), kind=kLoop, calls=%fused_computation.7 | loop fusion | flops 3538944 | bytes 7086080 | tf_op jit(solution)/shard_map/sub | solution.py:986
  215.6 0.0 copy-done.5
  215.6 0.6 reshape_squeeze.7
  216.2 0.6 reshape_squeeze.6
  216.8 0.0 copy-done.8
  216.8 0.7 copy.36
  217.5 0.0 copy-done.4
  217.5 0.7 pad_maximum_fusion
  218.2 0.6 fusion.5
  218.8 0.6 fusion.6
  219.5 0.6 fusion.8
  220.1 0.6 pad_maximum_fusion.1
  220.7 0.6 reshape.67
  221.3 0.1 reshape_reshape_transpose.3
  221.4 0.6 reduce_sum.39
  222.0 0.0 copy-done.3
  222.0 0.7 copy.40
  222.7 0.0 copy-done.7
  222.7 0.6 copy.41
  223.3 0.0 copy-done.2
  223.3 0.7 copy.42
  (14 shorter events, 0.1 us)
Async XLA Ops:
  209.5 2.2 copy-start
  209.5 2.4 %copy-start.1 = (f32[256,1536]{1,0:T(8,128)S(1)}, f32[256,1536]{1,0:T(8,128)}, u32[]{:S(2)}) copy-start(f32[256,1536]{1,0:T(8,128)} %get-tuple-element.49) | copy-start | bytes 4718596
  209.5 2.4 %copy-start.6 = (f32[1536]{0:T(1024)S(1)}, f32[1536]{0:T(1024)}, u32[]{:S(2)}) copy-start(f32[1536]{0:T(1024)} %param.19) | copy-start | bytes 18436
  211.9 3.7 %copy-start.5 = (f32[4,16,768]{2,1,0:T(8,128)S(1)}, f32[4,16,768]{2,1,0:T(8,128)}, u32[]{:S(2)}) copy-start(f32[4,16,768]{2,1,0:T(8,128)} %get-tuple-element.50) | copy-start | bytes 589828
  211.9 4.9 %copy-start.8 = (f32[48,512]{1,0:T(8,128)S(1)}, f32[48,512]{1,0:T(8,128)}, u32[]{:S(2)}) copy-start(f32[48,512]{1,0:T(8,128)} %get-tuple-element.53) | copy-start | bytes 294916
  211.9 5.6 %copy-start.4 = (f32[48,640]{1,0:T(8,128)S(1)}, f32[48,640]{1,0:T(8,128)}, u32[]{:S(2)}) copy-start(f32[48,640]{1,0:T(8,128)} %get-tuple-element.52) | copy-start | bytes 368644
  211.9 10.1 %copy-start.3 = (f32[48,768]{1,0:T(8,128)S(1)}, f32[48,768]{1,0:T(8,128)}, u32[]{:S(2)}) copy-start(f32[48,768]{1,0:T(8,128)} %get-tuple-element.126) | copy-start | bytes 442372
  211.9 10.8 %copy-start.7 = (f32[48,256]{1,0:T(8,128)S(1)}, f32[48,256]{1,0:T(8,128)}, u32[]{:S(2)}) copy-start(f32[48,256]{1,0:T(8,128)} %get-tuple-element.128) | copy-start | bytes 147460
  211.9 11.4 %copy-start.2 = (f32[48,768]{1,0:T(8,128)S(1)}, f32[48,768]{1,0:T(8,128)}, u32[]{:S(2)}) copy-start(f32[48,768]{1,0:T(8,128)} %get-tuple-element.55) | copy-start | bytes 442372

commit v5 on v4

--- a/solution.py
+++ b/solution.py
@@ -460,9 +460,9 @@
 
 def forward_kernel(
     names, nv,
-    hid, cot_own, w_own0, w_own1, w_own2, w_own3, pgain, segc, segr, cx, cbc, hp, ggain,
-    o_w0, o_w1, o_w2, o_w3, o_nrm, o_cot, o_vals, o_states, o_no, o_lg, o_dy, o_gg,
-    w0, w1, w2, w3, nrm, cot, vals, states, ssd, gate, gno, no, lg, dy, sums_own, sums_in,
+    hid, cot_own, p_x, p_bc, p_dt, p_gate, p_out, pgain, seg, conv_x, bias_x, conv_bc, bias_bc, dt_bias, a_log, skip_d, gate_gain,
+    o_w0, o_w1, o_w2, o_w3, o_nrm, o_cot, o_vals, o_states, o_no, o_lg, o_dy, o_gg, cx, cbc, hp, segc, segr,
+    square, w_own1, w0, w1, w2, w3, nrm, cot, vals, states, ssd, gate, gno, no, lg, dy, sums_own, sums_in,
     wsend, wrecv, tsend, trecv, ssend, srecv, lsem, *scan_scratch,
 ):
     s = dict(zip(names, scan_scratch))
@@ -470,6 +470,14 @@
     yl, co = t // 2, t % 2
     tp, slots = tensor_peers()
     width = hid.shape[1]
+    cut = w0.shape[1]
+    w_own0, w_own2, w_own3 = p_x.at[:, :cut], p_gate, p_out
+    w_own1[...] = jnp.zeros_like(w_own1)
+    w_own1[:, : nv - cut] = p_x[:, cut:]
+    w_own1[:, nv - cut : nv - cut + 256] = p_bc[...]
+    square[...] = jnp.zeros_like(square)
+    square[: p_dt.shape[0], : p_dt.shape[1]] = p_dt[...].astype(F32)
+    w_own1[:, nv - cut + 256 :] = square[...].T[: p_dt.shape[1]].astype(BF)
     greet([dev(x, z, 1 - yh, t)] + [neighbour(a, d) for a in "xz" for d in (1, -1)] + tp)
     owns, dsts, outs = (w_own0, w_own1, w_own2, w_own3), (w0, w1, w2, w3), (o_w0, o_w1, o_w2, o_w3)
     groups = lambda ks: [Gather(owns[k], dsts[k], "xz"[k % 2], wsend.at[k], wrecv.at[k]) for k in ks]
@@ -504,6 +512,27 @@
         return 0
 
     lax.fori_loop(0, 4, norm_rows, 0)
+    own_lanes = pl.ds(pl.multiple_of(t * nv, 128), nv)
+    heads = p_dt.shape[0]
+
+    def own_heads(v, lanes, per):
+        i, j = ii((v.shape[1], lanes), 0), ii((v.shape[1], lanes), 1)
+        pick = ((i == t * heads + j // per) & (j < heads * per)).astype(BF)
+        return sum(dnn(part, pick) for part in split3(jnp.broadcast_to(v[...], (8, v.shape[1]))))
+
+    cx[0:4] = conv_x[:, own_lanes]
+    cx[4:5] = bias_x[:, own_lanes]
+    cx[5:8] = own_heads(skip_d, nv, 64)[5:8]
+    cbc[0:4] = conv_bc[...]
+    cbc[4:8] = jnp.broadcast_to(bias_bc[...], (4, 256))
+    hp[0:1] = own_heads(dt_bias, 128, 1)[0:1]
+    hp[1:2] = jnp.where(ii((1, 128), 1) < heads, -jnp.exp(own_heads(a_log, 128, 1)[0:1]), 0.0)
+    hp[2:8] = jnp.zeros((6, 128), F32)
+    gains = gate_gain[:, own_lanes]
+    sf = seg[...].astype(F32)
+    for k in range(seg.shape[0]):
+        segr[:, k * 128 : k * 128 + 128] = jnp.broadcast_to(sf[k : k + 1], (8, 128))
+        segc[k * 128 : k * 128 + 128] = jnp.broadcast_to(sf[k : k + 1], (128, 128)).T
     for k in range(4):
         g = groups((k,))[0]
         g.mine[...] = g.own[...]
@@ -564,7 +593,7 @@
         gno[rows] = o
         gated = ssd[rows] * (g * sigmoid(g))
         sq = jnp.sum(gated * gated, axis=1, keepdims=True)
-        cr = jnp.sum(o * ggain[0:1] * gated, axis=1, keepdims=True)
+        cr = jnp.sum(o * gains * gated, axis=1, keepdims=True)
         lane = ii((256, 128), 1)
         both = jnp.where(lane == 0, sq, jnp.where(lane == 1, cr, 0.0))
         sums_own[:, rows] = both.T[:8]
@@ -586,7 +615,7 @@
         cross = inv * inv * inv * cols[:, 1:2] / INNER
         for k in range(nv // 128):
             lanes = pl.ds(k * 128, 128)
-            g, y, o, gain = gate[rows, lanes], ssd[rows, lanes], gno[rows, lanes], ggain[0:1, lanes]
+            g, y, o, gain = gate[rows, lanes], ssd[rows, lanes], gno[rows, lanes], gains[:, k * 128 : k * 128 + 128]
             sig = sigmoid(g)
             silu = g * sig
             gated = y * silu
@@ -610,25 +639,27 @@
         saved(*e).wait()
 
 
-def run_k1(hid, cot_own, w_owns, pgain, segc, segr, cx, cbc, hp, ggain):
+def run_k1(hid, cot_own, projs, pgain, seg, params):
     anys, vm = pl.BlockSpec(memory_space=pl.ANY), pl.BlockSpec(memory_space=pltpu.VMEM)
-    nv = cx.shape[1]
-    rows = segc.shape[0]
-    d = hid.shape[1]
+    nv = projs[0].shape[1]
+    rows = seg.shape[0] * seg.shape[1]
+    n, d = projs[0].shape[0], hid.shape[1]
     sh = jax.ShapeDtypeStruct
-    cols = [w.shape[1] for w in w_owns]
+    cols = [nv - 128, 512, nv, nv]
     nvals = cols[0] + cols[1]
-    outs = [sh((d, c), BF) for c in cols] + [sh((rows, d), BF)] * 2 + [sh((rows, nvals), F32), sh((rows // Q, 128, nv), BF)] + [sh((rows, nv), BF)] * 3 + [sh((8, nv), F32)]
+    outs = [sh((d, c), BF) for c in cols] + [sh((rows, d), BF)] * 2 + [sh((rows, nvals), F32), sh((rows // Q, 128, nv), BF)] + [sh((rows, nv), BF)] * 3
+    outs += [sh((8, nv), F32), sh((8, nv), F32), sh((8, 256), F32), sh((8, 128), F32), sh((rows, 128), F32), sh((8, rows), F32)]
     V = lambda shape, dt: pltpu.VMEM(shape, dt)
     D = pltpu.SemaphoreType.DMA
     scan = fwd_scratch(nv)
-    scratch = [V((d, c), BF) for c in cols] + [V((rows, d), BF)] * 2 + [V((rows, nvals), F32), V((rows // Q, 128, nv), BF)] + [V((rows, nv), F32)] * 3 + [V((rows, nv), BF)] * 3
+    scratch = [V((128, 128), F32), V((n, cols[1]), BF)] + [V((d, c), BF) for c in cols] + [V((rows, d), BF)] * 2
+    scratch += [V((rows, nvals), F32), V((rows // Q, 128, nv), BF)] + [V((rows, nv), F32)] * 3 + [V((rows, nv), BF)] * 3
     scratch += [V((8, rows), F32), V((3, 8, rows), F32), D((4, Gather.N)), D((4, Gather.N)), D((2, 3)), D((2, 3)), D((3,)), D((3,)), D((11,))]
     scratch += list(scan.values())
     return pl.pallas_call(
-        functools.partial(forward_kernel, list(scan), nv), out_shape=outs, in_specs=[vm] * 13, out_specs=[anys] * 11 + [vm], scratch_shapes=scratch,
+        functools.partial(forward_kernel, list(scan), nv), out_shape=outs, in_specs=[vm] * 17, out_specs=[anys] * 11 + [vm] * 6, scratch_shapes=scratch,
         compiler_params=pltpu.CompilerParams(collective_id=0, has_side_effects=True, vmem_limit_bytes=62 * 2**20), name="forward_all",
-    )(hid, cot_own, *w_owns, pgain, segc, segr, cx, cbc, hp, ggain)
+    )(hid, cot_own, *projs, pgain, seg, *params)
 
 
 class Scatter:
@@ -938,64 +969,90 @@
     )(*ws, nrm, cot, vals, states, no, lg, dy, pgain, segc, segr, cx, cbc, hp, gg)
 
 
-def dot_nt(left, right):
-    return lax.dot_general(left, right, (((1,), (1,)), ((), ())), preferred_element_type=F32)
-
-
-def dot_tn(left, right):
-    return lax.dot_general(left, right, (((0,), (0,)), ((), ())), preferred_element_type=F32)
+def finish_kernel(
+    heads, hid, cot, pgain, own_out, grad_own, smalls, r_gate, r_out, r_x0, r_x1, r_bc,
+    out, d_hid, d_pre, d_gate, d_x, d_bc, d_dt, d_conv_x, d_bias_x, d_conv_bc, d_bias_bc, d_dt_bias, d_a_log, d_skip, d_gain, d_out, square,
+):
+    def rows(i, _):
+        at = pl.ds(pl.multiple_of(i * 64, 64), 64)
+        h = hid[at].astype(F32)
+        g = grad_own[at]
+        inv = lax.rsqrt(jnp.mean(h * h, axis=1, keepdims=True) + EPS)
+        scaled = g * pgain[...]
+        back = jnp.mean(scaled * h, axis=1, keepdims=True)
+        out[at] = (h + own_out[at]).astype(BF)
+        d_hid[at] = cot[at].astype(F32) + scaled * inv - h * (inv * inv * inv * back)
+        return 0
+
+    lax.fori_loop(0, hid.shape[0] // 64, rows, 0)
+    nv = smalls.shape[2]
+    square[...] = jnp.zeros_like(square)
+    d_gate[...] = r_gate[...]
+    d_out[...] = r_out[...]
+    cut = r_x0.shape[1]
+    d_x[:, :cut] = r_x0[...]
+    d_x[:, cut:] = r_x1[:, : nv - cut]
+    d_bc[...] = r_bc[...]
+    square[: r_x1.shape[0]] = r_x1[:, nv - cut + 256 :]
+    d_dt[...] = square[...].T[:heads, : r_x1.shape[0]]
+    parts = [smalls[k] for k in range(4)]
+    both = parts[0] + parts[1] + parts[2] + parts[3]
+    d_pre[:, :nv] = both[7:8]
+    d_pre[:, nv:] = both[8:9]
+    for k in range(3):
+        d_conv_bc[k : k + 1] = both[9:10, k * 256 : k * 256 + 256]
+    d_conv_bc[3:4] = both[10:11, :256]
+    d_bias_bc[...] = both[10:11, 256:512]
+    per_head = [jnp.zeros((8, 128), F32)] * 3
+    for k in range(4):
+        lanes = slice(k * nv, k * nv + nv)
+        d_conv_x[:, lanes] = parts[k][0:4]
+        d_bias_x[:, lanes] = parts[k][4:5]
+        d_gain[:, lanes] = parts[k][6:7]
+        row = parts[k][8:16]
+        i, j = ii((128, 128), 0), ii((128, 128), 1)
+        pick = ((i + k * heads == j) & (i < heads)).astype(BF)
+        for n in range(2):
+            per_head[n] = per_head[n] + sum(dnn(p, pick) for p in split3(row[:, n * 128 : n * 128 + 128]))
+        i, j = ii((nv, 128), 0), ii((nv, 128), 1)
+        group = (i // 64 + k * heads == j).astype(BF)
+        per_head[2] = per_head[2] + sum(dnn(p, group) for p in split3(parts[k][0:8]))
+    d_dt_bias[...] = per_head[0][3:4, : 4 * heads]
+    d_a_log[...] = per_head[1][3:4, : 4 * heads]
+    d_skip[...] = per_head[2][5:6, : 4 * heads]
+
+
+def run_k3(heads, *args):
+    vm = pl.BlockSpec(memory_space=pltpu.VMEM)
+    smalls, r_gate = args[5], args[6]
+    n, nv = r_gate.shape
+    d = args[0].shape[1]
+    sh = lambda *s: jax.ShapeDtypeStruct(s, F32)
+    outs = [jax.ShapeDtypeStruct(args[0].shape, BF), sh(*args[0].shape), sh(1, d), sh(n, nv), sh(n, nv), sh(n, 256), sh(heads, n), sh(4, 4 * nv), sh(1, 4 * nv), sh(4, 256), sh(1, 256)]
+    outs += [sh(1, 4 * heads)] * 3 + [sh(1, 4 * nv), sh(n, nv)]
+    return pl.pallas_call(
+        functools.partial(finish_kernel, heads), out_shape=outs, in_specs=[vm] * len(args), out_specs=[vm] * len(outs), scratch_shapes=[pltpu.VMEM((128, 128), F32)],
+        compiler_params=pltpu.CompilerParams(vmem_limit_bytes=62 * 2**20), name="finish",
+    )(*args)
 
 
 def per_device(
     hidden_in, seg_ids, pre_gain, proj_gate, proj_x, proj_bc, proj_dt, conv_x, conv_bias_x, conv_bc, conv_bias_bc,
     dt_bias, a_log, skip_d, gate_gain, proj_out, cotangent,
 ):
-    t = lax.axis_index("tensor")
-    inner = proj_gate.shape[1]
-    heads = proj_dt.shape[1]
-    own = lambda v, n: lax.dynamic_slice_in_dim(v, t * n, n, v.ndim - 1)
-    gain_dev = own(gate_gain, inner)
-    hidden = hidden_in.astype(F32)
-    inv_rms = lax.rsqrt(jnp.mean(hidden * hidden, axis=1) + EPS)
-    rows = proj_x.shape[0]
-    cut = inner - 128
-    w_owns = (
-        proj_x[:, :cut],
-        jnp.concatenate([proj_x[:, cut:], proj_bc, proj_dt, jnp.zeros((rows, 128 - heads), BF)], axis=1),
-        proj_gate,
-        proj_out.T,
+    row = lambda v: v.reshape(1, -1)
+    pgain = row(pre_gain)
+    params = (conv_x, row(conv_bias_x), conv_bc, row(conv_bias_bc), row(dt_bias), row(a_log), row(skip_d), row(gate_gain))
+    w0, w1, w2, w3, normed, cot, vals, states, normed_out, low_gate, dy, gg, cx, cbc, hp, segc, segr = run_k1(
+        hidden_in, cotangent, (proj_x, proj_bc, proj_dt.T, proj_gate, proj_out.T), pgain, seg_ids.reshape(-1, 128), params
     )
-    seg = seg_ids.astype(F32)
-    segc = jnp.broadcast_to(seg[:, None], (seg.shape[0], 128))
-    segr = jnp.broadcast_to(seg[None, :], (8, seg.shape[0]))
-    heads_row = lambda v: jnp.pad(own(v, heads), (0, 128 - heads))[None]
-    skip_row = jnp.broadcast_to(own(skip_d, heads)[:, None], (heads, 64)).reshape(1, inner)
-    cx = jnp.concatenate([own(conv_x, inner), own(conv_bias_x, inner)[None], skip_row, jnp.zeros((2, inner), F32)])
-    cbc = jnp.concatenate([conv_bc, conv_bias_bc[None], jnp.zeros((3, 256), F32)])
-    hp = jnp.concatenate([heads_row(dt_bias), -jnp.exp(heads_row(a_log)), jnp.zeros((6, 128), F32)])
-    spread8 = lambda v: jnp.broadcast_to(v[None, :], (8, v.shape[0]))
-    w0, w1, w_gate, w_out, normed_all, cot_all, vals, states, normed_out, low_gate, dy, gg = run_k1(
-        hidden_in, cotangent, w_owns, spread8(pre_gain), segc, segr, cx, cbc, hp, spread8(gain_dev)
+    r_gate, r_out, r_x0, r_x1, r_bc, own_out, grad_own, smalls = run_k2(
+        (w0, w1, w2, w3), normed, cot, vals, states, normed_out, low_gate, dy, pgain, segc, segr, cx, cbc, hp, gg
     )
-    r_gate, r_out, r_x0, r_x1, d_bc, own_out, grad_own, smalls = run_k2(
-        (w0, w1, w_gate, w_out), normed_all, cot_all, vals, states, normed_out, low_gate, dy, spread8(pre_gain), segc, segr, cx, cbc, hp, gg
-    )
-    output = (hidden + own_out).astype(BF)
-    scaled = grad_own * pre_gain[None, :]
-    proj = jnp.mean(scaled * hidden, axis=1)
-    grad_hidden = cotangent.astype(F32) + scaled * inv_rms[:, None] - hidden * (inv_rms * inv_rms * inv_rms * proj)[:, None]
-    across = lambda i, k=1: smalls[:, i : i + k].transpose(1, 0, 2).reshape(k, -1)
-    d_skip = across(5).reshape(-1, 64).sum(axis=1)
-    both = jnp.sum(smalls[:, 7:11], axis=0)
-    taps = both[2:4].reshape(2, 3, 256)
-    d_conv_bc = jnp.concatenate([taps[0], taps[1, :1]])
-    per_head = lambda i: smalls[:, 11, 128 * i : 128 * i + heads].reshape(-1)
-    return (
-        output, grad_hidden, both[:2].reshape(-1), r_gate, jnp.concatenate([r_x0, r_x1[:, : inner - cut]], axis=1), d_bc,
-        r_x1[:, inner - cut + 256 : inner - cut + 256 + heads],
-        across(0, 4), across(4)[0], d_conv_bc, taps[1, 1], per_head(0), per_head(1), d_skip, across(6)[0],
-        r_out.T,
-    )
+    outs = run_k3(proj_dt.shape[1], hidden_in, cotangent, pgain, own_out, grad_own, smalls, r_gate, r_out, r_x0, r_x1, r_bc)
+    flat = (2, 8, 10, 11, 12, 13, 14)
+    turned = (6, 15)
+    return tuple(o.reshape(-1) if k in flat else o.T if k in turned else o for k, o in enumerate(outs))
 
 
 def solution(mesh):

time: 225 us -> 201 us (0.89)
  local copies, waits for them, and re-layouts: 17.4 us -> 1.3 us
  other arithmetic: 13.2 us -> 1.31 us
  Pallas kernels: 193 us -> 198 us
    concatenate x6 -> x0, other arithmetic: 5.35 us -> none  [the longest x1 1.37 us: per_device(): jnp.concatenate([conv_bc, conv_bias_bc[None], jnp.zeros((3, 256), F32)])]
    pallas_call x0 -> x1, Pallas kernels: none -> 5.02 us  [run_k3(): pl.pallas_call(functools.partial(finish_kernel, heads), out_shape=outs, i...]
    dynamic_slice x6 -> x0, local copies, waits for them, and re-layouts: 4.44 us -> none  [per_device(): own = lambda v, n: lax.dynamic_slice_in_dim(v, t * n, n, v.ndim - 1)]
    sub x1 -> x0, other arithmetic: 3.68 us -> none  [per_device(): cotangent.astype(F32) + scaled * inv_rms[:, None]]
    broadcast_in_dim x10 -> x0, local copies, waits for them, and re-layouts: 3.62 us -> none  [the longest x2 1.93 us: per_device(): spread8 = lambda v: jnp.broadcast_to(v[None, :], (8, v.shape[0]))]
    unnamed x23 -> x0, local copies, waits for them, and re-layouts: 3.62 us -> none
    slice x9 -> x0, local copies, waits for them, and re-layouts: 3.42 us -> none  [the longest x1 1.46 us: per_device(): proj_x[:, :cut]]
    reduce_sum x2 -> x0, other arithmetic: 2.78 us -> none  [the longest x1 2.15 us: per_device(): inv_rms = lax.rsqrt(jnp.mean(hidden * hidden, axis=1) + EPS)]
where the time goes in v5:
time: 201 us
  Pallas kernels  198 us (99%)
    pallas_call x1, Pallas kernels, run_k2(): pl.pallas_call(functools.partial(backward_kernel, list(scan), nv), out_sh...  108 us
    pallas_call x1, Pallas kernels, run_k1(): pl.pallas_call(functools.partial(forward_kernel, list(scan), nv), out_sha...  84.6 us
    pallas_call x1, Pallas kernels, run_k3(): pl.pallas_call(functools.partial(finish_kernel, heads), out_shape=outs, i...  5.02 us

profile of v5, /device:TPU:1, one launch (start us, length us, event | category | flops | bytes accessed | tf_op | source)
XLA Modules:
  0.0 201.0 jit_solution(11959133173055458135)
XLA Ops:
  0.6 1.3 reshape.77.pgain
  1.9 84.6 %forward_all.1 = (bf16[1536,640]{1,0:T(8,128)(2,1)}, bf16[1536,512]{1,0:T(8,128)(2,1)}, bf16[1536,768]{1,0:T(8,128)(2,1)}, bf16[1536,768]{1,0:T(8,128)(2,1)}, bf...) custom-call(bf16[256,1536]{1,0:T(8,128)(2,1)} %hid.3, ...), custom_call_target="tpu_custom_call" | custom-call | tf_op jit(solution)/shard_map/forward_all/pallas_call | solution.py:659
  86.5 108.2 %backward_all.1 = (f32[48,768]{1,0:T(8,128)}, f32[48,768]{1,0:T(8,128)}, f32[48,640]{1,0:T(8,128)}, f32[48,512]{1,0:T(8,128)}, f32[48,256]{1,0:T(8,128)}, /*inde...) custom-call(bf16[1536,640]{1,0:T(8,128)(2,1)} %get-tuple-element.57.h_w0, ...), custom_call_target="tpu_custom_call" | custom-call | tf_op jit(solution)/shard_map/backward_all/pallas_call | solution.py:966
  194.7 5.0 %finish.1 = (bf16[256,1536]{1,0:T(8,128)(2,1)}, f32[256,1536]{1,0:T(8,128)}, f32[1,1536]{1,0:T(1,128)}, f32[48,768]{1,0:T(8,128)}, f32[48,768]{1,0:T(8,128)}, /*...) custom-call(bf16[256,1536]{1,0:T(8,128)(2,1)} %hid.3, ...), custom_call_target="tpu_custom_call" | custom-call | tf_op jit(solution)/shard_map/finish/pallas_call | solution.py:1033
  199.7 1.3 reduce

commit v6 on v5

--- a/solution.py
+++ b/solution.py
@@ -233,7 +233,7 @@
     nh = nv // 64
     return dict(
         bt=V((128, Q), BF), b=V((Q, 128), BF), c=V((Q, 128), BF), qk=V((Q, Q)), bias=V((Q, Q)), cum=V((Q, nh * 128)), cumt=V((nh, 8, Q)),
-        step=V((Q, nv)), tail=V((Q, nv)), keep=V((8, nv)), ecum=V((Q, nv)), ex=V((128, nh * 128), BF), state=V((128, nv)), m=V((2, Q, Q), BF),
+        step=V((Q, nv)), tail=V((Q, nv)), keep=V((8, nv)), ecum=V((Q, nv)), ex=V((128, nh * 128), BF), state=V((128, nv)), m=V((4, Q, Q), BF),
     )
 
 
@@ -248,47 +248,43 @@
         match, *_r = block_setup(c, nv, vals, segc, segr, cbc, hp, s["bt"], s["b"], s["c"], None, s["qk"], s["bias"], s["cum"], s["cumt"], s["step"], s["tail"], s["keep"], s["ex"], s["ecum"])
         states[c] = s["state"][...].astype(BF)
 
-        def pair(j, _):
-            hook(c * (nv // 128) + j)
-            lanes = pl.ds(pl.multiple_of(j * 128, 128), 128)
-            pre, _sh = conv_terms(with_earlier(vals, r0, lanes), match, cx[:, lanes])
-            x = pre * sigmoid(pre)
-            u = x * s["step"][:, lanes]
-            ub = u.astype(BF)
-            st = s["state"][:, lanes]
-            y = dnn(s["c"][...], st.astype(BF)) * s["ecum"][:, lanes]
-            y = y + cx[5:6, lanes] * x
-            for e in range(2):
-                for r in range(4):
-                    rows = slice(r * 64, r * 64 + 64)
-                    for k in range(1 if r < 2 else 2):
-                        cols = slice(k * 128, k * 128 + 128)
-                        s["m"][e, rows, cols] = (decay(s["cum"], s["cumt"], s["bias"], 2 * j + e, rows, cols) * s["qk"][rows, cols]).astype(BF)
-            y0 = dnn(s["m"][0], ub)
-            y1 = dnn(s["m"][1], ub)
-            ssd[pl.ds(r0, Q), lanes] = y + jnp.where(ii((Q, 128), 1) < 64, y0, y1)
-            s["state"][:, lanes] = st * s["keep"][0:1, lanes] + dnn(s["bt"][...], (u * s["tail"][:, lanes]).astype(BF))
+        def pairs(jj, _):
+            hook(c * (nv // 256) + jj)
+            done = []
+            for p in range(2):
+                j = 2 * jj + p
+                lanes = pl.ds(pl.multiple_of(j * 128, 128), 128)
+                pre, _sh = conv_terms(with_earlier(vals, r0, lanes), match, cx[:, lanes])
+                x = pre * sigmoid(pre)
+                u = x * s["step"][:, lanes]
+                st = s["state"][:, lanes]
+                y = dnn(s["c"][...], st.astype(BF)) * s["ecum"][:, lanes] + cx[5:6, lanes] * x
+                new = st * s["keep"][0:1, lanes] + dnn(s["bt"][...], (u * s["tail"][:, lanes]).astype(BF))
+                done.append((j, lanes, u.astype(BF), y, new))
+            for r in range(4):
+                rows = slice(r * 64, r * 64 + 64)
+                for k in range(1 if r < 2 else 2):
+                    cols = slice(k * 128, k * 128 + 128)
+                    qk, bias = s["qk"][rows, cols], s["bias"][rows, cols]
+                    for p in range(2):
+                        for e in range(2):
+                            h = 2 * done[p][0] + e
+                            col = s["cum"][rows, pl.ds(pl.multiple_of(h * 128, 128), 128)]
+                            s["m"][2 * p + e, rows, cols] = (jnp.exp2(col - s["cumt"][h, 0:1, cols] + bias) * qk).astype(BF)
+            outs = []
+            for p in range(2):
+                _j, lanes, ub, y, new = done[p]
+                y0, y1 = dnn(s["m"][2 * p], ub), dnn(s["m"][2 * p + 1], ub)
+                outs.append(y + jnp.where(ii((Q, 128), 1) < 64, y0, y1))
+            for p in range(2):
+                ssd[pl.ds(r0, Q), done[p][1]] = outs[p]
+                s["state"][:, done[p][1]] = done[p][4]
             return 0
 
-        lax.fori_loop(0, nv // 128, pair, 0)
+        lax.fori_loop(0, nv // 256, pairs, 0)
         return 0
 
     lax.fori_loop(0, vals.shape[0] // Q, block, 0)
-
-
-def bwd_scratch(nv):
-    V = lambda s, d=F32: pltpu.VMEM(s, d)
-    d = fwd_scratch(nv)
-    d.update(ct=V((128, Q), BF), dqk=V((Q, Q)), dstate=V((128, nv)), dcs=V((Q, 128)), dbs=V((Q, 128)), rowg=V((Q, 128)), colg=V((nv // 64, 8, Q)), rs=V((Q, 128)),
-             gs=V((Q, 128)), ds=V((Q, 128)), krow=V((8, nv)), halo=V((8, nv)), halobc=V((8, 256)), dm=V((Q, Q)))
-    return d
-
-
-def to_head(v, j):
-    red = (ii((128, 128), 1) == 2 * j + ii((128, 128), 0) // 64).astype(BF)
-    hi = v.astype(BF)
-    lo = (v - hi.astype(F32)).astype(BF)
-    return dnn(jnp.concatenate([hi, lo], axis=1), jnp.concatenate([red, red], axis=0))
 
 
 def later_sum(dpre, halo, match_ext, taps):
@@ -300,120 +296,6 @@
     return out
 
 
-def ssd_backward(nv, vals, segc, segr, cx, cbc, hp, dy_ref, states, low, gx, gbc, gh, s, hook=lambda at: None):
-    nh = nv // 64
-    nb = vals.shape[0] // Q
-    s["ex"][...] = (ii((128, nh * 128), 0) == ii((128, nh * 128), 1) // 128).astype(BF)
-    for n in ("dstate", "halo", "halobc", "colg", "m"):
-        s[n][...] = jnp.zeros_like(s[n])
-    gx[...] = jnp.zeros_like(gx)
-    gbc[...] = jnp.zeros_like(gbc)
-    gh[...] = jnp.zeros_like(gh)
-
-    def block(i, _):
-        c = nb - 1 - i
-        r0 = pl.multiple_of(c * Q, Q)
-        match, bc_pre, bc_shifted, raw, step = block_setup(c, nv, vals, segc, segr, cbc, hp, s["bt"], s["b"], s["c"], s["ct"], s["qk"], s["bias"], s["cum"], s["cumt"], s["step"], s["tail"], s["keep"], s["ex"], s["ecum"])
-        nxt = segc[pl.ds(pl.multiple_of(jnp.minimum(r0 + Q, segc.shape[0] - 8), 8), 8), :]
-        seg = segc[pl.ds(r0, Q), :]
-        ext = jnp.concatenate([seg, nxt], axis=0)
-        after = [None] + [ext[k : Q + k] == seg for k in (1, 2, 3)]
-        for n in ("dqk", "dcs", "dbs", "rowg", "rs", "gs", "ds"):
-            s[n][...] = jnp.zeros_like(s[n])
-
-        def pair(j, _):
-            hook(i * (nv // 128) + j)
-            lanes = pl.ds(pl.multiple_of(j * 128, 128), 128)
-            taps = cx[:, lanes]
-            pre, shifted = conv_terms(with_earlier(vals, r0, lanes), match, taps)
-            sig = sigmoid(pre)
-            x = pre * sig
-            stepe = s["step"][:, lanes]
-            taile = s["tail"][:, lanes]
-            u = x * stepe
-            ub = u.astype(BF)
-            dy = dy_ref[pl.ds(r0, Q), lanes].astype(F32)
-            dyb = dy.astype(BF)
-            dyt = dy.T.astype(BF)
-            stb = states[c, :, lanes]
-            dst = s["dstate"][:, lanes]
-            dstb = dst.astype(BF)
-            edy = s["ecum"][:, lanes] * dy
-            edyb = edy.astype(BF)
-            s["rs"][...] += to_head(edy * dnn(s["c"][...], stb), j)
-            s["dcs"][...] += dnt(edyb, stb)
-            tu = taile * u
-            v = dnn(s["b"][...], dstb)
-            s["dbs"][...] += dnt(tu.astype(BF), dstb)
-            s["gs"][...] += to_head(tu * v, j)
-            keep = s["keep"][0:1, lanes]
-            s["krow"][:, lanes] = jnp.broadcast_to(keep * jnp.sum(stb.astype(F32) * dst, axis=0, keepdims=True), (8, 128))
-            s["dstate"][:, lanes] = keep * dst + dnn(s["ct"][...], edyb)
-            lane = ii((Q, 128), 1)
-            parts = []
-            for e in range(2):
-                h = 2 * j + e
-                mine = (lane < 64) if e == 0 else (lane >= 64)
-                s["dm"][...] = dnt(jnp.where(mine, dy, 0.0).astype(BF), ub)
-                colsum = [jnp.zeros((1, 128), F32), jnp.zeros((1, 128), F32)]
-                for r in range(4):
-                    rows = slice(r * 64, r * 64 + 64)
-                    rowsum = jnp.zeros((64, 128), F32)
-                    for k in range(1 if r < 2 else 2):
-                        cols = slice(k * 128, k * 128 + 128)
-                        dec = decay(s["cum"], s["cumt"], s["bias"], h, rows, cols)
-                        qk = s["qk"][rows, cols]
-                        p = s["dm"][rows, cols] * dec
-                        s["dqk"][rows, cols] += p
-                        g = p * qk
-                        rowsum = rowsum + g
-                        colsum[k] = colsum[k] + jnp.sum(g, axis=0, keepdims=True)
-                        s["m"][e, rows, cols] = (dec * qk).astype(BF)
-                    tot = jnp.sum(rowsum, axis=1, keepdims=True)
-                    s["rowg"][rows] += jnp.where(ii((64, 128), 1) == h, tot, 0.0)
-                s["colg"][h] = jnp.broadcast_to(jnp.concatenate(colsum, axis=1), (8, Q))
-                parts.append(dnn(dyt[e * 64 : e * 64 + 64], s["m"][e]))
-            du = jnp.concatenate(parts, axis=0).T + taile * v
-            s["ds"][...] += to_head(du * x, j)
-            skip = taps[5:6]
-            dx = du * stepe + skip * dy
-            dpre = dx * (sig + x * (1.0 - sig))
-            low[pl.ds(r0, Q), lanes] = later_sum(dpre, s["halo"][:, lanes], after, taps).astype(BF)
-            s["halo"][:, lanes] = dpre[:8]
-            gx[:, lanes] += jnp.concatenate(
-                [jnp.sum(dpre * shifted[3 - k], axis=0, keepdims=True) for k in range(4)]
-                + [jnp.sum(dpre, axis=0, keepdims=True), jnp.sum(dy * x, axis=0, keepdims=True), jnp.zeros((2, 128), F32)], axis=0)
-            return 0
-
-        lax.fori_loop(0, nv // 128, pair, 0)
-        tt, ss = ii((Q, Q), 0), ii((Q, Q), 1)
-        e64t = (ii((nv, 128), 0) // 64 == ii((nv, 128), 1)).astype(BF)
-        kh, km, kl = split3(s["krow"][...])
-        kterm = dnn(kh, e64t) + dnn(km, e64t) + dnn(kl, e64t)
-        colg = jnp.concatenate([s["colg"][h, 0:1] for h in range(nh)] + [jnp.zeros((128 - nh, Q), F32)], axis=0)
-        dcum = s["rowg"][...] - colg.T + s["rs"][...]
-        da = tri_times((ss >= tt).astype(BF), dcum) + tri_times((ss < tt).astype(BF), s["gs"][...]) + kterm[0:1]
-        rate = hp[1:2]
-        dstep = s["ds"][...] + rate * da
-        draw = dstep * sigmoid(raw)
-        draw = jnp.where(ii((Q, 128), 1) < nh, draw, 0.0)
-        low[pl.ds(r0, Q), pl.ds(nv + 256, 128)] = draw.astype(BF)
-        gh[...] += jnp.concatenate([jnp.sum(draw, axis=0, keepdims=True), jnp.sum(da * step, axis=0, keepdims=True) * rate, jnp.zeros((6, 128), F32)], axis=0)
-        dqk = s["dqk"][...]
-        dc = dnn(dqk.astype(BF), s["b"][...]) + s["dcs"][...]
-        db = dnn(dqk.T.astype(BF), s["c"][...]) + s["dbs"][...]
-        sig = sigmoid(bc_pre)
-        dpre = jnp.concatenate([db, dc], axis=1) * (sig + bc_pre * sig * (1.0 - sig))
-        after2 = [None] + [jnp.concatenate([m, m], axis=1) for m in after[1:]]
-        low[pl.ds(r0, Q), pl.ds(nv, 256)] = later_sum(dpre, s["halobc"][...], after2, cbc[...]).astype(BF)
-        s["halobc"][...] = dpre[:8]
-        gbc[...] += jnp.concatenate(
-            [jnp.sum(dpre * bc_shifted[3 - k], axis=0, keepdims=True) for k in range(4)] + [jnp.sum(dpre, axis=0, keepdims=True), jnp.zeros((3, 256), F32)], axis=0)
-        return 0
-
-    lax.fori_loop(0, nb, block, 0)
-
-
 def run_forward(nv, vals, segc, segr, cx, cbc, hp):
     sc = fwd_scratch(nv)
     names = list(sc)
@@ -430,13 +312,239 @@
     )(vals, segc, segr, cx, cbc, hp)
 
 
-def run_backward(nv, vals, segc, segr, cx, cbc, hp, dy, states):
-    sc = bwd_scratch(nv)
+def pack_heads(nh, cum, step, tail, ecum):
+    parts = list(split3(cum))
+    for v in (step, tail, ecum):
+        hi = v.astype(BF)
+        parts += [hi, (v - hi.astype(F32)).astype(BF)]
+    out = parts[0].astype(F32)
+    for k, p in enumerate(parts[1:]):
+        out = out + pltpu.roll(p.astype(F32), (k + 1) * nh, 1)
+    return out.astype(BF)
+
+
+def unpack_matrix(nh, j):
+    k, col = ii((128, 640), 0), ii((128, 640), 1)
+    kind = jnp.where(k < 3 * nh, 0, jnp.where(k < 5 * nh, 1, jnp.where(k < 7 * nh, 2, jnp.where(k < 9 * nh, 3, 9))))
+    want = jnp.maximum(col // 128 - 1, 0)
+    sub = jnp.where(col < 256, col // 128, (col % 128) // 64)
+    return ((kind == want) & (k % nh == 2 * j + sub)).astype(BF)
+
+
+def back_scratch(nv, rows):
+    V = lambda s, d=F32: pltpu.VMEM(s, d)
+    nb, nh = rows // Q, nv // 64
+    return dict(
+        b=V((rows, 128), BF), c=V((rows, 128), BF), bt=V((nb, 128, Q), BF), ct=V((nb, 128, Q), BF), qk=V((nb, Q, Q)), bias=V((nb, Q, Q)), pack=V((rows, 128), BF),
+        cumt=V((nb, nh, 8, Q)), un=V((2, 128, 640), BF), ex=V((2, Q, 640)), dqk=V((nb, Q, Q)), dcs=V((rows, 128)), dbs=V((rows, 128)), hsum=V((rows, 128)),
+        colg=V((nb, nh, 8, Q)), krow=V((nb, 8, nv)), dstate=V((2, 128, 128)), halo=V((2, 8, 128)), halobc=V((8, 256)), m=V((4, Q, Q), BF), dm=V((4, Q, Q)),
+    )
+
+
+def block_rows(c):
+    return pl.ds(pl.multiple_of(c * Q, Q), Q)
+
+
+def wide(match):
+    return [None] + [jnp.concatenate([m, m], axis=1) for m in match[1:]]
+
+
+def back_setup(nv, vals, segc, segr, cbc, hp, s):
+    nh = nv // 64
+    for n in ("dqk", "dcs", "dbs", "hsum", "m"):
+        s[n][...] = jnp.zeros_like(s[n])
+
+    def block(c, _):
+        r0 = pl.multiple_of(c * Q, Q)
+        rows = block_rows(c)
+        pre, _sh = conv_terms(with_earlier(vals, r0, pl.ds(nv, 256)), wide(match_rows(segc, r0)), cbc[...])
+        bc = pre * sigmoid(pre)
+        bb, cc = bc[:, :128].astype(BF), bc[:, 128:].astype(BF)
+        s["b"][rows], s["c"][rows] = bb, cc
+        s["bt"][c], s["ct"][c] = bc[:, :128].T.astype(BF), bc[:, 128:].T.astype(BF)
+        s["qk"][c] = dnt(cc, bb)
+        seg = segc[rows]
+        tt, ss = ii((Q, Q), 0), ii((Q, Q), 1)
+        allowed = (tt >= ss) & (jnp.concatenate([seg, seg], axis=1) == segr[0:1, rows])
+        s["bias"][c] = jnp.where(allowed, 0.0, NEG)
+        mine = ii((Q, 128), 1) < nh
+        step = jnp.where(mine, softplus(vals[rows, pl.ds(nv + 256, 128)] + hp[0:1]), 0.0)
+        cum = tri_times((tt >= ss).astype(BF), step * (hp[1:2] * LOG2E))
+        cumt = cum.T
+        for h in range(nh):
+            s["cumt"][c, h] = jnp.broadcast_to(cumt[h : h + 1], (8, Q))
+        before = segc[pl.ds(pl.multiple_of(jnp.maximum(r0 - 8, 0), 8), 8)][7:8]
+        before = jnp.where(c > 0, before, -1.0)
+        zero = lambda v: jnp.where(mine, v, 0.0)
+        tail = zero(jnp.exp2(cum[Q - 1 :] - cum) * (seg == seg[Q - 1 :]).astype(F32))
+        ecum = zero(jnp.exp2(cum) * (seg == before).astype(F32))
+        s["pack"][rows] = pack_heads(nh, cum, step, tail, ecum)
+        return 0
+
+    lax.fori_loop(0, vals.shape[0] // Q, block, 0)
+
+
+def back_pairs(at, nv, vals, segc, cx, dy_ref, states, low, gx, s):
+    nb, nh = vals.shape[0] // Q, nv // 64
+    jj, i = at // nb, at % nb
+    c = nb - 1 - i
+    r0 = pl.multiple_of(c * Q, Q)
+    rows_c = block_rows(c)
+
+    @pl.when(i == 0)
+    def _():
+        s["dstate"][...] = jnp.zeros_like(s["dstate"])
+        s["halo"][...] = jnp.zeros_like(s["halo"])
+        for p in range(2):
+            s["un"][p] = unpack_matrix(nh, 2 * jj + p)
+
+    match, after = match_rows(segc, r0), match_after(segc, r0)
+    lane = ii((Q, 128), 1)
+    one = []
+    dcs = dbs = 0.0
+    for p in range(2):
+        j = 2 * jj + p
+        lanes = pl.ds(pl.multiple_of(j * 128, 128), 128)
+        s["ex"][p] = dnn(s["pack"][rows_c], s["un"][p])
+        stepe, taile, ecume = s["ex"][p, :, 256:384], s["ex"][p, :, 384:512], s["ex"][p, :, 512:640]
+        keep = s["ex"][p, Q - 1 : Q, 512:640]
+        taps = cx[:, lanes]
+        pre, shifted = conv_terms(with_earlier(vals, r0, lanes), match, taps)
+        sig = sigmoid(pre)
+        x = pre * sig
+        u = x * stepe
+        dy = dy_ref[rows_c, lanes].astype(F32)
+        stb = states[c, :, lanes]
+        dst = s["dstate"][p]
+        dstb = dst.astype(BF)
+        edy = ecume * dy
+        edyb = edy.astype(BF)
+        rs = edy * dnn(s["c"][rows_c], stb)
+        dcs = dcs + dnt(edyb, stb)
+        tu = taile * u
+        v = dnn(s["b"][rows_c], dstb)
+        dbs = dbs + dnt(tu.astype(BF), dstb)
+        krow = keep * jnp.sum(stb.astype(F32) * dst, axis=0, keepdims=True)
+        s["dstate"][p] = keep * dst + dnn(s["ct"][c], edyb)
+        ub = u.astype(BF)
+        for e in range(2):
+            mine = (lane < 64) if e == 0 else (lane >= 64)
+            s["dm"][2 * p + e] = dnt(jnp.where(mine, dy, 0.0).astype(BF), ub)
+        one.append((j, lanes, stepe, taile, taps, shifted, sig, x, dy, dy.T.astype(BF), rs, tu, v, krow))
+    s["dcs"][rows_c] += dcs
+    s["dbs"][rows_c] += dbs
+    colsum = [[jnp.zeros((8, 128), F32) for _ in range(2)] for _ in range(4)]
+    rowg = []
+    for r in range(4):
+        rows = slice(r * 64, r * 64 + 64)
+        rowsum = [None] * 4
+        for k in range(1 if r < 2 else 2):
+            cols = slice(k * 128, k * 128 + 128)
+            qk, bias = s["qk"][c, rows, cols], s["bias"][c, rows, cols]
+            total = None
+            for n in range(4):
+                p, e = n // 2, n % 2
+                dec = jnp.exp2(s["ex"][p, rows, e * 128 : e * 128 + 128] - s["cumt"][c, 4 * jj + n, 0:1, cols] + bias)
+                s["m"][n, rows, cols] = (dec * qk).astype(BF)
+                g = s["dm"][n, rows, cols] * dec
+                total = g if n == 0 else total + g
+                g = g * qk
+                rowsum[n] = g if k == 0 else rowsum[n] + g
+                colsum[n][k] = colsum[n][k] + jnp.sum(g.reshape(8, 8, 128), axis=0)
+            s["dqk"][c, rows, cols] += total
+        at_lane = ii((64, 128), 1)
+        row = jnp.zeros((64, 128), F32)
+        for n in range(4):
+            row = jnp.where(at_lane == 48 + 4 * jj + n, jnp.sum(rowsum[n], axis=1, keepdims=True), row)
+        rowg.append(row)
+    heads = jnp.concatenate(rowg, axis=0)
+    ends = []
+    for p in range(2):
+        j, lanes, stepe, taile, taps, shifted, sig, x, dy, dyt, rs, tu, v, krow = one[p]
+        parts = [dnn(dyt[e * 64 : e * 64 + 64], s["m"][2 * p + e]) for e in range(2)]
+        du = jnp.concatenate(parts, axis=0).T + taile * v
+        k, col = ii((384, 128), 0), ii((384, 128), 1)
+        red = (col == 16 * (k // 128) + 2 * j + (k % 128) // 64).astype(BF)
+        heads = heads + dnn(jnp.concatenate([rs.astype(BF), (tu * v).astype(BF), (du * x).astype(BF)], axis=1), red)
+        dx = du * stepe + taps[5:6] * dy
+        dpre = dx * (sig + x * (1.0 - sig))
+        grow = jnp.concatenate(
+            [jnp.sum(dpre * shifted[3 - k], axis=0, keepdims=True) for k in range(4)]
+            + [jnp.sum(dpre, axis=0, keepdims=True), jnp.sum(dy * x, axis=0, keepdims=True), jnp.zeros((2, 128), F32)], axis=0)
+        ends.append((later_sum(dpre, s["halo"][p], after, taps).astype(BF), dpre[:8], grow))
+    s["hsum"][rows_c] += heads
+    for n in range(4):
+        s["colg"][c, 4 * jj + n] = jnp.broadcast_to(jnp.concatenate([jnp.sum(q, axis=0, keepdims=True) for q in colsum[n]], axis=1), (8, Q))
+    for p in range(2):
+        lanes = one[p][1]
+        low[rows_c, lanes], s["halo"][p] = ends[p][0], ends[p][1]
+        gx[:, lanes] += ends[p][2]
+        s["krow"][c, :, lanes] = jnp.broadcast_to(one[p][13], (8, 128))
+
+
+def match_after(segc, r0):
+    nxt = segc[pl.ds(pl.multiple_of(jnp.minimum(r0 + Q, segc.shape[0] - 8), 8), 8)]
+    seg = segc[pl.ds(r0, Q)]
+    ext = jnp.concatenate([seg, nxt], axis=0)
+    return [None] + [ext[k : Q + k] == seg for k in (1, 2, 3)]
+
+
+def back_finish(nv, vals, segc, cbc, hp, low, gbc, gh, s):
+    nb, nh = vals.shape[0] // Q, nv // 64
+    s["halobc"][...] = jnp.zeros_like(s["halobc"])
+    gbc[...] = jnp.zeros_like(gbc)
+    gh[...] = jnp.zeros_like(gh)
+
+    def block(i, _):
+        c = nb - 1 - i
+        r0 = pl.multiple_of(c * Q, Q)
+        rows = block_rows(c)
+        tt, ss = ii((Q, Q), 0), ii((Q, Q), 1)
+        e64t = (ii((nv, 128), 0) // 64 == ii((nv, 128), 1)).astype(BF)
+        kterm = sum(dnn(p, e64t) for p in split3(s["krow"][c]))
+        colg = jnp.concatenate([s["colg"][c, h, 0:1] for h in range(nh)] + [jnp.zeros((128 - nh, Q), F32)], axis=0)
+        hs = s["hsum"][rows]
+        mine = ii((Q, 128), 1) < nh
+        part = lambda k: jnp.where(mine, hs if k == 0 else pltpu.roll(hs, 128 - 16 * k, 1), 0.0)
+        dcum = part(3) - colg.T + part(0)
+        da = tri_times((ss >= tt).astype(BF), dcum) + tri_times((ss < tt).astype(BF), part(1)) + kterm[0:1]
+        rate = hp[1:2]
+        raw = vals[rows, pl.ds(nv + 256, 128)] + hp[0:1]
+        draw = jnp.where(mine, (part(2) + rate * da) * sigmoid(raw), 0.0)
+        low[rows, pl.ds(nv + 256, 128)] = draw.astype(BF)
+        gh[...] += jnp.concatenate(
+            [jnp.sum(draw, axis=0, keepdims=True), jnp.sum(da * softplus(raw), axis=0, keepdims=True) * rate, jnp.zeros((6, 128), F32)], axis=0)
+        dqk = s["dqk"][c]
+        dc = dnn(dqk.astype(BF), s["b"][rows]) + s["dcs"][rows]
+        db = dnn(dqk.T.astype(BF), s["c"][rows]) + s["dbs"][rows]
+        pre, shifted = conv_terms(with_earlier(vals, r0, pl.ds(nv, 256)), wide(match_rows(segc, r0)), cbc[...])
+        sig = sigmoid(pre)
+        dpre = jnp.concatenate([db, dc], axis=1) * (sig + pre * sig * (1.0 - sig))
+        low[rows, pl.ds(nv, 256)] = later_sum(dpre, s["halobc"][...], wide(match_after(segc, r0)), cbc[...]).astype(BF)
+        s["halobc"][...] = dpre[:8]
+        gbc[...] += jnp.concatenate(
+            [jnp.sum(dpre * shifted[3 - k], axis=0, keepdims=True) for k in range(4)] + [jnp.sum(dpre, axis=0, keepdims=True), jnp.zeros((3, 256), F32)], axis=0)
+        return 0
+
+    lax.fori_loop(0, nb, block, 0)
+
+
+def run_backward2(nv, vals, segc, segr, cx, cbc, hp, dy, states):
+    rows = vals.shape[0]
+    sc = back_scratch(nv, rows)
     names = list(sc)
-    rows = vals.shape[0]
 
     def kernel(vals, segc, segr, cx, cbc, hp, dy, states, low, gx, gbc, gh, *scr):
-        ssd_backward(nv, vals, segc, segr, cx, cbc, hp, dy, states, low, gx, gbc, gh, dict(zip(names, scr)))
+        s = dict(zip(names, scr))
+        gx[...] = jnp.zeros_like(gx)
+        back_setup(nv, vals, segc, segr, cbc, hp, s)
+
+        def body(at, _):
+            back_pairs(at, nv, vals, segc, cx, dy, states, low, gx, s)
+            return 0
+
+        lax.fori_loop(0, nv // 256 * (rows // Q), body, 0)
+        back_finish(nv, vals, segc, cbc, hp, low, gbc, gh, s)
 
     vm = pl.BlockSpec(memory_space=pltpu.VMEM)
     outs = (jax.ShapeDtypeStruct((rows, nv + 384), BF), jax.ShapeDtypeStruct((8, nv), F32), jax.ShapeDtypeStruct((8, 256), F32), jax.ShapeDtypeStruct((8, 128), F32))
@@ -576,7 +684,7 @@
         cot_copies[0].wait_recv()
         cot_copies[2].start()
 
-    events = [(1, lambda: step(second, 3)), (6, lambda: step(second, 5)), (10, lambda: step(second, 6)), (14, cot_forward)]
+    events = [(1, lambda: step(second, 3)), (3, lambda: step(second, 5)), (5, lambda: step(second, 6)), (7, cot_forward)]
     ssd_forward(nv, vals, segc, segr, cx, cbc, hp, ssd, states, s, lambda at: at_step(at, events))
     step(second, 7)
     cot_copies[1].wait_recv()
@@ -713,7 +821,7 @@
                 def add(j, _, side=side, at=at):
                     e, y = j // 2, j % 2
                     ix = (2 * side + e, at, y) if self.a1 == "z" else (at, 2 * side + e, y)
-                    v[ix] = (v[ix].astype(F32) + r1[side, e, y].astype(F32)).astype(BF)
+                    v[ix] = v[ix] + r1[side, e, y]
                     return 0
 
                 lax.fori_loop(0, 4, add, 0)
@@ -724,7 +832,7 @@
             def add(j, _):
                 e, y = j // 2, j % 2
                 own = v[e, p, y] if self.a1 == "z" else v[p, e, y]
-                h[e, y] = (own.astype(F32) + r2[0, e, y].astype(F32) + r2[1, e, y].astype(F32)).astype(BF)
+                h[e, y] = own + (r2[0, e, y] + r2[1, e, y])
                 return 0
 
             lax.fori_loop(0, 8, add, 0)
@@ -733,7 +841,7 @@
             for side, d in ((0, 1), (1, -1)):
                 self.arrive(6 + side)
                 at = m4(q + d)
-                h[at, side] = (h[at, side].astype(F32) + q1[side].astype(F32)).astype(BF)
+                h[at, side] = h[at, side] + q1[side]
                 self.start(10 + side)
         elif n == 4:
             self.arrive(8, 9, 10, 11)
@@ -771,7 +879,7 @@
             def add(j, _):
                 rows = pl.ds(pl.multiple_of(j * 32, 32), 32)
                 own = pl.ds(pl.multiple_of(self.pass_on * 256 + j * 32, 32), 32)
-                self.v[own] = (self.v[own].astype(F32) + self.from_core[0, rows].astype(F32)).astype(BF)
+                self.v[own] = self.v[own] + self.from_core[0, rows]
                 return 0
 
             lax.fori_loop(0, 8, add, 0)
@@ -796,12 +904,12 @@
 def backward_kernel(
     names, nv,
     h_w0, h_w1, h_w2, h_w3, h_nrm, h_cot, h_vals, h_states, h_no, h_lg, h_dy, pgain, segc, segr, cx, cbc, hp, gg,
-    o_gate, o_out, o_x0, o_x1, o_bc, o_own, o_grad, o_small,
-    w0, w1, w23, nrm, cot, vals, states, nody, lg, low, po, t_gate, t_out, t_x0, t_x1,
-    own_v, sx, sz, sy, st, sacc, bct, fc0, ch0, fc1, ch1, gx, gbc, gh, pre,
+    o_gate, o_out, o_x, o_dt, o_bc, o_own, o_grad, o_small,
+    w0, w1, w23, nrm, cot, vals, states, nody, lg, low, po, t_out, t_gate, t_0, t_1, t_2, t_bc, t_dt,
+    bc_sum, own_v, sx, sz, sy, st, sacc, bct, fc0, ch0, fc1, ch1, gx, gbc, gh, pre,
     wsend, wrecv, tsend, trecv, ssend, srecv, bsend, brecv, lsem, *rest,
 ):
-    bufs, s = [rest[6 * k : 6 * k + 6] for k in range(4)], dict(zip(names, rest[24:]))
+    bufs, s = [rest[6 * k : 6 * k + 6] for k in range(7)], dict(zip(names, rest[42:]))
     x, z, yh, t = place()
     tp, slots = tensor_peers()
     loads = [
@@ -812,11 +920,13 @@
         c.start()
     load_dy, load_w2 = pltpu.make_async_copy(h_dy, nody, lsem.at[9]), pltpu.make_async_copy(h_w2, w23, lsem.at[10])
     greet([dev(x, z, 1 - yh, t)] + [neighbour(a, d) for a in "xz" for d in (1, 2, 3)] + tp)
+    wide_x = o_x.shape[1] // 3
+    x_part = lambda k: o_x.at[:, k * wide_x : k * wide_x + wide_x]
     scat = [
-        Scatter(v, bufs[k], o, a1, wsend.at[k], wrecv.at[k])
-        for k, (v, o, a1) in enumerate(((t_out, o_out, "x"), (t_gate, o_gate, "z"), (t_x0, o_x0, "x"), (t_x1, o_x1, "z")))
+        Scatter(v, bufs[k], o, "xzxzxzx"[k], wsend.at[k], wrecv.at[k])
+        for k, (v, o) in enumerate(((t_out, o_out), (t_gate, o_gate), (t_0, x_part(0)), (t_1, x_part(1)), (t_2, x_part(2)), (t_bc, bc_sum), (t_dt, o_dt)))
     ]
-    s_out, s_gate, s_x0, s_x1 = scat
+    s_out, s_gate, s_0, s_1, s_2, s_bc, s_dt = scat
     k_out = TokenScatter(po, fc0, ch0, o_own, tsend.at[0], trecv.at[0])
     k_nrm = TokenScatter(cot, fc1, ch1, o_grad, tsend.at[1], trecv.at[1])
 
@@ -836,32 +946,65 @@
 
         lax.fori_loop(0, 4, body, 0)
 
-    for k in (0, 1):
-        loads[k].wait()
+    loads[0].wait()
+    loads[2].wait()
+    outer_product(t_out, cot, nody)
+    s_out.step(0)
+    loads[3].wait()
+    loads[4].wait()
+    outer_product(t_gate, nrm, lg)
+    s_gate.step(0)
 
     def out_rows(rows):
         left = nody[rows]
         for k in range(0, po.shape[1], 512):
             po[rows, k : k + 512] = dnt(left, w23[k : k + 512]).astype(BF)
 
+    loads[1].wait()
     by_rows(out_rows)
     load_w2.start()
+    load_dy.start()
     k_out.step(0)
-    loads[2].wait()
-    outer_product(t_out, cot, nody)
-    load_dy.start()
-    s_out.step(0)
-    k_out.step(1)
-    loads[3].wait()
-    loads[4].wait()
-    outer_product(t_gate, nrm, lg)
-    s_gate.step(0)
     for k in (5, 6, 7, 8):
         loads[k].wait()
+    back_setup(nv, vals, segc, segr, cbc, hp, s)
     load_dy.wait()
     both = lambda n: lambda: (s_out.step(n), s_gate.step(n))
-    events = [(6, both(1)), (12, both(2)), (16, both(3)), (18, both(4)), (20, both(5)), (22, lambda: k_out.step(2))]
-    ssd_backward(nv, vals, segc, segr, cx, cbc, hp, nody, states, low, gx, gbc, gh, s, lambda at: at_step(at, events))
+
+    def chunk(n):
+        def go():
+            outer_product((t_0, t_1, t_2)[n], nrm, low.at[:, n * wide_x : n * wide_x + wide_x])
+            scat[2 + n].step(0)
+
+        return go
+
+    gx[...] = jnp.zeros_like(gx)
+    events = [
+        (1, lambda: k_out.step(1)),
+        (4, both(1)),
+        (6, chunk(0)),
+        (8, both(2)),
+        (9, chunk(1)),
+        (10, lambda: k_out.step(2)),
+        (11, both(3)),
+    ]
+
+    def scan_step(at, _):
+        at_step(at, events)
+        back_pairs(at, nv, vals, segc, cx, nody, states, low, gx, s)
+        return 0
+
+    lax.fori_loop(0, nv // 256 * (vals.shape[0] // Q), scan_step, 0)
+    chunk(2)()
+    back_finish(nv, vals, segc, cbc, hp, low, gbc, gh, s)
+    outer_product(t_bc, nrm, low.at[:, nv : nv + 256])
+    s_bc.step(0)
+    outer_product(t_dt, nrm, low.at[:, nv + 256 :])
+    s_dt.step(0)
+    s_out.step(4)
+    s_gate.step(4)
+    s_0.step(1)
+    s_1.step(1)
     load_w2.wait()
     pre[...] = jnp.zeros_like(pre)
     c0 = w0.shape[1]
@@ -873,11 +1016,13 @@
             pre[0:1, cols] += jnp.sum(g * nrm[rows, cols].astype(F32), axis=0, keepdims=True)
             cot[rows, cols] = g.astype(BF)
 
-    by_rows(grad_rows)
-    k_nrm.step(0)
-    outer_product(t_x0, nrm, low.at[:, :c0])
-    s_x0.step(0)
-    k_nrm.step(1)
+    def grad_slot(i, _):
+        slot = ((t // 2 + 1 - i // 2) % 2) * 2 + (t + 1 - i % 2) % 2
+        grad_rows(pl.ds(pl.multiple_of(slot * 256, 256), 256))
+        at_step(i, [(0, lambda: k_nrm.copies(0).start()), (1, lambda: k_nrm.step(1)), (2, lambda: k_nrm.copies(1).start())])
+        return 0
+
+    lax.fori_loop(0, 4, grad_slot, 0)
     own_v[...] = jnp.zeros_like(own_v)
     own_v[0:6] = gx[0:6]
     own_v[6:7] = gg[0:1]
@@ -891,9 +1036,13 @@
     small = [send(own_v, sx.at[d - 1], ssend.at[d - 1], srecv.at[d - 1], neighbour("x", d)) for d in (1, 2, 3)]
     for c in small:
         c.start()
-    outer_product(t_x1, nrm, low.at[:, c0:])
-    s_x1.step(0)
-    last = lambda n: (s_x0.step(n), s_x1.step(n))
+    s_2.step(1)
+    s_bc.step(1)
+    s_dt.step(1)
+    s_out.step(5)
+    s_gate.step(5)
+    s_0.step(2)
+    s_1.step(2)
 
     def next_small(have, total, copies):
         for c in have:
@@ -913,20 +1062,31 @@
         sacc[2] = sacc[1] + sy[...]
 
     small_z = next_small(small, total_x, [send(sacc.at[0], sz.at[d - 1], ssend.at[2 + d], srecv.at[2 + d], neighbour("z", d)) for d in (1, 2, 3)])
-    last(1)
+    s_2.step(2)
+    s_bc.step(2)
+    s_dt.step(2)
     small_y = next_small(small_z, total_z, [send(sacc.at[1], sy, ssend.at[6], srecv.at[6], dev(x, z, 1 - yh, t))])
-    last(2)
+    s_0.step(3)
+    s_1.step(3)
+    s_2.step(3)
+    s_bc.step(3)
+    s_dt.step(3)
     small_t = next_small(small_y, total_y, [send(sacc.at[2], st.at[k], ssend.at[7 + k], srecv.at[7 + k], p) for k, p in enumerate(tp)])
-    k_nrm.step(2)
-    last(3)
-    last(4)
-    s_x1.step(5)
-    bc0 = o_x1.shape[1] - 384
-    bct[3] = o_x1[:, bc0 : bc0 + 256]
+    s_2.step(4)
+    s_bc.step(4)
+    s_dt.step(4)
+    s_0.step(4)
+    s_1.step(4)
+    s_2.step(5)
+    s_bc.step(5)
+    s_dt.step(5)
+    s_0.step(5)
+    s_1.step(5)
+    bct[3] = bc_sum[...]
     bcs = [send(bct.at[3], bct.at[k], bsend.at[k], brecv.at[k], p) for k, p in enumerate(tp)]
     for c in bcs:
         c.start()
-    s_x0.step(5)
+    k_nrm.step(2)
     for c in small_t:
         c.wait_recv()
     o_small[t] = sacc[2]
@@ -950,18 +1110,20 @@
     n = d // 32
     V = lambda *s, dt=BF: pltpu.VMEM(s, dt)
     D = pltpu.SemaphoreType.DMA
-    outs = [sh(n, cols[2]), sh(n, cols[3]), sh(n, cols[0]), sh(n, cols[1]), sh(n, 256), sh(256, d), sh(256, d), sh(4, 16, nv)]
+    parts = (nv, nv, nv // 3, nv // 3, nv // 3, 256, 128)
+    outs = [sh(n, nv), sh(n, nv), sh(n, nv), sh(n, 128), sh(n, 256), sh(256, d), sh(256, d), sh(4, 16, nv)]
     term = lambda c: V(4, 4, 2, n, c)
     scratch = [V(d, cols[0]), V(d, cols[1]), V(d, cols[2]), V(rows, d), V(rows, d), V(*vals.shape, dt=F32), V(*states.shape), V(rows, nv), V(rows, nv), V(*vals.shape), V(rows, d)]
-    scratch += [term(cols[2]), term(cols[3]), term(cols[0]), term(cols[1])]
+    scratch += [term(c) for c in parts]
     sv = (16, nv)
+    scratch += [V(n, 256, dt=F32)]
     scratch += [V(*sv, dt=F32), V(3, *sv, dt=F32), V(3, *sv, dt=F32), V(*sv, dt=F32), V(3, *sv, dt=F32), V(3, *sv, dt=F32), V(4, n, 256, dt=F32)]
     scratch += [V(2, 256, d), V(256, d)] * 2
     scratch += [V(8, nv, dt=F32), V(8, 256, dt=F32), V(8, 128, dt=F32), V(8, d, dt=F32)]
-    scratch += [D((4, Scatter.N))] * 2 + [D((2, 3))] * 2 + [D((10,))] * 2 + [D((3,))] * 2 + [D((11,))]
-    for c in (cols[3], cols[2], cols[0], cols[1]):
+    scratch += [D((7, Scatter.N))] * 2 + [D((2, 3))] * 2 + [D((10,))] * 2 + [D((3,))] * 2 + [D((11,))]
+    for c in parts:
         scratch += [V(2, 2, 2, n, c), V(2, 4, 2, n, c), V(2, n, c), V(2, 2, n, c), V(n, c), V(n, c)]
-    scan = bwd_scratch(nv)
+    scan = back_scratch(nv, rows)
     scratch += list(scan.values())
     return pl.pallas_call(
         functools.partial(backward_kernel, list(scan), nv), out_shape=outs, in_specs=[anys] * 11 + [vm] * 7, out_specs=[vm] * 8, scratch_shapes=scratch,
@@ -970,7 +1132,7 @@
 
 
 def finish_kernel(
-    heads, hid, cot, pgain, own_out, grad_own, smalls, r_gate, r_out, r_x0, r_x1, r_bc,
+    heads, hid, cot, pgain, own_out, grad_own, smalls, r_gate, r_out, r_x, r_last, r_bc,
     out, d_hid, d_pre, d_gate, d_x, d_bc, d_dt, d_conv_x, d_bias_x, d_conv_bc, d_bias_bc, d_dt_bias, d_a_log, d_skip, d_gain, d_out, square,
 ):
     def rows(i, _):
@@ -989,12 +1151,10 @@
     square[...] = jnp.zeros_like(square)
     d_gate[...] = r_gate[...]
     d_out[...] = r_out[...]
-    cut = r_x0.shape[1]
-    d_x[:, :cut] = r_x0[...]
-    d_x[:, cut:] = r_x1[:, : nv - cut]
+    d_x[...] = r_x[...]
     d_bc[...] = r_bc[...]
-    square[: r_x1.shape[0]] = r_x1[:, nv - cut + 256 :]
-    d_dt[...] = square[...].T[:heads, : r_x1.shape[0]]
+    square[: r_last.shape[0]] = r_last[...]
+    d_dt[...] = square[...].T[:heads, : r_last.shape[0]]
     parts = [smalls[k] for k in range(4)]
     both = parts[0] + parts[1] + parts[2] + parts[3]
     d_pre[:, :nv] = both[7:8]
@@ -1046,10 +1206,10 @@
     w0, w1, w2, w3, normed, cot, vals, states, normed_out, low_gate, dy, gg, cx, cbc, hp, segc, segr = run_k1(
         hidden_in, cotangent, (proj_x, proj_bc, proj_dt.T, proj_gate, proj_out.T), pgain, seg_ids.reshape(-1, 128), params
     )
-    r_gate, r_out, r_x0, r_x1, r_bc, own_out, grad_own, smalls = run_k2(
+    r_gate, r_out, r_x, r_last, r_bc, own_out, grad_own, smalls = run_k2(
         (w0, w1, w2, w3), normed, cot, vals, states, normed_out, low_gate, dy, pgain, segc, segr, cx, cbc, hp, gg
     )
-    outs = run_k3(proj_dt.shape[1], hidden_in, cotangent, pgain, own_out, grad_own, smalls, r_gate, r_out, r_x0, r_x1, r_bc)
+    outs = run_k3(proj_dt.shape[1], hidden_in, cotangent, pgain, own_out, grad_own, smalls, r_gate, r_out, r_x, r_last, r_bc)
     flat = (2, 8, 10, 11, 12, 13, 14)
     turned = (6, 15)
     return tuple(o.reshape(-1) if k in flat else o.T if k in turned else o for k, o in enumerate(outs))

time: 201 us -> 189 us (0.940)
  Pallas kernels: 198 us -> 185 us
    pallas_call x1, Pallas kernels: 108 us -> 98.2 us  [run_k2(): pl.pallas_call(functools.partial(backward_kernel, list(scan), nv), out_sh...]
    pallas_call x1, Pallas kernels: 84.6 us -> 81.8 us  [run_k1(): pl.pallas_call(functools.partial(forward_kernel, list(scan), nv), out_sha...]
where the time goes in v6:
time: 189 us; the launch traced here: 188 us
  Pallas kernels  185 us (98%)
    pallas_call x1, Pallas kernels, run_k2(): pl.pallas_call(functools.partial(backward_kernel, list(scan), nv), out_sh...  98.2 us
    pallas_call x1, Pallas kernels, run_k1(): pl.pallas_call(functools.partial(forward_kernel, list(scan), nv), out_sha...  81.8 us
    pallas_call x1, Pallas kernels, run_k3(): pl.pallas_call(functools.partial(finish_kernel, heads), out_shape=outs, i...  5 us

profile of v6, /device:TPU:1, one launch (start us, length us, event | category | flops | bytes accessed | tf_op | source)
XLA Modules:
  0.0 188.3 jit_solution(4513702225093628486)
XLA Ops:
  0.6 1.3 reshape.77.pgain
  1.9 81.8 %forward_all.1 = (bf16[1536,640]{1,0:T(8,128)(2,1)}, bf16[1536,512]{1,0:T(8,128)(2,1)}, bf16[1536,768]{1,0:T(8,128)(2,1)}, bf16[1536,768]{1,0:T(8,128)(2,1)}, bf...) custom-call(bf16[256,1536]{1,0:T(8,128)(2,1)} %hid.3, ...), custom_call_target="tpu_custom_call" | custom-call | tf_op jit(solution)/shard_map/forward_all/pallas_call | solution.py:767
  83.8 98.2 %backward_all.1 = (f32[48,768]{1,0:T(8,128)}, f32[48,768]{1,0:T(8,128)}, f32[48,768]{1,0:T(8,128)}, f32[48,128]{1,0:T(8,128)}, f32[48,256]{1,0:T(8,128)}, /*inde...) custom-call(bf16[1536,640]{1,0:T(8,128)(2,1)} %get-tuple-element.57.h_w0, ...), custom_call_target="tpu_custom_call" | custom-call | tf_op jit(solution)/shard_map/backward_all/pallas_call | solution.py:1128
  182.0 5.0 %finish.1 = (bf16[256,1536]{1,0:T(8,128)(2,1)}, f32[256,1536]{1,0:T(8,128)}, f32[1,1536]{1,0:T(1,128)}, f32[48,768]{1,0:T(8,128)}, f32[48,768]{1,0:T(8,128)}, /*...) custom-call(bf16[256,1536]{1,0:T(8,128)(2,1)} %hid.3, ...), custom_call_target="tpu_custom_call" | custom-call | tf_op jit(solution)/shard_map/finish/pallas_call | solution.py:1193
  187.0 1.3 reduce

commit v7 on v6

--- a/solution.py
+++ b/solution.py
@@ -131,11 +131,6 @@
     return hi, mid, lo
 
 
-def spread3(v, mat):
-    hi, mid, lo = split3(v)
-    return dnn(jnp.concatenate([hi, mid, lo], axis=1), jnp.concatenate([mat, mat, mat], axis=0))
-
-
 def tri_times(mat, v):
     hi, mid, lo = split3(v)
     out = dnn(mat, jnp.concatenate([hi, mid, lo], axis=1))
@@ -176,140 +171,6 @@
     cur = segc[pl.ds(r0, Q), :]
     ext = jnp.concatenate([prev, cur], axis=0)
     return [None] + [ext[8 - k : 8 + Q - k] == cur for k in (1, 2, 3)]
-
-
-def block_setup(c, nv, vals, segc, segr, cbc, hp, bt_ref, b_ref, c_ref, ct_ref, qk_ref, bias_ref, cum_ref, cumt_ref, step_ref, tail_ref, keep_ref, ex_ref, keep_out):
-    r0 = pl.multiple_of(c * Q, Q)
-    match = match_rows(segc, r0)
-    m2 = [None] + [jnp.concatenate([m, m], axis=1) for m in match[1:]]
-    ext = with_earlier(vals, r0, pl.ds(nv, 256))
-    pre, shifted = conv_terms(ext, m2, cbc[...])
-    bc = pre * sigmoid(pre)
-    bb = bc[:, :128].astype(BF)
-    cc = bc[:, 128:].astype(BF)
-    b_ref[...] = bb
-    c_ref[...] = cc
-    bt_ref[...] = bc[:, :128].T.astype(BF)
-    if ct_ref is not None:
-        ct_ref[...] = bc[:, 128:].T.astype(BF)
-    qk_ref[...] = dnt(cc, bb)
-    seg = segc[pl.ds(r0, Q), :]
-    segs = segr[0:1, pl.ds(r0, Q)]
-    tt, ss = ii((Q, Q), 0), ii((Q, Q), 1)
-    allowed = (tt >= ss) & (jnp.concatenate([seg, seg], axis=1) == segs)
-    bias_ref[...] = jnp.where(allowed, 0.0, NEG)
-    raw = vals[pl.ds(r0, Q), pl.ds(nv + 256, 128)] + hp[0:1]
-    step = softplus(raw)
-    tri = (tt >= ss).astype(BF)
-    cum = tri_times(tri, step * (hp[1:2] * LOG2E))
-    cumt = cum.T
-    for h in range(nv // 64):
-        cumt_ref[h] = jnp.broadcast_to(cumt[h : h + 1], (8, Q))
-    exm = ex_ref[...]
-    cum_ref[...] = spread3(cum, exm)
-    e64 = (ii((128, nv), 0) == ii((128, nv), 1) // 64).astype(BF)
-    step_ref[...] = spread3(step, e64)
-    prev_seg = jnp.where(c > 0, segc[pl.ds(pl.multiple_of(jnp.maximum(r0 - 8, 0), 8), 8), :][7:8], -1.0)
-    last_seg = seg[Q - 1 :]
-    cum_last = cum[Q - 1 :]
-    carry = (seg == prev_seg).astype(F32)
-    tailm = (seg == last_seg).astype(F32)
-    tail = jnp.exp2(cum_last - cum) * tailm
-    tail_ref[...] = spread3(tail, e64)
-    keep = jnp.exp2(cum_last) * (last_seg == prev_seg).astype(F32)
-    keep_ref[...] = spread3(jnp.broadcast_to(keep, (8, 128)), e64)
-    keep_out[...] = spread3(jnp.exp2(cum) * carry, e64)
-    return match, pre, shifted, raw, step
-
-
-def decay(cum_ref, cumt_ref, bias_ref, h, rows, cols):
-    col = cum_ref[rows, pl.ds(pl.multiple_of(h * 128, 128), 128)]
-    row = cumt_ref[h, 0:1, cols]
-    return jnp.exp2(col - row + bias_ref[rows, cols])
-
-
-def fwd_scratch(nv):
-    V = lambda s, d=F32: pltpu.VMEM(s, d)
-    nh = nv // 64
-    return dict(
-        bt=V((128, Q), BF), b=V((Q, 128), BF), c=V((Q, 128), BF), qk=V((Q, Q)), bias=V((Q, Q)), cum=V((Q, nh * 128)), cumt=V((nh, 8, Q)),
-        step=V((Q, nv)), tail=V((Q, nv)), keep=V((8, nv)), ecum=V((Q, nv)), ex=V((128, nh * 128), BF), state=V((128, nv)), m=V((4, Q, Q), BF),
-    )
-
-
-def ssd_forward(nv, vals, segc, segr, cx, cbc, hp, ssd, states, s, hook=lambda at: None):
-    nh = nv // 64
-    s["ex"][...] = (ii((128, nh * 128), 0) == ii((128, nh * 128), 1) // 128).astype(BF)
-    s["state"][...] = jnp.zeros_like(s["state"])
-    s["m"][...] = jnp.zeros_like(s["m"])
-
-    def block(c, _):
-        r0 = pl.multiple_of(c * Q, Q)
-        match, *_r = block_setup(c, nv, vals, segc, segr, cbc, hp, s["bt"], s["b"], s["c"], None, s["qk"], s["bias"], s["cum"], s["cumt"], s["step"], s["tail"], s["keep"], s["ex"], s["ecum"])
-        states[c] = s["state"][...].astype(BF)
-
-        def pairs(jj, _):
-            hook(c * (nv // 256) + jj)
-            done = []
-            for p in range(2):
-                j = 2 * jj + p
-                lanes = pl.ds(pl.multiple_of(j * 128, 128), 128)
-                pre, _sh = conv_terms(with_earlier(vals, r0, lanes), match, cx[:, lanes])
-                x = pre * sigmoid(pre)
-                u = x * s["step"][:, lanes]
-                st = s["state"][:, lanes]
-                y = dnn(s["c"][...], st.astype(BF)) * s["ecum"][:, lanes] + cx[5:6, lanes] * x
-                new = st * s["keep"][0:1, lanes] + dnn(s["bt"][...], (u * s["tail"][:, lanes]).astype(BF))
-                done.append((j, lanes, u.astype(BF), y, new))
-            for r in range(4):
-                rows = slice(r * 64, r * 64 + 64)
-                for k in range(1 if r < 2 else 2):
-                    cols = slice(k * 128, k * 128 + 128)
-                    qk, bias = s["qk"][rows, cols], s["bias"][rows, cols]
-                    for p in range(2):
-                        for e in range(2):
-                            h = 2 * done[p][0] + e
-                            col = s["cum"][rows, pl.ds(pl.multiple_of(h * 128, 128), 128)]
-                            s["m"][2 * p + e, rows, cols] = (jnp.exp2(col - s["cumt"][h, 0:1, cols] + bias) * qk).astype(BF)
-            outs = []
-            for p in range(2):
-                _j, lanes, ub, y, new = done[p]
-                y0, y1 = dnn(s["m"][2 * p], ub), dnn(s["m"][2 * p + 1], ub)
-                outs.append(y + jnp.where(ii((Q, 128), 1) < 64, y0, y1))
-            for p in range(2):
-                ssd[pl.ds(r0, Q), done[p][1]] = outs[p]
-                s["state"][:, done[p][1]] = done[p][4]
-            return 0
-
-        lax.fori_loop(0, nv // 256, pairs, 0)
-        return 0
-
-    lax.fori_loop(0, vals.shape[0] // Q, block, 0)
-
-
-def later_sum(dpre, halo, match_ext, taps):
-    ext = jnp.concatenate([dpre, halo], axis=0)
-    n = dpre.shape[0]
-    out = taps[3:4] * dpre
-    for k in (1, 2, 3):
-        out = out + taps[3 - k : 4 - k] * jnp.where(match_ext[k], ext[k : n + k], 0.0)
-    return out
-
-
-def run_forward(nv, vals, segc, segr, cx, cbc, hp):
-    sc = fwd_scratch(nv)
-    names = list(sc)
-    rows = vals.shape[0]
-
-    def kernel(vals, segc, segr, cx, cbc, hp, ssd, states, *scr):
-        ssd_forward(nv, vals, segc, segr, cx, cbc, hp, ssd, states, dict(zip(names, scr)))
-
-    vm = pl.BlockSpec(memory_space=pltpu.VMEM)
-    return pl.pallas_call(
-        kernel, out_shape=(jax.ShapeDtypeStruct((rows, nv), F32), jax.ShapeDtypeStruct((rows // Q, 128, nv), F32)),
-        in_specs=[vm] * 6, out_specs=[vm] * 2, scratch_shapes=[sc[n] for n in names],
-        compiler_params=pltpu.CompilerParams(vmem_limit_bytes=60 * 2**20), name="scan_forward",
-    )(vals, segc, segr, cx, cbc, hp)
 
 
 def pack_heads(nh, cum, step, tail, ecum):
@@ -323,12 +184,124 @@
     return out.astype(BF)
 
 
-def unpack_matrix(nh, j):
-    k, col = ii((128, 640), 0), ii((128, 640), 1)
+def unpack_matrix(nh, jj):
+    k, col = ii((128, 1280), 0), ii((128, 1280), 1)
     kind = jnp.where(k < 3 * nh, 0, jnp.where(k < 5 * nh, 1, jnp.where(k < 7 * nh, 2, jnp.where(k < 9 * nh, 3, 9))))
-    want = jnp.maximum(col // 128 - 1, 0)
-    sub = jnp.where(col < 256, col // 128, (col % 128) // 64)
-    return ((kind == want) & (k % nh == 2 * j + sub)).astype(BF)
+    want = jnp.where(col < 512, 0, (col - 256) // 256)
+    sub = jnp.where(col < 512, col // 128, (col % 256) // 64)
+    return ((kind == want) & (k % nh == 4 * jj + sub)).astype(BF)
+
+
+def block_rows(c):
+    return pl.ds(pl.multiple_of(c * Q, Q), Q)
+
+
+def wide(match):
+    return [None] + [jnp.concatenate([m, m], axis=1) for m in match[1:]]
+
+
+def prepare_block(c, nv, vals, segc, segr, cbc, hp):
+    nh = nv // 64
+    r0 = pl.multiple_of(c * Q, Q)
+    rows = block_rows(c)
+    pre, _sh = conv_terms(with_earlier(vals, r0, pl.ds(nv, 256)), wide(match_rows(segc, r0)), cbc[...])
+    bc = pre * sigmoid(pre)
+    bb, cc = bc[:, :128].astype(BF), bc[:, 128:].astype(BF)
+    seg = segc[rows]
+    tt, ss = ii((Q, Q), 0), ii((Q, Q), 1)
+    allowed = (tt >= ss) & (jnp.concatenate([seg, seg], axis=1) == segr[0:1, rows])
+    bias = jnp.where(allowed, 0.0, NEG)
+    mine = ii((Q, 128), 1) < nh
+    zero = lambda v: jnp.where(mine, v, 0.0)
+    step = zero(softplus(vals[rows, pl.ds(nv + 256, 128)] + hp[0:1]))
+    cum = tri_times((tt >= ss).astype(BF), step * (hp[1:2] * LOG2E))
+    before = segc[pl.ds(pl.multiple_of(jnp.maximum(r0 - 8, 0), 8), 8)][7:8]
+    before = jnp.where(c > 0, before, -1.0)
+    tail = zero(jnp.exp2(cum[Q - 1 :] - cum) * (seg == seg[Q - 1 :]).astype(F32))
+    ecum = zero(jnp.exp2(cum) * (seg == before).astype(F32))
+    return bb, cc, bc[:, :128].T.astype(BF), bc[:, 128:].T.astype(BF), dnt(cc, bb), bias, cum.T, pack_heads(nh, cum, step, tail, ecum)
+
+
+def fwd_scratch(nv):
+    V = lambda s, d=F32: pltpu.VMEM(s, d)
+    nh = nv // 64
+    return dict(
+        bt=V((128, Q), BF), c=V((Q, 128), BF), qk=V((Q, Q)), bias=V((Q, Q)), cumt=V((nh, 8, Q)), pack=V((Q, 128), BF),
+        un=V((nh // 4, 128, 1280), BF), ex=V((Q, 1280)), state=V((128, nv)), m=V((4, Q, Q), BF),
+    )
+
+
+def ssd_forward(nv, vals, segc, segr, cx, cbc, hp, ssd, states, s, hook=lambda at: None):
+    nh = nv // 64
+    for jj in range(nh // 4):
+        s["un"][jj] = unpack_matrix(nh, jj)
+    s["state"][...] = jnp.zeros_like(s["state"])
+    s["m"][...] = jnp.zeros_like(s["m"])
+
+    def block(c, _):
+        r0 = pl.multiple_of(c * Q, Q)
+        _bb, s["c"][...], s["bt"][...], _ct, s["qk"][...], s["bias"][...], cumt, s["pack"][...] = prepare_block(c, nv, vals, segc, segr, cbc, hp)
+        for h in range(nh):
+            s["cumt"][h] = jnp.broadcast_to(cumt[h : h + 1], (8, Q))
+        states[c] = s["state"][...].astype(BF)
+        match = wide(match_rows(segc, r0))
+
+        def quad(jj, _):
+            hook(c * (nv // 256) + jj)
+            lanes = pl.ds(pl.multiple_of(jj * 256, 256), 256)
+            s["ex"][...] = dnn(s["pack"][...], s["un"][jj])
+            pre, _sh = conv_terms(with_earlier(vals, r0, lanes), match, cx[:, lanes])
+            x = pre * sigmoid(pre)
+            u = x * s["ex"][:, 512:768]
+            ub = u.astype(BF)
+            st = s["state"][:, lanes]
+            y = dnn(s["c"][...], st.astype(BF)) * s["ex"][:, 1024:1280] + cx[5:6, lanes] * x
+            s["state"][:, lanes] = st * s["ex"][Q - 1 : Q, 1024:1280] + dnn(s["bt"][...], (u * s["ex"][:, 768:1024]).astype(BF))
+            for r in range(4):
+                rows = slice(r * 64, r * 64 + 64)
+                for k in range(1 if r < 2 else 2):
+                    cols = slice(k * 128, k * 128 + 128)
+                    qk, bias = s["qk"][rows, cols], s["bias"][rows, cols]
+                    for n in range(4):
+                        dec = jnp.exp2(s["ex"][rows, n * 128 : n * 128 + 128] - s["cumt"][4 * jj + n, 0:1, cols] + bias)
+                        s["m"][n, rows, cols] = (dec * qk).astype(BF)
+            low_half = ii((Q, 128), 1) < 64
+            outs = []
+            for p in range(2):
+                right = ub[:, p * 128 : p * 128 + 128]
+                outs.append(jnp.where(low_half, dnn(s["m"][2 * p], right), dnn(s["m"][2 * p + 1], right)))
+            ssd[pl.ds(r0, Q), lanes] = y + jnp.concatenate(outs, axis=1)
+            return 0
+
+        lax.fori_loop(0, nv // 256, quad, 0)
+        return 0
+
+    lax.fori_loop(0, vals.shape[0] // Q, block, 0)
+
+
+def later_sum(dpre, halo, match_ext, taps):
+    ext = jnp.concatenate([dpre, halo], axis=0)
+    n = dpre.shape[0]
+    out = taps[3:4] * dpre
+    for k in (1, 2, 3):
+        out = out + taps[3 - k : 4 - k] * jnp.where(match_ext[k], ext[k : n + k], 0.0)
+    return out
+
+
+def run_forward(nv, vals, segc, segr, cx, cbc, hp):
+    sc = fwd_scratch(nv)
+    names = list(sc)
+    rows = vals.shape[0]
+
+    def kernel(vals, segc, segr, cx, cbc, hp, ssd, states, *scr):
+        ssd_forward(nv, vals, segc, segr, cx, cbc, hp, ssd, states, dict(zip(names, scr)))
+
+    vm = pl.BlockSpec(memory_space=pltpu.VMEM)
+    return pl.pallas_call(
+        kernel, out_shape=(jax.ShapeDtypeStruct((rows, nv), F32), jax.ShapeDtypeStruct((rows // Q, 128, nv), F32)),
+        in_specs=[vm] * 6, out_specs=[vm] * 2, scratch_shapes=[sc[n] for n in names],
+        compiler_params=pltpu.CompilerParams(vmem_limit_bytes=60 * 2**20), name="scan_forward",
+    )(vals, segc, segr, cx, cbc, hp)
 
 
 def back_scratch(nv, rows):
@@ -336,17 +309,9 @@
     nb, nh = rows // Q, nv // 64
     return dict(
         b=V((rows, 128), BF), c=V((rows, 128), BF), bt=V((nb, 128, Q), BF), ct=V((nb, 128, Q), BF), qk=V((nb, Q, Q)), bias=V((nb, Q, Q)), pack=V((rows, 128), BF),
-        cumt=V((nb, nh, 8, Q)), un=V((2, 128, 640), BF), ex=V((2, Q, 640)), dqk=V((nb, Q, Q)), dcs=V((rows, 128)), dbs=V((rows, 128)), hsum=V((rows, 128)),
-        colg=V((nb, nh, 8, Q)), krow=V((nb, 8, nv)), dstate=V((2, 128, 128)), halo=V((2, 8, 128)), halobc=V((8, 256)), m=V((4, Q, Q), BF), dm=V((4, Q, Q)),
+        cumt=V((nb, nh, 8, Q)), un=V((128, 1280), BF), ex=V((Q, 1280)), dqk=V((nb, Q, Q)), dcs=V((rows, 128)), dbs=V((rows, 128)), hsum=V((rows, 128)),
+        colg=V((nb, nh, 8, Q)), krow=V((nb, 8, nv)), dstate=V((128, 256)), halo=V((8, 256)), halobc=V((8, 256)), m=V((4, Q, Q), BF), dm=V((4, Q, Q)),
     )
-
-
-def block_rows(c):
-    return pl.ds(pl.multiple_of(c * Q, Q), Q)
-
-
-def wide(match):
-    return [None] + [jnp.concatenate([m, m], axis=1) for m in match[1:]]
 
 
 def back_setup(nv, vals, segc, segr, cbc, hp, s):
@@ -355,30 +320,10 @@
         s[n][...] = jnp.zeros_like(s[n])
 
     def block(c, _):
-        r0 = pl.multiple_of(c * Q, Q)
         rows = block_rows(c)
-        pre, _sh = conv_terms(with_earlier(vals, r0, pl.ds(nv, 256)), wide(match_rows(segc, r0)), cbc[...])
-        bc = pre * sigmoid(pre)
-        bb, cc = bc[:, :128].astype(BF), bc[:, 128:].astype(BF)
-        s["b"][rows], s["c"][rows] = bb, cc
-        s["bt"][c], s["ct"][c] = bc[:, :128].T.astype(BF), bc[:, 128:].T.astype(BF)
-        s["qk"][c] = dnt(cc, bb)
-        seg = segc[rows]
-        tt, ss = ii((Q, Q), 0), ii((Q, Q), 1)
-        allowed = (tt >= ss) & (jnp.concatenate([seg, seg], axis=1) == segr[0:1, rows])
-        s["bias"][c] = jnp.where(allowed, 0.0, NEG)
-        mine = ii((Q, 128), 1) < nh
-        step = jnp.where(mine, softplus(vals[rows, pl.ds(nv + 256, 128)] + hp[0:1]), 0.0)
-        cum = tri_times((tt >= ss).astype(BF), step * (hp[1:2] * LOG2E))
-        cumt = cum.T
+        s["b"][rows], s["c"][rows], s["bt"][c], s["ct"][c], s["qk"][c], s["bias"][c], cumt, s["pack"][rows] = prepare_block(c, nv, vals, segc, segr, cbc, hp)
         for h in range(nh):
             s["cumt"][c, h] = jnp.broadcast_to(cumt[h : h + 1], (8, Q))
-        before = segc[pl.ds(pl.multiple_of(jnp.maximum(r0 - 8, 0), 8), 8)][7:8]
-        before = jnp.where(c > 0, before, -1.0)
-        zero = lambda v: jnp.where(mine, v, 0.0)
-        tail = zero(jnp.exp2(cum[Q - 1 :] - cum) * (seg == seg[Q - 1 :]).astype(F32))
-        ecum = zero(jnp.exp2(cum) * (seg == before).astype(F32))
-        s["pack"][rows] = pack_heads(nh, cum, step, tail, ecum)
         return 0
 
     lax.fori_loop(0, vals.shape[0] // Q, block, 0)
@@ -390,49 +335,43 @@
     c = nb - 1 - i
     r0 = pl.multiple_of(c * Q, Q)
     rows_c = block_rows(c)
+    lanes = pl.ds(pl.multiple_of(jj * 256, 256), 256)
 
     @pl.when(i == 0)
     def _():
         s["dstate"][...] = jnp.zeros_like(s["dstate"])
         s["halo"][...] = jnp.zeros_like(s["halo"])
-        for p in range(2):
-            s["un"][p] = unpack_matrix(nh, 2 * jj + p)
-
-    match, after = match_rows(segc, r0), match_after(segc, r0)
+        s["un"][...] = unpack_matrix(nh, jj)
+
+    match, after = wide(match_rows(segc, r0)), wide(match_after(segc, r0))
+    s["ex"][...] = dnn(s["pack"][rows_c], s["un"][...])
+    stepe, taile, ecume = s["ex"][:, 512:768], s["ex"][:, 768:1024], s["ex"][:, 1024:1280]
+    keep = s["ex"][Q - 1 : Q, 1024:1280]
+    taps = cx[:, lanes]
+    pre, shifted = conv_terms(with_earlier(vals, r0, lanes), match, taps)
+    sig = sigmoid(pre)
+    x = pre * sig
+    u = x * stepe
+    ub = u.astype(BF)
+    dy = dy_ref[rows_c, lanes].astype(F32)
+    dyt = dy.T.astype(BF)
+    stb = states[c, :, lanes]
+    dst = s["dstate"][...]
+    dstb = dst.astype(BF)
+    edy = ecume * dy
+    edyb = edy.astype(BF)
+    rs = edy * dnn(s["c"][rows_c], stb)
+    tu = taile * u
+    v = dnn(s["b"][rows_c], dstb)
+    s["dcs"][rows_c] += dnt(edyb, stb)
+    s["dbs"][rows_c] += dnt(tu.astype(BF), dstb)
+    krow = keep * jnp.sum(stb.astype(F32) * dst, axis=0, keepdims=True)
+    s["dstate"][...] = keep * dst + dnn(s["ct"][c], edyb)
     lane = ii((Q, 128), 1)
-    one = []
-    dcs = dbs = 0.0
-    for p in range(2):
-        j = 2 * jj + p
-        lanes = pl.ds(pl.multiple_of(j * 128, 128), 128)
-        s["ex"][p] = dnn(s["pack"][rows_c], s["un"][p])
-        stepe, taile, ecume = s["ex"][p, :, 256:384], s["ex"][p, :, 384:512], s["ex"][p, :, 512:640]
-        keep = s["ex"][p, Q - 1 : Q, 512:640]
-        taps = cx[:, lanes]
-        pre, shifted = conv_terms(with_earlier(vals, r0, lanes), match, taps)
-        sig = sigmoid(pre)
-        x = pre * sig
-        u = x * stepe
-        dy = dy_ref[rows_c, lanes].astype(F32)
-        stb = states[c, :, lanes]
-        dst = s["dstate"][p]
-        dstb = dst.astype(BF)
-        edy = ecume * dy
-        edyb = edy.astype(BF)
-        rs = edy * dnn(s["c"][rows_c], stb)
-        dcs = dcs + dnt(edyb, stb)
-        tu = taile * u
-        v = dnn(s["b"][rows_c], dstb)
-        dbs = dbs + dnt(tu.astype(BF), dstb)
-        krow = keep * jnp.sum(stb.astype(F32) * dst, axis=0, keepdims=True)
-        s["dstate"][p] = keep * dst + dnn(s["ct"][c], edyb)
-        ub = u.astype(BF)
-        for e in range(2):
-            mine = (lane < 64) if e == 0 else (lane >= 64)
-            s["dm"][2 * p + e] = dnt(jnp.where(mine, dy, 0.0).astype(BF), ub)
-        one.append((j, lanes, stepe, taile, taps, shifted, sig, x, dy, dy.T.astype(BF), rs, tu, v, krow))
-    s["dcs"][rows_c] += dcs
-    s["dbs"][rows_c] += dbs
+    for n in range(4):
+        half = slice(n // 2 * 128, n // 2 * 128 + 128)
+        mine = (lane < 64) if n % 2 == 0 else (lane >= 64)
+        s["dm"][n] = dnt(jnp.where(mine, dy[:, half], 0.0).astype(BF), ub[:, half])
     colsum = [[jnp.zeros((8, 128), F32) for _ in range(2)] for _ in range(4)]
     rowg = []
     for r in range(4):
@@ -443,8 +382,7 @@
             qk, bias = s["qk"][c, rows, cols], s["bias"][c, rows, cols]
             total = None
             for n in range(4):
-                p, e = n // 2, n % 2
-                dec = jnp.exp2(s["ex"][p, rows, e * 128 : e * 128 + 128] - s["cumt"][c, 4 * jj + n, 0:1, cols] + bias)
+                dec = jnp.exp2(s["ex"][rows, n * 128 : n * 128 + 128] - s["cumt"][c, 4 * jj + n, 0:1, cols] + bias)
                 s["m"][n, rows, cols] = (dec * qk).astype(BF)
                 g = s["dm"][n, rows, cols] * dec
                 total = g if n == 0 else total + g
@@ -457,29 +395,22 @@
         for n in range(4):
             row = jnp.where(at_lane == 48 + 4 * jj + n, jnp.sum(rowsum[n], axis=1, keepdims=True), row)
         rowg.append(row)
-    heads = jnp.concatenate(rowg, axis=0)
-    ends = []
-    for p in range(2):
-        j, lanes, stepe, taile, taps, shifted, sig, x, dy, dyt, rs, tu, v, krow = one[p]
-        parts = [dnn(dyt[e * 64 : e * 64 + 64], s["m"][2 * p + e]) for e in range(2)]
-        du = jnp.concatenate(parts, axis=0).T + taile * v
-        k, col = ii((384, 128), 0), ii((384, 128), 1)
-        red = (col == 16 * (k // 128) + 2 * j + (k % 128) // 64).astype(BF)
-        heads = heads + dnn(jnp.concatenate([rs.astype(BF), (tu * v).astype(BF), (du * x).astype(BF)], axis=1), red)
-        dx = du * stepe + taps[5:6] * dy
-        dpre = dx * (sig + x * (1.0 - sig))
-        grow = jnp.concatenate(
-            [jnp.sum(dpre * shifted[3 - k], axis=0, keepdims=True) for k in range(4)]
-            + [jnp.sum(dpre, axis=0, keepdims=True), jnp.sum(dy * x, axis=0, keepdims=True), jnp.zeros((2, 128), F32)], axis=0)
-        ends.append((later_sum(dpre, s["halo"][p], after, taps).astype(BF), dpre[:8], grow))
-    s["hsum"][rows_c] += heads
+    parts = [dnn(dyt[n * 64 : n * 64 + 64], s["m"][n]) for n in range(4)]
+    du = jnp.concatenate(parts, axis=0).T + taile * v
+    k, col = ii((768, 128), 0), ii((768, 128), 1)
+    red = (col == 16 * (k // 256) + 4 * jj + (k % 256) // 64).astype(BF)
+    sums = jnp.concatenate([rs.astype(BF), (tu * v).astype(BF), (du * x).astype(BF)], axis=1)
+    s["hsum"][rows_c] += dnn(sums, red) + jnp.concatenate(rowg, axis=0)
+    dx = du * stepe + taps[5:6] * dy
+    dpre = dx * (sig + x * (1.0 - sig))
+    low[rows_c, lanes] = later_sum(dpre, s["halo"][...], after, taps).astype(BF)
+    s["halo"][...] = dpre[:8]
+    gx[:, lanes] += jnp.concatenate(
+        [jnp.sum(dpre * shifted[3 - k], axis=0, keepdims=True) for k in range(4)]
+        + [jnp.sum(dpre, axis=0, keepdims=True), jnp.sum(dy * x, axis=0, keepdims=True), jnp.zeros((2, 256), F32)], axis=0)
     for n in range(4):
         s["colg"][c, 4 * jj + n] = jnp.broadcast_to(jnp.concatenate([jnp.sum(q, axis=0, keepdims=True) for q in colsum[n]], axis=1), (8, Q))
-    for p in range(2):
-        lanes = one[p][1]
-        low[rows_c, lanes], s["halo"][p] = ends[p][0], ends[p][1]
-        gx[:, lanes] += ends[p][2]
-        s["krow"][c, :, lanes] = jnp.broadcast_to(one[p][13], (8, 128))
+    s["krow"][c, :, lanes] = jnp.broadcast_to(krow, (8, 256))
 
 
 def match_after(segc, r0):
@@ -941,18 +872,21 @@
         def body(i, _):
             cols = pl.ds(pl.multiple_of(i * 384, 384), 384)
             r = lax.dot_general(left[:, cols], right[...], (((0,), (0,)), ((), ())), preferred_element_type=F32)
-            dst[i] = r.astype(BF).reshape(dst.shape[1:])
+            first = 0
+            for d in dst:
+                d[i] = r[:, first : first + d.shape[-1]].astype(BF).reshape(d.shape[1:])
+                first += d.shape[-1]
             return 0
 
         lax.fori_loop(0, 4, body, 0)
 
     loads[0].wait()
     loads[2].wait()
-    outer_product(t_out, cot, nody)
+    outer_product((t_out,), cot, nody)
     s_out.step(0)
     loads[3].wait()
     loads[4].wait()
-    outer_product(t_gate, nrm, lg)
+    outer_product((t_gate,), nrm, lg)
     s_gate.step(0)
 
     def out_rows(rows):
@@ -973,7 +907,7 @@
 
     def chunk(n):
         def go():
-            outer_product((t_0, t_1, t_2)[n], nrm, low.at[:, n * wide_x : n * wide_x + wide_x])
+            outer_product(((t_0, t_1, t_2)[n],), nrm, low.at[:, n * wide_x : n * wide_x + wide_x])
             scat[2 + n].step(0)
 
         return go
@@ -997,9 +931,8 @@
     lax.fori_loop(0, nv // 256 * (vals.shape[0] // Q), scan_step, 0)
     chunk(2)()
     back_finish(nv, vals, segc, cbc, hp, low, gbc, gh, s)
-    outer_product(t_bc, nrm, low.at[:, nv : nv + 256])
+    outer_product((t_bc, t_dt), nrm, low.at[:, nv:])
     s_bc.step(0)
-    outer_product(t_dt, nrm, low.at[:, nv + 256 :])
     s_dt.step(0)
     s_out.step(4)
     s_gate.step(4)

time: 189 us -> 186 us (0.984)
  Pallas kernels: 185 us -> 183 us
    pallas_call x1, Pallas kernels: 98.2 us -> 95.6 us  [run_k2(): pl.pallas_call(functools.partial(backward_kernel, list(scan), nv), out_sh...]
where the time goes in v7:
time: 186 us
  Pallas kernels  183 us (98%)
    pallas_call x1, Pallas kernels, run_k2(): pl.pallas_call(functools.partial(backward_kernel, list(scan), nv), out_sh...  95.6 us
    pallas_call x1, Pallas kernels, run_k1(): pl.pallas_call(functools.partial(forward_kernel, list(scan), nv), out_sha...  82 us
    pallas_call x1, Pallas kernels, run_k3(): pl.pallas_call(functools.partial(finish_kernel, heads), out_shape=outs, i...  5 us

profile of v7, /device:TPU:1, one launch (start us, length us, event | category | flops | bytes accessed | tf_op | source)
XLA Modules:
  0.0 185.8 jit_solution(14999673423613724513)
XLA Ops:
  0.6 1.3 reshape.77.pgain
  1.9 82.0 %forward_all.1 = (bf16[1536,640]{1,0:T(8,128)(2,1)}, bf16[1536,512]{1,0:T(8,128)(2,1)}, bf16[1536,768]{1,0:T(8,128)(2,1)}, bf16[1536,768]{1,0:T(8,128)(2,1)}, bf...) custom-call(bf16[256,1536]{1,0:T(8,128)(2,1)} %hid.3, ...), custom_call_target="tpu_custom_call" | custom-call | tf_op jit(solution)/shard_map/forward_all/pallas_call | solution.py:698
  83.9 95.6 %backward_all.1 = (f32[48,768]{1,0:T(8,128)}, f32[48,768]{1,0:T(8,128)}, f32[48,768]{1,0:T(8,128)}, f32[48,128]{1,0:T(8,128)}, f32[48,256]{1,0:T(8,128)}, /*inde...) custom-call(bf16[1536,640]{1,0:T(8,128)(2,1)} %get-tuple-element.57.h_w0, ...), custom_call_target="tpu_custom_call" | custom-call | tf_op jit(solution)/shard_map/backward_all/pallas_call | solution.py:1061
  179.5 5.0 %finish.1 = (bf16[256,1536]{1,0:T(8,128)(2,1)}, f32[256,1536]{1,0:T(8,128)}, f32[1,1536]{1,0:T(1,128)}, f32[48,768]{1,0:T(8,128)}, f32[48,768]{1,0:T(8,128)}, /*...) custom-call(bf16[256,1536]{1,0:T(8,128)(2,1)} %hid.3, ...), custom_call_target="tpu_custom_call" | custom-call | tf_op jit(solution)/shard_map/finish/pallas_call | solution.py:1126
  184.5 1.3 reduce

commit v8 on v7

--- a/solution.py
+++ b/solution.py
@@ -551,6 +551,11 @@
         return 0
 
     lax.fori_loop(0, 4, norm_rows, 0)
+    nrm_copies = tensor_copies(0, nrm.at[mine], nrm)
+    cot_copies = tensor_copies(1, cot_own, cot)
+    nrm_copies[0].start()
+    nrm_copies[1].start()
+    step(first, 1)
     own_lanes = pl.ds(pl.multiple_of(t * nv, 128), nv)
     heads = p_dt.shape[0]
 
@@ -576,11 +581,7 @@
         g = groups((k,))[0]
         g.mine[...] = g.own[...]
     cot[mine] = cot_own[...]
-    nrm_copies = tensor_copies(0, nrm.at[mine], nrm)
-    cot_copies = tensor_copies(1, cot_own, cot)
-    nrm_copies[0].start()
-    nrm_copies[1].start()
-    for n in (1, 4, 2, 3):
+    for n in (4, 2, 3):
         step(first, n)
     cot_copies[0].start()
     cot_copies[1].start()
@@ -847,8 +848,8 @@
         pltpu.make_async_copy(a, b, lsem.at[k])
         for k, (a, b) in enumerate(((h_no, nody), (h_w3, w23), (h_cot, cot), (h_nrm, nrm), (h_lg, lg), (h_vals, vals), (h_states, states), (h_w0, w0), (h_w1, w1)))
     ]
-    for c in loads:
-        c.start()
+    for k in (0, 2, 3, 4, 1, 5, 6, 7, 8):
+        loads[k].start()
     load_dy, load_w2 = pltpu.make_async_copy(h_dy, nody, lsem.at[9]), pltpu.make_async_copy(h_w2, w23, lsem.at[10])
     greet([dev(x, z, 1 - yh, t)] + [neighbour(a, d) for a in "xz" for d in (1, 2, 3)] + tp)
     wide_x = o_x.shape[1] // 3
@@ -969,13 +970,13 @@
     small = [send(own_v, sx.at[d - 1], ssend.at[d - 1], srecv.at[d - 1], neighbour("x", d)) for d in (1, 2, 3)]
     for c in small:
         c.start()
+    s_0.step(2)
+    s_1.step(2)
+    s_out.step(5)
+    s_gate.step(5)
     s_2.step(1)
     s_bc.step(1)
     s_dt.step(1)
-    s_out.step(5)
-    s_gate.step(5)
-    s_0.step(2)
-    s_1.step(2)
 
     def next_small(have, total, copies):
         for c in have:
@@ -995,30 +996,30 @@
         sacc[2] = sacc[1] + sy[...]
 
     small_z = next_small(small, total_x, [send(sacc.at[0], sz.at[d - 1], ssend.at[2 + d], srecv.at[2 + d], neighbour("z", d)) for d in (1, 2, 3)])
+    s_0.step(3)
+    s_1.step(3)
     s_2.step(2)
     s_bc.step(2)
     s_dt.step(2)
     small_y = next_small(small_z, total_z, [send(sacc.at[1], sy, ssend.at[6], srecv.at[6], dev(x, z, 1 - yh, t))])
-    s_0.step(3)
-    s_1.step(3)
+    s_0.step(4)
+    s_1.step(4)
     s_2.step(3)
     s_bc.step(3)
     s_dt.step(3)
     small_t = next_small(small_y, total_y, [send(sacc.at[2], st.at[k], ssend.at[7 + k], srecv.at[7 + k], p) for k, p in enumerate(tp)])
+    s_0.step(5)
+    s_1.step(5)
     s_2.step(4)
     s_bc.step(4)
     s_dt.step(4)
-    s_0.step(4)
-    s_1.step(4)
     s_2.step(5)
     s_bc.step(5)
-    s_dt.step(5)
-    s_0.step(5)
-    s_1.step(5)
     bct[3] = bc_sum[...]
     bcs = [send(bct.at[3], bct.at[k], bsend.at[k], brecv.at[k], p) for k, p in enumerate(tp)]
     for c in bcs:
         c.start()
+    s_dt.step(5)
     k_nrm.step(2)
     for c in small_t:
         c.wait_recv()

time: 186 us -> 184 us (0.989)
  Pallas kernels: 183 us -> 181 us
    pallas_call x1, Pallas kernels: 95.6 us -> 93.7 us  [run_k2(): pl.pallas_call(functools.partial(backward_kernel, list(scan), nv), out_sh...]
where the time goes in v8:
time: 184 us
  Pallas kernels  181 us (98%)
    pallas_call x1, Pallas kernels, run_k2(): pl.pallas_call(functools.partial(backward_kernel, list(scan), nv), out_sh...  93.7 us
    pallas_call x1, Pallas kernels, run_k1(): pl.pallas_call(functools.partial(forward_kernel, list(scan), nv), out_sha...  82 us
    pallas_call x1, Pallas kernels, run_k3(): pl.pallas_call(functools.partial(finish_kernel, heads), out_shape=outs, i...  5 us

profile of v8, /device:TPU:1, one launch (start us, length us, event | category | flops | bytes accessed | tf_op | source)
XLA Modules:
  0.0 183.9 jit_solution(2003765296658642011)
XLA Ops:
  0.6 1.3 reshape.77.pgain
  1.9 82.0 %forward_all.1 = (bf16[1536,640]{1,0:T(8,128)(2,1)}, bf16[1536,512]{1,0:T(8,128)(2,1)}, bf16[1536,768]{1,0:T(8,128)(2,1)}, bf16[1536,768]{1,0:T(8,128)(2,1)}, bf...) custom-call(bf16[256,1536]{1,0:T(8,128)(2,1)} %hid.3, ...), custom_call_target="tpu_custom_call" | custom-call | tf_op jit(solution)/shard_map/forward_all/pallas_call | solution.py:699
  83.9 93.7 %backward_all.1 = (f32[48,768]{1,0:T(8,128)}, f32[48,768]{1,0:T(8,128)}, f32[48,768]{1,0:T(8,128)}, f32[48,128]{1,0:T(8,128)}, f32[48,256]{1,0:T(8,128)}, /*inde...) custom-call(bf16[1536,640]{1,0:T(8,128)(2,1)} %get-tuple-element.57.h_w0, ...), custom_call_target="tpu_custom_call" | custom-call | tf_op jit(solution)/shard_map/backward_all/pallas_call | solution.py:1062
  177.6 5.0 %finish.1 = (bf16[256,1536]{1,0:T(8,128)(2,1)}, f32[256,1536]{1,0:T(8,128)}, f32[1,1536]{1,0:T(1,128)}, f32[48,768]{1,0:T(8,128)}, f32[48,768]{1,0:T(8,128)}, /*...) custom-call(bf16[256,1536]{1,0:T(8,128)(2,1)} %hid.3, ...), custom_call_target="tpu_custom_call" | custom-call | tf_op jit(solution)/shard_map/finish/pallas_call | solution.py:1127
  182.6 1.3 reduce
